TPU v7x, 32 devices: a whole 2x2x4 slice. The times are simulated.
32 devices in a mesh: seg: 8 (over z, x), tile: 4 (over y, core).
Axes of the slice: x: 2, y: 2, z: 4, core: 2. Of those that a mesh axis runs over, the one named last changes fastest.
Arguments:
- x_input: bfloat16 [64, 24, 16, 24], P('seg', 'tile'), may hold values from -6 to 6
- expand_w: bfloat16 [24, 144], replicated, may hold values from -1.25 to 1.25
- gain0: float32 [144], replicated, may hold values from 0.25 to 1.75
- bias0: float32 [144], replicated, may hold values from -3 to 3
- dw_kernel: bfloat16 [3, 3, 144], replicated, may hold values from -2 to 2
- gain1: float32 [144], replicated, may hold values from 0.25 to 1.75
- bias1: float32 [144], replicated, may hold values from -3 to 3
- reduce_w: float32 [144, 6], replicated, may hold values from -0.5 to 0.5
- reduce_b: float32 [6], replicated, may hold values from -3 to 3
- restore_w: float32 [6, 144], replicated, may hold values from -2.5 to 2.5
- restore_b: float32 [144], replicated, may hold values from -3 to 3
- project_w: bfloat16 [144, 24], replicated, may hold values from -0.5 to 0.5
- gain2: float32 [24], replicated, may hold values from 0.25 to 1.75
- bias2: float32 [24], replicated, may hold values from -3 to 3
- cotangent: bfloat16 [64, 24, 16, 24], P('seg', 'tile'), may hold values from -6 to 6
- seg_count: int32 [8], P('seg'), may hold values from 1 to 8, as said below
- seg_len: int32 [64], P('seg'), may hold values from 6 to 24, as said below
Outputs:
- block_out: bfloat16 [64, 24, 16, 24], P('seg', 'tile')
- x_grad: bfloat16 [64, 24, 16, 24], P('seg', 'tile')
- expand_w_grad: float32 [24, 144], replicated
- gain0_grad: float32 [144], replicated
- bias0_grad: float32 [144], replicated
- dw_kernel_grad: float32 [3, 3, 144], replicated
- gain1_grad: float32 [144], replicated
- bias1_grad: float32 [144], replicated
- reduce_w_grad: float32 [144, 6], replicated
- reduce_b_grad: float32 [6], replicated
- restore_w_grad: float32 [6, 144], replicated
- restore_b_grad: float32 [144], replicated
- project_w_grad: float32 [144, 24], replicated
- gain2_grad: float32 [24], replicated
- bias2_grad: float32 [24], replicated
- rms_values: float32 [5], replicated
Inputs may be any that keep to these rules, and one draw needn't show every extreme that they name: Slots s with s mod 8 below seg_count of their index of seg hold segments, the others are empty; some index has all 8 live, some only one. `seg_len`: frames from the start of a segment; in every index of seg some live segment has all 24 frames.
All inputs are finite; a program needn't handle non-finite values.
Results may differ from a plain program's by a relative error of at most 0.007.
The roundings to bfloat16 on the way count: a program that leaves them out, or rounds other values in their place, can miss the bound.
Values may be sent and summed in bfloat16 or wider, within the bound.
No kernel may reach another device: no remote copies, remote signals or barrier semaphores. Data moves between devices by JAX's collectives and lax.ppermute only.
A program may use at most 64 MiB of HBM per device.

v0:
```python
import jax
import jax.numpy as jnp
from jax import lax
from jax.sharding import PartitionSpec as P

EPSILON = 0.001
PRECISE = lax.Precision.HIGHEST


def extended(cells, sides, width):
    for axis, dim in sides:
        count = lax.axis_size(axis)
        ends = count - 1
        head = lax.slice_in_dim(cells, 0, width, axis=dim)
        tail = lax.slice_in_dim(cells, cells.shape[dim] - width, cells.shape[dim], axis=dim)
        cells = jnp.concatenate(
            [
                lax.ppermute(tail, axis, [(i, (i + 1) % count) for i in range(ends)]),
                cells,
                lax.ppermute(head, axis, [((i + 1) % count, i) for i in range(ends)]),
            ],
            axis=dim,
        )
    return cells


def swish(values):
    return values * jax.nn.sigmoid(values)


def swish_slope(values):
    squashed = jax.nn.sigmoid(values)
    return squashed * (1.0 + values * (1.0 - squashed))


def row_dot(field, weight):
    return jnp.einsum("stmc,cd->stmd", field, weight, preferred_element_type=jnp.float32)


def depthwise(padded, kernel, rows, width):
    result = jnp.zeros((padded.shape[0], rows, width, padded.shape[3]), jnp.float32)
    for row in range(3):
        for col in range(3):
            result = result + padded[:, row : row + rows, col : col + width, :].astype(
                jnp.float32
            ) * kernel[row, col].astype(jnp.float32)
    return result


def moments(values, weights, count_local):
    local_sum = jnp.sum(values * weights, axis=(0, 1, 2))
    first = lax.psum((local_sum, count_local), ("seg", "tile"))
    total = first[1]
    mean_val = first[0] / total
    centred = values - mean_val
    variance = (
        lax.psum(jnp.sum(centred * centred * weights, axis=(0, 1, 2)), ("seg", "tile")) / total
    )
    return (mean_val, lax.rsqrt(variance + EPSILON), total)


def norm_back(grad_out, normed, gain, inv_std, weights, total):
    sums = lax.psum(
        (jnp.sum(grad_out, axis=(0, 1, 2)), jnp.sum(grad_out * normed, axis=(0, 1, 2))),
        ("seg", "tile"),
    )
    bias_grad = sums[0]
    gain_grad = sums[1]
    grad_in = inv_std * gain * (grad_out - weights * (bias_grad + normed * gain_grad) / total)
    return (grad_in, gain_grad, bias_grad)


def block_pass(
    x_input,
    expand_w,
    gain0,
    bias0,
    dw_kernel,
    gain1,
    bias1,
    reduce_w,
    reduce_b,
    restore_w,
    restore_b,
    project_w,
    gain2,
    bias2,
    cotangent,
    seg_count,
    local_len,
    slot_index,
    first_row,
):
    segs, rows, width, chans = x_input.shape
    wide_chans = expand_w.shape[1]
    is_live = slot_index < seg_count[0]
    time_index = first_row + lax.iota(jnp.int32, rows)
    valid = (
        is_live[:, None] & (time_index[None, :] >= 0) & (time_index[None, :] < local_len[:, None])
    )
    own_mask = valid.astype(jnp.float32)[:, :, None, None]
    count_local = jnp.sum(own_mask) * width
    seg_frames = jnp.maximum(jnp.where(is_live, local_len, 0).astype(jnp.float32) * width, 1.0)
    expanded = row_dot(x_input, expand_w)
    mean0, inv0, total = moments(expanded, own_mask, count_local)
    normed0 = (expanded - mean0) * inv0
    act0 = (swish(normed0 * gain0 + bias0) * own_mask).astype(jnp.bfloat16)
    wide_act = extended(act0, (("tile", 1),), 1)
    padded0 = jnp.pad(wide_act, ((0, 0), (0, 0), (1, 1), (0, 0)))
    deep = depthwise(padded0, dw_kernel, rows, width)
    mean1, inv1, _ = moments(deep, own_mask, count_local)
    normed1 = (deep - mean1) * inv1
    pre1 = normed1 * gain1 + bias1
    act1 = swish(pre1) * own_mask
    pool_local = jnp.sum(act1, axis=(1, 2))
    pool_sum = lax.psum(pool_local, "tile")
    pooled = pool_sum / seg_frames[:, None]
    squeeze_pre = jnp.dot(pooled, reduce_w, precision=PRECISE) + reduce_b
    squeezed = swish(squeeze_pre)
    gate = jax.nn.sigmoid(jnp.dot(squeezed, restore_w, precision=PRECISE) + restore_b)
    act2 = (act1 * gate[:, None, None, :]).astype(jnp.bfloat16)
    projected = row_dot(act2, project_w)
    mean2, inv2, _ = moments(projected, own_mask, count_local)
    normed2 = (projected - mean2) * inv2
    branch = (normed2 * gain2 + bias2) * own_mask
    result = x_input.astype(jnp.float32) + branch
    cot_full = cotangent.astype(jnp.float32)
    grad_proj, gain2_grad, bias2_grad = norm_back(
        cot_full * own_mask, normed2, gain2, inv2, own_mask, total
    )
    grad_proj = grad_proj.astype(jnp.bfloat16)
    project_grad = jnp.einsum("stme,stmc->ec", act2, grad_proj, preferred_element_type=jnp.float32)
    grad_act2 = jnp.einsum(
        "stmc,ec->stme", grad_proj, project_w, preferred_element_type=jnp.float32
    )
    gate_local = jnp.sum(grad_act2 * act1, axis=(1, 2))
    gate_sum = lax.psum(gate_local, "tile")
    leader = (lax.axis_index("tile") == 0).astype(jnp.float32)
    gate_pre = gate_sum * gate * (1.0 - gate)
    restore_b_grad = jnp.sum(gate_pre, axis=0) * leader
    restore_w_grad = jnp.dot(squeezed.T, gate_pre, precision=PRECISE) * leader
    squeeze_grad = jnp.dot(gate_pre, restore_w.T, precision=PRECISE) * swish_slope(squeeze_pre)
    reduce_b_grad = jnp.sum(squeeze_grad, axis=0) * leader
    reduce_w_grad = jnp.dot(pooled.T, squeeze_grad, precision=PRECISE) * leader
    pooled_back = jnp.dot(squeeze_grad, reduce_w.T, precision=PRECISE) / seg_frames[:, None]
    grad_act1 = grad_act2 * gate[:, None, None, :] + pooled_back[:, None, None, :]
    grad_pre1 = grad_act1 * own_mask * swish_slope(pre1)
    grad_deep, gain1_grad, bias1_grad = norm_back(grad_pre1, normed1, gain1, inv1, own_mask, total)
    grad_deep = grad_deep.astype(jnp.bfloat16)
    wide_grad = extended(grad_deep, (("tile", 1),), 1)
    padded_grad = jnp.pad(wide_grad, ((0, 0), (0, 0), (1, 1), (0, 0)))
    deep_full = grad_deep.astype(jnp.float32)
    kernel_rows = []
    grad_act0 = jnp.zeros((segs, rows, width, wide_chans), jnp.float32)
    for row in range(3):
        kernel_cols = []
        for col in range(3):
            kernel_cols.append(
                jnp.sum(
                    padded0[:, row : row + rows, col : col + width, :].astype(jnp.float32)
                    * deep_full,
                    axis=(0, 1, 2),
                )
            )
            grad_act0 = grad_act0 + padded_grad[
                :, 2 - row : 2 - row + rows, 2 - col : 2 - col + width, :
            ].astype(jnp.float32) * dw_kernel[row, col].astype(jnp.float32)
        kernel_rows.append(jnp.stack(kernel_cols))
    kernel_grad = jnp.stack(kernel_rows)
    grad_pre0 = grad_act0 * own_mask * swish_slope(normed0 * gain0 + bias0)
    grad_exp, gain0_grad, bias0_grad = norm_back(grad_pre0, normed0, gain0, inv0, own_mask, total)
    grad_exp = grad_exp.astype(jnp.bfloat16)
    expand_grad = jnp.einsum("stmc,stme->ce", x_input, grad_exp, preferred_element_type=jnp.float32)
    x_grad = (
        cot_full
        + jnp.einsum("stme,ce->stmc", grad_exp, expand_w, preferred_element_type=jnp.float32)
    ).astype(jnp.bfloat16)
    act0_full = act0.astype(jnp.float32)
    act2_full = act2.astype(jnp.float32)
    square_sums = jnp.stack(
        [
            jnp.sum(own_mask * result * result),
            jnp.sum(own_mask * act0_full * act0_full),
            jnp.sum(own_mask * act1 * act1),
            jnp.sum(own_mask * act2_full * act2_full),
            jnp.sum(own_mask * branch * branch),
        ]
    )
    summed = lax.psum(
        (
            expand_grad,
            kernel_grad,
            reduce_w_grad,
            reduce_b_grad,
            restore_w_grad,
            restore_b_grad,
            project_grad,
            square_sums,
        ),
        ("seg", "tile"),
    )
    widths = jnp.array([chans, wide_chans, wide_chans, wide_chans, chans], jnp.float32)
    rms_values = jnp.sqrt(summed[7] / (total * widths))
    return (
        result.astype(jnp.bfloat16),
        x_grad,
        summed[0],
        gain0_grad,
        bias0_grad,
        summed[1],
        gain1_grad,
        bias1_grad,
        summed[2],
        summed[3],
        summed[4],
        summed[5],
        summed[6],
        gain2_grad,
        bias2_grad,
        rms_values,
    )


def shards(
    x_input,
    expand_w,
    gain0,
    bias0,
    dw_kernel,
    gain1,
    bias1,
    reduce_w,
    reduce_b,
    restore_w,
    restore_b,
    project_w,
    gain2,
    bias2,
    cotangent,
    seg_count,
    seg_len,
):
    segs = x_input.shape[0]
    rows = x_input.shape[1]
    tile_pos = lax.axis_index("tile")
    slot_index = lax.iota(jnp.int32, segs)
    return block_pass(
        x_input,
        expand_w,
        gain0,
        bias0,
        dw_kernel,
        gain1,
        bias1,
        reduce_w,
        reduce_b,
        restore_w,
        restore_b,
        project_w,
        gain2,
        bias2,
        cotangent,
        seg_count,
        seg_len,
        slot_index,
        tile_pos * rows,
    )


def solution(mesh):
    return jax.shard_map(
        shards,
        mesh=mesh,
        in_specs=(
            P("seg", "tile", None, None),
            P(),
            P(),
            P(),
            P(),
            P(),
            P(),
            P(),
            P(),
            P(),
            P(),
            P(),
            P(),
            P(),
            P("seg", "tile", None, None),
            P("seg"),
            P("seg"),
        ),
        out_specs=(
            P("seg", "tile", None, None),
            P("seg", "tile", None, None),
            P(),
            P(),
            P(),
            P(),
            P(),
            P(),
            P(),
            P(),
            P(),
            P(),
            P(),
            P(),
            P(),
            P(),
        ),
        check_vma=False,
    )
```

profile of v0, /device:TPU:0, one launch (start us, length us, event | category | flops | bytes accessed | tf_op | source)
XLA Modules:
  0.0 481.7 jit_solution(12046652455592117734)
XLA Ops:
  1.4 1.3 fusion.51
  2.7 0.7 and_convert_fusion.1
  4.1 1.2 multiply_reduce_fusion.6
  5.3 42.0 %all-reduce.6 = (f32[144]{0:T(256)S(1)}, f32[]{:T(128)}) all-reduce(f32[144]{0:T(256)S(1)} %get-tuple-element.86, f32[]{:T(128)S(6)} %mul.257), channel_id=1, replica_groups=mesh['seg'=8,'tile'=4] {'seg','tile'}, use_global_device_ids=true, to_apply=%region_1.2 | all-reduce | flops 145 | bytes 1160 | tf_op jit(solution)/shard_map/psum | solution.py:52
  48.2 40.3 %psum.169 = f32[144]{0:T(256)S(1)} all-reduce(f32[144]{0:T(256)S(1)} %multiply_reduce_fusion.5), channel_id=1, replica_groups=mesh['seg'=8,'tile'=4] {'seg','tile'}, use_global_device_ids=true, to_apply=%region_5.6 | all-reduce | flops 144 | bytes 1152 | tf_op jit(solution)/shard_map/psum | solution.py:57
  88.5 1.2 fusion.60
  90.0 1.3 collective-permute-start
  91.3 1.3 collective-permute-start.1
  93.3 3.7 collective-permute-done.1
  97.4 0.9 multiply_reduce_fusion.4
  98.4 40.6 %psum.170 = f32[144]{0:T(256)S(1)} all-reduce(f32[144]{0:T(256)S(1)} %get-tuple-element.70), channel_id=1, replica_groups=mesh['seg'=8,'tile'=4] {'seg','tile'}, use_global_device_ids=true, to_apply=%region_7.8 | all-reduce | flops 144 | bytes 1152 | tf_op jit(solution)/shard_map/psum | solution.py:52
  139.8 40.1 %psum.171 = f32[144]{0:T(256)S(1)} all-reduce(f32[144]{0:T(256)S(1)} %multiply_reduce_fusion.3), channel_id=1, replica_groups=mesh['seg'=8,'tile'=4] {'seg','tile'}, use_global_device_ids=true, to_apply=%region_9.10 | all-reduce | flops 144 | bytes 1152 | tf_op jit(solution)/shard_map/psum | solution.py:57
  179.9 1.2 fusion.62
  181.1 1.6 fusion.64
  182.7 7.4 %psum.172 = f32[8,144]{1,0:T(8,128)} all-reduce(f32[8,144]{1,0:T(8,128)} %get-tuple-element.68), channel_id=1, replica_groups=mesh['seg'=8,'tile'=4] {'tile'}, use_global_device_ids=true, to_apply=%region_11.12 | all-reduce | flops 1152 | bytes 9216 | tf_op jit(solution)/shard_map/psum | solution.py:116
  190.1 0.9 convolution_add_fusion.2
  191.1 0.6 copy-done.19
  191.7 0.8 fusion.5
  193.1 1.5 multiply_reduce_fusion.8
  194.6 39.2 %psum.173 = f32[24]{0:T(128)} all-reduce(f32[24]{0:T(128)} %get-tuple-element.88), channel_id=1, replica_groups=mesh['seg'=8,'tile'=4] {'seg','tile'}, use_global_device_ids=true, to_apply=%region_13.14 | all-reduce | flops 24 | bytes 192 | tf_op jit(solution)/shard_map/psum | solution.py:52
  233.9 1.2 broadcast_divide_fusion.5
  235.6 1.7 multiply_reduce_fusion.7
  237.3 40.6 %psum.174 = f32[24]{0:T(128)} all-reduce(f32[24]{0:T(128)} %multiply_reduce_fusion.7), channel_id=1, replica_groups=mesh['seg'=8,'tile'=4] {'seg','tile'}, use_global_device_ids=true, to_apply=%region_15.16 | all-reduce | flops 24 | bytes 192 | tf_op jit(solution)/shard_map/psum | solution.py:57
  277.9 1.8 fusion.63
  280.2 2.9 fusion.41
  283.0 40.2 %all-reduce.5 = (f32[24]{0:T(128)}, f32[24]{0:T(128)}) all-reduce(f32[24]{0:T(128)} %get-tuple-element.33, f32[24]{0:T(128)} %get-tuple-element.41), channel_id=1, replica_groups=mesh['seg'=8,'tile'=4] {'seg','tile'}, use_global_device_ids=true, to_apply=%region_19.20 | all-reduce | flops 48 | bytes 384 | tf_op jit(solution)/shard_map/psum | solution.py:63
  323.2 1.8 fusion.39
  325.1 0.8 convolution_bitcast_fusion
  325.9 1.9 fusion.14
  327.8 6.4 %psum.177 = f32[8,144]{1,0:T(8,128)S(1)} all-reduce(f32[8,144]{1,0:T(8,128)} %get-tuple-element.23), channel_id=1, replica_groups=mesh['seg'=8,'tile'=4] {'tile'}, use_global_device_ids=true, to_apply=%region_21.22 | all-reduce | flops 1152 | bytes 9216 | tf_op jit(solution)/shard_map/psum | solution.py:137
  334.2 0.7 fusion.57
  334.9 0.9 fusion.68
  335.8 0.9 convolution_multiply_fusion
  336.7 0.9 convolution_multiply_fusion.1
  337.6 0.8 convolution_divide_fusion
  338.5 2.6 fusion.59
  341.1 40.1 %all-reduce.4 = (f32[144]{0:T(256)S(1)}, f32[144]{0:T(256)S(1)}) all-reduce(f32[144]{0:T(256)S(1)} %get-tuple-element.30, f32[144]{0:T(256)S(1)} %get-tuple-element.29), channel_id=1, replica_groups=mesh['seg'=8,'tile'=4] {'seg','tile'}, use_global_device_ids=true, to_apply=%region_25.26 | all-reduce | flops 288 | bytes 2304 | tf_op jit(solution)/shard_map/psum | solution.py:63
  381.3 3.7 fusion.25
  385.2 1.3 collective-permute-start.2
  386.5 1.3 collective-permute-start.3
  387.8 3.4 stack.87
  391.2 0.9 collective-permute-done.3
  392.6 1.5 fusion.58
  394.1 41.9 %all-reduce.3 = (f32[144]{0:T(256)S(1)}, f32[144]{0:T(256)S(1)}) all-reduce(f32[144]{0:T(256)S(1)} %get-tuple-element.28, f32[144]{0:T(256)S(1)} %get-tuple-element.27), channel_id=1, replica_groups=mesh['seg'=8,'tile'=4] {'seg','tile'}, use_global_device_ids=true, to_apply=%region_29.30 | all-reduce | flops 288 | bytes 2304 | tf_op jit(solution)/shard_map/psum | solution.py:63
  436.1 0.9 multiply_convert_fusion
  437.2 0.9 fusion.1
  438.1 42.4 %all-reduce.2 = (f32[24,144]{1,0:T(8,128)}, f32[3,3,144]{2,1,0:T(4,128)}, f32[144,6]{0,1:T(8,128)}, f32[6]{0:T(128)}, f32[6,144]{1,0:T(8,128)}, /*index=5*/f32[144]{0:T(256)}, f32[144,24]{0,1:T(8,128)}, f32[5]{0:T(128)S(1)}) all-reduce(f32[24,144]{1,0:T(8,128)S(1)} %convolution_bitcast_fusion.1,, ...), channel_id=1, replica_groups=mesh['seg'=8,'tile'=4] {'seg','tile'}, use_global_device_ids=true, to_apply=%region_30.31 | all-reduce | flops 10091 | bytes 80728 | tf_op jit(solution)/shard_map/psum | solution.py:189
  480.6 1.1 fusion.54
  (129 shorter events, 5.3 us)
Async XLA Ops:
  0.6 192.5 %copy-start = (bf16[144,24]{0,1:T(8,128)(2,1)S(1)}, bf16[144,24]{0,1:T(8,128)(2,1)}, u32[]{:S(2)}) copy-start(bf16[144,24]{0,1:T(8,128)(2,1)} %param.29) | copy-start | bytes 20740
  4.1 84.5 %copy-start.22 = (f32[144]{0:T(256)S(1)}, f32[144]{0:T(256)}, u32[]{:S(2)}) copy-start(f32[144]{0:T(256)} %param.20) | copy-start | bytes 1732
  4.1 85.6 %copy-start.44 = (f32[144]{0:T(256)S(1)}, f32[144]{0:T(256)}, u32[]{:S(2)}) copy-start(f32[144]{0:T(256)} %param.21) | copy-start | bytes 1732
  48.0 42.0 %copy-start.11 = (f32[144]{0:T(256)}, f32[144]{0:T(256)S(1)}, u32[]{:S(2)}) copy-start(f32[144]{0:T(256)S(1)} %broadcast_divide_fusion.4) | copy-start | bytes 1732
  48.2 44.4 %copy-start.20 = (bf16[3,3,144]{2,1,0:T(4,128)(2,1)S(1)}, bf16[3,3,144]{2,1,0:T(4,128)(2,1)}, u32[]{:S(2)}) copy-start(bf16[3,3,144]{2,1,0:T(4,128)(2,1)} %param.22) | copy-start | bytes 7780
  48.2 44.5 %copy-start.48 = (s32[8]{0:T(128)S(1)}, s32[8]{0:T(128)}, u32[]{:S(2)}) copy-start(s32[8]{0:T(128)} %param.34) | copy-start | bytes 100
  89.7 3.6 copy-start.15
  90.0 3.2 collective-permute-start
  91.3 5.7 %collective-permute-start.1 = (bf16[8,1,16,144]{3,2,1,0:T(8,128)(2,1)S(1)}, bf16[8,1,16,144]{3,2,1,0:T(8,128)(2,1)S(1)}, u32[]{:S(2)}, u32[]{:S(2)}) collective-permute-start(bf16[8,1,16,144]{3,2,1,0:T(8,128)(2,1)S(1)} %get-tuple-element.76), channel_id=1, source_target_pairs={{1,0},{2,1},{3,2},{5,4},{6,5},{7,6},{9,8},{10,9},{11,10},{13,12},{... | collective-permute-start | bytes 110600 | tf_op jit(solution)/shard_map/ppermute | solution.py:20
  92.6 5.6 %copy-start.24 = (f32[1,1,144]{2,1,0:T(1,128)}, f32[1,1,144]{2,1,0:T(1,128)S(1)}, u32[]{:S(2)}) copy-start(f32[1,1,144]{2,1,0:T(1,128)S(1)} %get-tuple-element.77) | copy-start | bytes 1732
  92.7 5.6 %copy-start.26 = (f32[1,1,144]{2,1,0:T(1,128)}, f32[1,1,144]{2,1,0:T(1,128)S(1)}, u32[]{:S(2)}) copy-start(f32[1,1,144]{2,1,0:T(1,128)S(1)} %get-tuple-element.78) | copy-start | bytes 1732
  92.7 5.6 %copy-start.28 = (f32[1,1,144]{2,1,0:T(1,128)}, f32[1,1,144]{2,1,0:T(1,128)S(1)}, u32[]{:S(2)}) copy-start(f32[1,1,144]{2,1,0:T(1,128)S(1)} %get-tuple-element.79) | copy-start | bytes 1732
  92.7 5.6 %copy-start.30 = (f32[1,1,144]{2,1,0:T(1,128)}, f32[1,1,144]{2,1,0:T(1,128)S(1)}, u32[]{:S(2)}) copy-start(f32[1,1,144]{2,1,0:T(1,128)S(1)} %get-tuple-element.80) | copy-start | bytes 1732
  92.7 5.6 %copy-start.32 = (f32[1,1,144]{2,1,0:T(1,128)}, f32[1,1,144]{2,1,0:T(1,128)S(1)}, u32[]{:S(2)}) copy-start(f32[1,1,144]{2,1,0:T(1,128)S(1)} %get-tuple-element.81) | copy-start | bytes 1732
  92.7 5.6 %copy-start.34 = (f32[1,1,144]{2,1,0:T(1,128)}, f32[1,1,144]{2,1,0:T(1,128)S(1)}, u32[]{:S(2)}) copy-start(f32[1,1,144]{2,1,0:T(1,128)S(1)} %get-tuple-element.82) | copy-start | bytes 1732
  92.7 5.6 %copy-start.36 = (f32[1,1,144]{2,1,0:T(1,128)}, f32[1,1,144]{2,1,0:T(1,128)S(1)}, u32[]{:S(2)}) copy-start(f32[1,1,144]{2,1,0:T(1,128)S(1)} %get-tuple-element.83) | copy-start | bytes 1732
  92.7 5.6 %copy-start.38 = (f32[1,1,144]{2,1,0:T(1,128)}, f32[1,1,144]{2,1,0:T(1,128)S(1)}, u32[]{:S(2)}) copy-start(f32[1,1,144]{2,1,0:T(1,128)S(1)} %get-tuple-element.84) | copy-start | bytes 1732
  92.7 5.6 %copy-start.40 = (f32[1,1,144]{2,1,0:T(1,128)}, f32[1,1,144]{2,1,0:T(1,128)S(1)}, u32[]{:S(2)}) copy-start(f32[1,1,144]{2,1,0:T(1,128)S(1)} %get-tuple-element.85) | copy-start | bytes 1732
  93.3 5.1 %copy-start.3 = (bf16[8,1,16,144]{3,2,1,0:T(8,128)(2,1)}, bf16[8,1,16,144]{3,2,1,0:T(8,128)(2,1)S(1)}, u32[]{:S(2)}) copy-start(bf16[8,1,16,144]{3,2,1,0:T(8,128)(2,1)S(1)} %collective-permute-done) | copy-start | bytes 110596
  97.0 1.4 copy-start.5
  98.4 81.5 %copy-start.21 = (f32[144]{0:T(256)S(1)}, f32[144]{0:T(256)}, u32[]{:S(2)}) copy-start(f32[144]{0:T(256)} %param.23) | copy-start | bytes 1732
  139.6 41.5 %copy-start.13 = (f32[144]{0:T(256)}, f32[144]{0:T(256)S(1)}, u32[]{:S(2)}) copy-start(f32[144]{0:T(256)S(1)} %broadcast_divide_fusion.3) | copy-start | bytes 1732
  181.1 1.6 copy-start.17
  323.2 1.8 copy-start.8
  338.5 42.8 %copy-start.4 = (bf16[8,1,16,144]{3,2,1,0:T(8,128)(2,1)S(1)}, bf16[8,1,16,144]{3,2,1,0:T(8,128)(2,1)}, u32[]{:S(2)}) copy-start(bf16[8,1,16,144]{3,2,1,0:T(8,128)(2,1)} %copy-done.3) | copy-start | bytes 110596
  338.5 42.8 %copy-start.6 = (bf16[8,1,16,144]{3,2,1,0:T(8,128)(2,1)S(1)}, bf16[8,1,16,144]{3,2,1,0:T(8,128)(2,1)}, u32[]{:S(2)}) copy-start(bf16[8,1,16,144]{3,2,1,0:T(8,128)(2,1)} %copy-done.5) | copy-start | bytes 110596
  338.5 42.8 %copy-start.14 = (f32[144]{0:T(256)S(1)}, f32[144]{0:T(256)}, u32[]{:S(2)}) copy-start(f32[144]{0:T(256)} %copy-done.13) | copy-start | bytes 1732
  338.5 42.8 %copy-start.18 = (f32[144]{0:T(256)S(1)}, f32[144]{0:T(256)}, u32[]{:S(2)}) copy-start(f32[144]{0:T(256)} %copy-done.17) | copy-start | bytes 1732
  338.5 42.8 %copy-start.47 = (f32[144]{0:T(256)S(1)}, f32[144]{0:T(256)}, u32[]{:S(2)}) copy-start(f32[144]{0:T(256)} %get-tuple-element.63) | copy-start | bytes 1732
  381.3 3.8 copy-start.49
  381.3 3.8 copy-start.50
  385.0 7.5 %copy-start.12 = (f32[144]{0:T(256)S(1)}, f32[144]{0:T(256)}, u32[]{:S(2)}) copy-start(f32[144]{0:T(256)} %copy-done.11) | copy-start | bytes 1732
  385.0 7.5 %copy-start.16 = (f32[144]{0:T(256)S(1)}, f32[144]{0:T(256)}, u32[]{:S(2)}) copy-start(f32[144]{0:T(256)} %copy-done.15) | copy-start | bytes 1732
  385.0 7.5 %copy-start.23 = (f32[144]{0:T(256)S(1)}, f32[144]{0:T(256)}, u32[]{:S(2)}) copy-start(f32[144]{0:T(256)} %param.20) | copy-start | bytes 1732
  385.0 7.5 %copy-start.25 = (f32[1,1,144]{2,1,0:T(1,128)S(1)}, f32[1,1,144]{2,1,0:T(1,128)}, u32[]{:S(2)}) copy-start(f32[1,1,144]{2,1,0:T(1,128)} %copy-done.24) | copy-start | bytes 1732
  385.0 7.5 %copy-start.27 = (f32[1,1,144]{2,1,0:T(1,128)S(1)}, f32[1,1,144]{2,1,0:T(1,128)}, u32[]{:S(2)}) copy-start(f32[1,1,144]{2,1,0:T(1,128)} %copy-done.26) | copy-start | bytes 1732
  385.1 7.5 %copy-start.29 = (f32[1,1,144]{2,1,0:T(1,128)S(1)}, f32[1,1,144]{2,1,0:T(1,128)}, u32[]{:S(2)}) copy-start(f32[1,1,144]{2,1,0:T(1,128)} %copy-done.28) | copy-start | bytes 1732
  385.1 7.5 %copy-start.31 = (f32[1,1,144]{2,1,0:T(1,128)S(1)}, f32[1,1,144]{2,1,0:T(1,128)}, u32[]{:S(2)}) copy-start(f32[1,1,144]{2,1,0:T(1,128)} %copy-done.30) | copy-start | bytes 1732
  385.1 7.5 %copy-start.33 = (f32[1,1,144]{2,1,0:T(1,128)S(1)}, f32[1,1,144]{2,1,0:T(1,128)}, u32[]{:S(2)}) copy-start(f32[1,1,144]{2,1,0:T(1,128)} %copy-done.32) | copy-start | bytes 1732
  385.1 7.5 %copy-start.35 = (f32[1,1,144]{2,1,0:T(1,128)S(1)}, f32[1,1,144]{2,1,0:T(1,128)}, u32[]{:S(2)}) copy-start(f32[1,1,144]{2,1,0:T(1,128)} %copy-done.34) | copy-start | bytes 1732
  385.1 7.5 %copy-start.37 = (f32[1,1,144]{2,1,0:T(1,128)S(1)}, f32[1,1,144]{2,1,0:T(1,128)}, u32[]{:S(2)}) copy-start(f32[1,1,144]{2,1,0:T(1,128)} %copy-done.36) | copy-start | bytes 1732
  385.1 7.5 %copy-start.39 = (f32[1,1,144]{2,1,0:T(1,128)S(1)}, f32[1,1,144]{2,1,0:T(1,128)}, u32[]{:S(2)}) copy-start(f32[1,1,144]{2,1,0:T(1,128)} %copy-done.38) | copy-start | bytes 1732
  385.1 7.5 %copy-start.41 = (f32[1,1,144]{2,1,0:T(1,128)S(1)}, f32[1,1,144]{2,1,0:T(1,128)}, u32[]{:S(2)}) copy-start(f32[1,1,144]{2,1,0:T(1,128)} %copy-done.40) | copy-start | bytes 1732
  385.1 7.5 %copy-start.45 = (f32[144]{0:T(256)S(1)}, f32[144]{0:T(256)}, u32[]{:S(2)}) copy-start(f32[144]{0:T(256)} %param.21) | copy-start | bytes 1732
  385.2 6.0 %collective-permute-start.2 = (bf16[8,1,16,144]{3,2,1,0:T(8,128)(2,1)S(1)}, bf16[8,1,16,144]{3,2,1,0:T(8,128)(2,1)S(1)}, u32[]{:S(2)}, u32[]{:S(2)}) collective-permute-start(bf16[8,1,16,144]{3,2,1,0:T(8,128)(2,1)S(1)} %get-tuple-element.73), channel_id=1, source_target_pairs={{0,1},{1,2},{2,3},{4,5},{5,6},{6,7},{8,9},{9,10},{10,11},{12,13},{... | collective-permute-start | bytes 110600 | tf_op jit(solution)/shard_map/ppermute | solution.py:18
  386.5 5.7 %collective-permute-start.3 = (bf16[8,1,16,144]{3,2,1,0:T(8,128)(2,1)S(1)}, bf16[8,1,16,144]{3,2,1,0:T(8,128)(2,1)S(1)}, u32[]{:S(2)}, u32[]{:S(2)}) collective-permute-start(bf16[8,1,16,144]{3,2,1,0:T(8,128)(2,1)S(1)} %get-tuple-element.74), channel_id=1, source_target_pairs={{1,0},{2,1},{3,2},{5,4},{6,5},{7,6},{9,8},{10,9},{11,10},{13,12},{... | collective-permute-start | bytes 110600 | tf_op jit(solution)/shard_map/ppermute | solution.py:20
  392.6 43.4 %copy-start.46 = (f32[144]{0:T(256)S(1)}, f32[144]{0:T(256)}, u32[]{:S(2)}) copy-start(f32[144]{0:T(256)} %get-tuple-element.60) | copy-start | bytes 1732
  437.0 43.6 %copy-start.53 = (f32[5]{0:T(128)S(1)}, f32[5]{0:T(128)}, u32[]{:S(2)}) copy-start(f32[5]{0:T(128)} %constant.5.clone) | copy-start | bytes 64
  (10 other events, 8.5 us)
where the time goes:
time: 484 us; the launch traced here: 482 us
  blocking collectives  421 us (87%)
  other arithmetic  30 us (6%)
  matrix products  11.9 us (2%)
  local copies, waits for them, and re-layouts  5.88 us (1%)
  starting transfers between devices  5.17 us (1%)
    psum x3, blocking collectives, norm_back(): lax.psum((jnp.sum(grad_out, axis=(0, 1, 2)), jnp.sum(grad_out * normed, a...  122 us
    psum x3, blocking collectives, moments(): first = lax.psum((local_sum, count_local), ('seg', 'tile'))  122 us
    psum x3, blocking collectives, moments(): lax.psum(jnp.sum(centred * centred * weights, axis=(0, 1, 2)), ('seg', 't...  121 us
    psum x1, blocking collectives, block_pass(): lax.psum((expand_grad, kernel_grad, reduce_w_grad, reduce_b_grad, restore...  42.4 us
  transfers between devices with their start and end apart: 4, of which 2 were waited for; matrix products, arithmetic and copies ran while one was open for 1% of the time, Pallas kernels for 0%

commit v1 on v0

v1 whole, which is shorter than its diff:
```python
import functools
from typing import NamedTuple

import jax
import jax.numpy as jnp
from jax import lax
from jax.experimental import pallas as pl
from jax.experimental.pallas import tpu as pltpu
from jax.sharding import PartitionSpec as P

EPSILON = 0.001
BOTH = ("seg", "tile")
LANES = 128
F32 = jnp.float32
BF16 = jnp.bfloat16
VMEM = pl.BlockSpec(memory_space=pltpu.VMEM)
SMEM = pl.BlockSpec(memory_space=pltpu.SMEM)
HBM = pl.BlockSpec(memory_space=pltpu.HBM)


class Sizes(NamedTuple):
    devices: int
    tiles: int
    segs: int
    own: int
    rows: int
    width: int
    chans: int
    wide: int
    squeeze: int


def iota(shape, dim):
    return lax.broadcasted_iota(jnp.int32, shape, dim)


def dot(left, right, left_dim, right_dim, precise=False):
    return lax.dot_general(
        left,
        right,
        (((left_dim,), (right_dim,)), ((), ())),
        precision=lax.Precision.HIGHEST if precise else None,
        preferred_element_type=F32,
    )


def eye(rows, cols, dtype=F32):
    return (iota((rows, cols), 0) == iota((rows, cols), 1)).astype(dtype)


def spread(column):
    return jnp.broadcast_to(column, (column.shape[0], LANES))


def lane_sum(values):
    return jnp.sum(values, axis=1, keepdims=True)


def sigmoid(values):
    return 0.5 * jnp.tanh(0.5 * values) + 0.5


def vector(ref):
    return ref[...].astype(F32).reshape(1, ref.shape[0])


def thirds(values):
    high = values.astype(BF16)
    rest = values - high.astype(F32)
    middle = rest.astype(BF16)
    return [high, middle, (rest - middle.astype(F32)).astype(BF16)]


def doubled(values):
    high = values.astype(BF16)
    return jnp.concatenate([high, (values - high.astype(F32)).astype(BF16)], axis=1)


def tripled(values):
    return jnp.concatenate(thirds(values), axis=1)


def row_sums(values):
    return dot(jnp.ones((8, 3 * LANES), BF16), tripled(values), 1, 1)[0:1]


def padded_rows(rows, count):
    spare = count - sum(row.shape[0] for row in rows)
    if spare:
        rows = rows + [jnp.zeros((spare, rows[0].shape[1]), F32)]
    return jnp.concatenate(rows, axis=0)


def spread_by(rows, unit):
    held = jnp.concatenate(thirds(rows), axis=0)
    return dot(held, jnp.concatenate([unit] * 3, axis=0), 0, 0)


def spread_rows(rows):
    count = len(rows)
    shape = (16, count * LANES)
    unit = jnp.where(iota(shape, 0) == lax.div(iota(shape, 1), LANES), 1.0, 0.0).astype(BF16)
    wide = spread_by(padded_rows(rows, 16), unit)
    return [wide[:, at * LANES : (at + 1) * LANES] for at in range(count)]


def columns_of(rows):
    held = padded_rows(rows, 8)
    width = held.shape[1]
    spare = (-width) % LANES
    if spare:
        held = jnp.concatenate([held, jnp.zeros((8, spare), F32)], axis=1)
    return held.T[:width]


def placed_cells(cells, first):
    rows = cells.shape[0]
    parts = [jnp.zeros((first, LANES), F32)] if first else []
    parts += [cells, jnp.zeros((LANES - first - rows, LANES), F32)]
    return jnp.concatenate(parts, axis=0).astype(BF16)


def placed_sums(acc_ref, count, start):
    lane = iota((2 * LANES, LANES), 1)
    result = 0.0
    for at in range(count):
        unit = jnp.where(lane == start + at, 1.0, 0.0).astype(BF16)
        result = result + dot(doubled(acc_ref[at]), unit, 1, 0)
    return result


def lane_at(sz):
    lane = iota((1, LANES), 1)
    step = sz.width * sz.own
    return lax.rem(lane, sz.width), lax.rem(lax.div(lane, sz.width), sz.own), lax.div(lane, step)


def seg_lanes(sz, rows):
    slot = lax.rem(lax.div(iota((rows, LANES), 1), sz.width), sz.own)
    return jnp.where(slot == iota((rows, LANES), 0), 1.0, 0.0).astype(BF16)


def seg_sums(sz, values):
    lanes = seg_lanes(sz, 16)
    return dot(jnp.concatenate([lanes] * 3, axis=1), tripled(values), 1, 1)[0:8]


def seg_spread(sz, rows):
    return spread_by(padded_rows([rows], 16), seg_lanes(sz, 16))


def mask_rows(sz, info):
    return [info[t : t + 1] for t in range(sz.rows)]


def half_of(ref, t, e):
    first = e - e % 16
    return ref[t, first : first + 16].astype(F32)[e - first : e - first + 8]


def shift_unit(sz):
    source = iota((LANES, 2 * LANES), 0)
    column = iota((LANES, 2 * LANES), 1)
    lane = lax.rem(column, LANES)
    spot = lax.rem(lane, sz.width)
    left = jnp.where((source == lane - 1) & (spot != 0), 1.0, 0.0)
    right = jnp.where((source == lane + 1) & (spot != sz.width - 1), 1.0, 0.0)
    return jnp.where(column < LANES, left, right).astype(BF16)


def block_unit(sz):
    source = iota((LANES, 2 * LANES), 0)
    column = iota((LANES, 2 * LANES), 1)
    lane = lax.rem(column, LANES)
    step = sz.width * sz.own
    before = jnp.where(source == lane - step, 1.0, 0.0)
    after = jnp.where(source == lane + step, 1.0, 0.0)
    return jnp.where(column < LANES, before, after).astype(BF16)


def field_shifts(sz, fields, sh_ref, unit_ref, exact):
    deep = LANES if exact else 2 * LANES

    def parts(values):
        return values.astype(BF16) if exact else doubled(values)

    before = dot(parts(fields[-1]), unit_ref[0:deep, 2 * LANES : 3 * LANES], 1, 0)
    after = dot(parts(fields[0]), unit_ref[0:deep, 3 * LANES :], 1, 0)
    rows = [before] + fields + [after]
    cells = parts(jnp.concatenate(rows, axis=0))
    sides = dot(cells, unit_ref[0:deep, 0 : 2 * LANES], 1, 0)
    for t, row in enumerate(rows):
        part = slice(t * sz.wide, (t + 1) * sz.wide)
        sh_ref[0, t] = sides[part, :LANES]
        sh_ref[1, t] = row
        sh_ref[2, t] = sides[part, LANES:]


def backward_parts(sz, sh_ref, tap_ref, part, acts, acc_ref):
    result = [0.0] * sz.rows
    for i in range(3):
        for j in range(3):
            tap = tap_ref[3 * i + j, part]
            held = 0.0
            for t in range(sz.rows):
                field = sh_ref[2 - j, t + 2 - i, part]
                result[t] = result[t] + field * tap
                if acts is not None:
                    held = held + field * acts[t]
            if acts is not None:
                acc_ref[3 * i + j, part] = held
    return result


def every(sz, ref, first, step):
    return ref[pl.ds(first, sz.devices, stride=step), :]


def wide_rows(first, second, half, last):
    tail = [first[:, LANES:], second[:, LANES:], jnp.zeros((1, LANES - 2 * half), F32)]
    tail = jnp.concatenate(tail, axis=1)
    return jnp.concatenate([first[:, :LANES], second[:, :LANES], tail, last], axis=0)


def wide_pair(block, half):
    first = jnp.concatenate([block[0:1], block[2:3, :half]], axis=1)
    second = jnp.concatenate([block[1:2], block[2:3, half : 2 * half]], axis=1)
    return first, second


def wide_moments(sz, ref, half):
    sums, squares, tails, counts = (every(sz, ref, at, 4) for at in range(4))
    total = jnp.sum(counts, axis=0, keepdims=True)
    inverse = 1.0 / jnp.maximum(counts, 1.0)
    means = []
    spares = []
    for held in (sums, tails):
        mean_val = jnp.sum(held, axis=0, keepdims=True) / total
        offset = held - counts * mean_val
        means.append(mean_val)
        spares.append(jnp.sum(offset * offset * inverse, axis=0, keepdims=True))
    low = jnp.sum(squares, axis=0, keepdims=True) + spares[0]
    high = jnp.sum(tails, axis=0, keepdims=True)[:, half : 2 * half] + spares[1][:, :half]
    square = jnp.concatenate([low, high], axis=1)
    mean_row = jnp.concatenate([means[0], means[1][:, :half]], axis=1)
    total_row = jnp.concatenate([total, total[:, :half]], axis=1)
    return mean_row, lax.rsqrt(square / total_row + EPSILON), total_row


def send_block(ref, block):
    count = block.shape[0]
    if count < 8:
        block = jnp.concatenate([block] * (8 // count), axis=0)
    for at in range(0, ref.shape[0], 8):
        ref[at : at + 8] = block


def partner(sz, step):
    return lax.rem(lax.axis_index("tile") + step, sz.tiles)


def entry_kernel(sz, x_hbm, w_hbm, len_hbm, count_hbm, pay_ref, *scratch):
    x_ref, w_ref, len_ref, count_ref, sems = scratch
    copies = [
        pltpu.make_async_copy(x_hbm, x_ref, sems.at[0]),
        pltpu.make_async_copy(w_hbm, w_ref, sems.at[1]),
        pltpu.make_async_copy(len_hbm, len_ref, sems.at[2]),
        pltpu.make_async_copy(count_hbm, count_ref, sems.at[3]),
    ]
    for copy in copies:
        copy.start()
    for copy in reversed(copies):
        copy.wait()
    tile_pos = lax.axis_index("tile")
    lane_seg = lax.div(iota((1, LANES), 1), sz.width)
    length = jnp.zeros((1, LANES), jnp.int32)
    count = jnp.zeros((), jnp.int32)
    for s in range(sz.segs):
        held = jnp.where(s < count_ref[0], len_ref[s], 0)
        length = jnp.where(lane_seg == s, held, length)
        count = count + jnp.clip(held - tile_pos * sz.rows, 0, sz.rows)
    count = (count * sz.width).astype(F32)
    masks = [(tile_pos * sz.rows + t < length).astype(F32) for t in range(sz.rows)]
    unit = eye(sz.chans, sz.chans, BF16)
    cells = [dot(unit, x_ref[:, t].reshape(LANES, sz.chans), 1, 1) for t in range(sz.rows)]
    sums = lane_sum(sum(cells[t] * masks[t] for t in range(sz.rows)))
    mean_val = spread(sums / jnp.maximum(count, 1.0))
    centred = [(cells[t] - mean_val) * masks[t] for t in range(sz.rows)]
    centred = jnp.concatenate(centred, axis=1)
    spare = dot(centred, centred, 1, 1, True)
    weights = w_ref[...].astype(F32)
    wide_sum = dot(jnp.broadcast_to(sums, (sz.chans, 8)), weights, 0, 0, True)[0:1]
    square = jnp.sum(dot(spare, weights, 1, 0, True) * weights, axis=0, keepdims=True)
    last = jnp.full((1, LANES), count, F32)
    send_block(pay_ref, wide_rows(wide_sum, square, sz.wide - LANES, last))


def send_kernel(sz, x_ref, c_ref, after_ref, *out_refs):
    del after_ref
    for step, out_ref in enumerate(out_refs):
        first = partner(sz, step) * sz.own
        out_ref[...] = jnp.zeros(out_ref.shape, BF16)
        for t in range(sz.rows):
            at = (t % 2) * 2 * sz.chans
            out_ref[:, t // 2, :, at : at + sz.chans] = x_ref[pl.ds(first, sz.own), t]
            at = at + sz.chans
            out_ref[:, t // 2, :, at : at + sz.chans] = c_ref[pl.ds(first, sz.own), t]


def setup_kernel(sz, *refs):
    wide_refs, small_refs, dw_ref, rw_ref, sw_ref, pw_in, w_in, len_ref, count_ref = (
        refs[0:5],
        refs[5:8],
        *refs[8:15],
    )
    par_ref, tap_ref, unit_ref, info_ref, pw_ref, w_ref = refs[15:]
    par_ref[...] = jnp.zeros(par_ref.shape, F32)
    for at, ref in enumerate(wide_refs):
        par_ref[at : at + 1] = vector(ref)
    for at, ref in enumerate(small_refs):
        par_ref[5 + at : 6 + at, 0 : ref.shape[0]] = vector(ref)
    par_ref[8 : 8 + sz.squeeze] = rw_ref[...]
    par_ref[16 : 16 + sz.squeeze] = sw_ref[...]
    pw_ref[...] = pw_in[...]
    w_ref[...] = w_in[...]
    taps = spread_rows([dw_ref[i, j : j + 1].astype(F32) for i in range(3) for j in range(3)])
    for at in range(9):
        tap_ref[at] = taps[at]
    for at, unit in enumerate([shift_unit(sz), block_unit(sz)]):
        part = slice(at * 2 * LANES, (at + 1) * 2 * LANES)
        unit_ref[0:LANES, part] = unit
        unit_ref[LANES:, part] = unit
    first = lax.axis_index("tile") * sz.own
    _, slot, block = lane_at(sz)
    length = jnp.zeros((1, LANES), jnp.int32)
    count = jnp.zeros((), jnp.int32)
    at = iota((8, LANES), 0)
    frames = jnp.ones((8, LANES), F32)
    for s in range(sz.own):
        held = jnp.where(first + s < count_ref[0], len_ref[first + s], 0)
        length = jnp.where(slot == s, held, length)
        count = count + jnp.minimum(held, sz.rows * sz.tiles)
        frame = jnp.maximum((held * sz.width).astype(F32), 1.0)
        frames = jnp.where(at == s, frame, frames)
    for t in range(sz.rows):
        info_ref[t : t + 1] = (block * sz.rows + t < length).astype(F32)
    info_ref[7:8] = jnp.full((1, LANES), (count * sz.width).astype(F32))
    info_ref[8:16] = frames


def gather_kernel(sz, *refs):
    own_refs, (w_ref, exp_ref, xc_ref, all_ref) = refs[: sz.tiles], refs[sz.tiles :]
    for step, ref in enumerate(own_refs):
        all_ref[partner(sz, sz.tiles - step)] = ref[...]
    unit = eye(LANES, LANES, BF16)
    weights = w_ref[...]
    for g in range(sz.rows // 2):
        flat = dot(unit, all_ref[:, :, g].reshape(LANES, LANES), 1, 1)
        for par in range(2):
            at = par * 2 * sz.chans
            t = 2 * g + par
            x_at = flat[at : at + sz.chans]
            xc_ref[t] = flat[at : at + 2 * sz.chans].astype(BF16)
            exp_ref[t] = dot(weights, x_at.astype(BF16), 0, 0)


def stage_one_kernel(sz, pay_ref, exp_ref, xc_ref, par_ref, tap_ref, unit_ref, info_ref, *refs):
    out_pay, act0_ref, deep_ref, ec_ref, s0_ref, row_ref, near_ref, part_ref = refs[:8]
    mat_ref, acc_ref, sh_ref, buf_ref = refs[8:]
    chans = sz.chans
    half = sz.wide - LANES
    mean0, inv0, total = wide_moments(sz, pay_ref, half)
    row_ref[0:1] = mean0
    row_ref[1:2] = inv0
    row_ref[2:3] = total
    info = info_ref[...]
    masks = mask_rows(sz, info)
    count = info[7:8]
    mean_c, slope_c, bias_c = spread_rows([mean0, inv0 * par_ref[0:1], par_ref[1:2]])
    acts = []
    squares = 0.0
    for t in range(sz.rows):
        centred = exp_ref[t] - mean_c
        pre = centred * slope_c + bias_c
        gate = sigmoid(pre)
        held = pre * gate
        ec_ref[t] = centred
        s0_ref[t] = (gate + held * (1.0 - gate)) * masks[t]
        act = (held * masks[t]).astype(BF16)
        act0_ref[t] = act
        act = act.astype(F32)
        squares = squares + act * act
        acts.append(act)
    field_shifts(sz, acts, sh_ref, unit_ref, True)
    step = sz.width * sz.own
    spot, _, block = lane_at(sz)
    full = [jnp.broadcast_to(mask, (8, LANES)) for mask in masks]
    before = jnp.where(block == 0, 0.0, pltpu.roll(full[-1], step, 1))
    after = jnp.where(block == sz.tiles - 1, 0.0, pltpu.roll(full[0], LANES - step, 1))
    full = [before] + full + [after]
    left = [jnp.where(spot == 0, 0.0, row) for row in full]
    right = [jnp.where(spot == sz.width - 1, 0.0, row) for row in full]
    moved = [right, full, left]
    total_sum = []
    for e in range(0, sz.wide, 8):
        part = slice(e, e + 8)
        taps = [tap_ref[at, part] for at in range(9)]
        acts = [half_of(act0_ref, t, e) for t in range(sz.rows)]
        sums = 0.0
        for t in range(sz.rows):
            deep = 0.0
            back = 0.0
            for i in range(3):
                for j in range(3):
                    deep = deep + sh_ref[j, t + i, part] * taps[3 * i + j]
                    back = back + moved[j][t + 2 - i] * taps[3 * i + j]
            deep_ref[t, part] = deep
            sums = sums + deep * masks[t]
            mat_ref[t, part] = back * s0_ref[t, part]
        total_sum.append(sums)
        for i in range(3):
            for j in range(3):
                held = sum(moved[j][t + 2 - i] * acts[t] for t in range(sz.rows))
                acc_ref[3 * i + j, part] = held
    total_sum = jnp.concatenate(total_sum, axis=0)
    mean_own = lane_sum(total_sum) / jnp.maximum(count[:, 0:1], 1.0)
    square = 0.0
    for t in range(sz.rows):
        centred = (deep_ref[t] - mean_own) * masks[t]
        square = square + centred * centred
    send_block(out_pay, wide_rows(row_sums(total_sum), row_sums(square), half, count))
    part_ref[...] = placed_sums(acc_ref, 9, 3 * chans + 9)
    held = jnp.zeros((sz.wide, LANES), F32)
    second = jnp.zeros((chans, chans), F32)
    x_sum = 0.0
    for t in range(sz.rows):
        x_at = xc_ref[t].astype(F32)[:chans]
        cells = placed_cells(x_at, 0)
        held = held + dot(doubled(mat_ref[t]), jnp.concatenate([cells, cells], axis=1), 1, 1)
        kept = x_at * masks[t]
        second = second + dot(kept.astype(BF16), x_at.astype(BF16), 1, 1)
        x_sum = x_sum + kept
    near_ref[...] = jnp.zeros(near_ref.shape, F32)
    buf_ref[...] = held
    for k in range(5):
        rows = min(32, sz.wide - 32 * k)
        near_ref[0:rows, chans * k : chans * (k + 1)] = buf_ref[32 * k : 32 * k + rows, 0:chans]
    near_ref[16:32, 4 * chans : 5 * chans] = second[0:16]
    near_ref[0:chans, 5 * chans : LANES] = second[:, 16:]
    x_row = row_sums(x_sum)
    for k in range(3):
        near_ref[chans + k : chans + k + 1, 5 * chans : LANES] = x_row[:, 8 * k : 8 * k + 8]
    squares = jnp.sum(squares.reshape(sz.wide // 8, 8, LANES), axis=0)
    squares = jnp.sum(lane_sum(squares), axis=0, keepdims=True)
    near_ref[chans + 3 : chans + 4, 5 * chans : 5 * chans + 1] = squares


def stage_two_kernel(
    sz,
    pay_ref,
    deep_ref,
    xc_ref,
    par_ref,
    tap_ref,
    unit_ref,
    info_ref,
    pw_ref,
    near_ref,
    act0_ref,
    s0_ref,
    part_ref,
    out_pay,
    act1_ref,
    dc_ref,
    s1_ref,
    proj_ref,
    gate_ref,
    seg_ref,
    row_ref,
    buf_ref,
    sq_ref,
    mat_ref,
    acc_ref,
    sh_ref,
):
    chans = sz.chans
    half = sz.wide - LANES
    mean1, inv1, _ = wide_moments(sz, pay_ref, half)
    row_ref[0:1] = mean1
    row_ref[1:2] = inv1
    info = info_ref[...]
    masks = mask_rows(sz, info)
    count = info[7:8]
    mean_c, slope_c, bias_c = spread_rows([mean1, inv1 * par_ref[2:3], par_ref[3:4]])
    pool = 0.0
    squares = 0.0
    fields = []
    for t in range(sz.rows):
        centred = deep_ref[t] - mean_c
        pre = centred * slope_c + bias_c
        gate = sigmoid(pre)
        held = pre * gate
        dc_ref[t] = centred
        s1_ref[t] = (gate + held * (1.0 - gate)) * masks[t]
        act = held * masks[t]
        act1_ref[t] = act
        pool = pool + act
        squares = squares + act * act
        fields.append(centred * masks[t])
    pooled = seg_sums(sz, pool) / info[8:16, 0:1]
    rw = par_ref[8:16]
    sw = par_ref[16:24]
    squeeze_pre = dot(pooled, rw, 1, 1, True) + par_ref[7:8, 0:8]
    squeezed = squeeze_pre * sigmoid(squeeze_pre)
    gate = sigmoid(dot(squeezed, sw, 1, 0, True) + par_ref[4:5])
    seg_ref[0] = pooled
    seg_ref[1] = gate
    seg_ref[2, :, 0:8] = squeeze_pre
    gate_wide = seg_spread(sz, gate)
    gate_ref[...] = gate_wide
    sums = 0.0
    sum_g = 0.0
    gated = 0.0
    for t in range(sz.rows):
        act = (act1_ref[t] * gate_wide).astype(BF16)
        cells = dot(pw_ref[...], act, 1, 0)
        proj_ref[t] = cells
        sums = sums + cells * masks[t]
        sum_g = sum_g + xc_ref[t].astype(F32)[chans:] * masks[t]
        act = act.astype(F32)
        gated = gated + act * act
    sq_ref[0:8] = jnp.sum(squares.reshape(sz.wide // 8, 8, LANES), axis=0)
    sq_ref[8:16] = jnp.sum(gated.reshape(sz.wide // 8, 8, LANES), axis=0)
    mean_own = lane_sum(sums) / jnp.maximum(count[:, 0:1], 1.0)
    square = 0.0
    sum_gp = 0.0
    for t in range(sz.rows):
        centred = (proj_ref[t] - mean_own) * masks[t]
        square = square + centred * centred
        sum_gp = sum_gp + centred * xc_ref[t].astype(F32)[chans:]
    row = row_sums(jnp.concatenate([sums, square, sum_g, sum_gp], axis=0))
    row = jnp.concatenate([row, count[:, 4 * chans :]], axis=1)
    each = near_ref.shape[0] // sz.devices
    out_pay[pl.ds(0, sz.devices, stride=2), :] = jnp.broadcast_to(row, (sz.devices, LANES))
    out_pay[pl.ds(1, sz.devices, stride=2), :] = near_ref[...]
    field_shifts(sz, fields, sh_ref, unit_ref, False)
    for e in range(0, sz.wide, 8):
        part = slice(e, e + 8)
        acts = [half_of(act0_ref, t, e) for t in range(sz.rows)]
        back = backward_parts(sz, sh_ref, tap_ref, part, acts, acc_ref)
        for t in range(sz.rows):
            mat_ref[t, part] = back[t] * s0_ref[t, part]
    buf = part_ref[...] + placed_sums(acc_ref, 9, 3 * chans + 18)
    for t in range(sz.rows):
        cells = placed_cells(xc_ref[t].astype(F32)[:chans], chans)
        buf = buf + dot(doubled(mat_ref[t]), jnp.concatenate([cells, cells], axis=1), 1, 1)
    buf_ref[...] = buf


def stage_three_kernel(
    sz,
    pay_ref,
    proj_ref,
    xc_ref,
    act0_ref,
    act1_ref,
    s0_ref,
    dc_ref,
    s1_ref,
    gate_ref,
    seg_ref,
    par_ref,
    tap_ref,
    unit_ref,
    info_ref,
    pw_ref,
    part_ref,
    sq_ref,
    row_ref,
    out_pay,
    res_ref,
    scaled_ref,
    bg2_ref,
    gg2_ref,
    ga_ref,
    mat_ref,
    acc_ref,
    sh_ref,
    buf_ref,
):
    chans = sz.chans
    half = sz.wide - LANES
    info = info_ref[...]
    masks = mask_rows(sz, info)
    parts = every(sz, pay_ref, 0, 2)
    near = every(sz, pay_ref, 1, 2)
    sums = jnp.sum(parts, axis=0, keepdims=True)
    counts = pltpu.roll(parts, LANES - 4 * chans, 1)
    grads = pltpu.roll(parts, LANES - 2 * chans, 1)
    total = sums[:, 4 * chans : 4 * chans + 1]
    mean_row = sums / total
    offset = parts - counts * mean_row
    scaled = offset / jnp.maximum(counts, 1.0)
    spare = jnp.sum(offset * scaled, axis=0, keepdims=True)
    cross = jnp.sum(scaled * grads, axis=0, keepdims=True)
    square = sums[:, chans : 2 * chans] + spare[:, :chans]
    inv2 = lax.rsqrt(square / total + EPSILON)
    bias_grad = sums[:, 2 * chans : 3 * chans]
    gain_grad = inv2 * (sums[:, 3 * chans : 4 * chans] + cross[:, :chans])
    bg2_ref[...] = bias_grad.reshape(chans)
    gg2_ref[...] = gain_grad.reshape(chans)
    rows = [mean_row[:, :chans], inv2, bias_grad / total, gain_grad / total]
    rows += [par_ref[5:6, :chans], par_ref[6:7, :chans]]
    columns = columns_of(rows)
    mean_c, inv_c, bg_c, gg_c, gain_c, bias_c = (
        spread(columns[:, at : at + 1]) for at in range(6)
    )
    scale = inv_c * gain_c
    gate_wide = gate_ref[...]
    branch_sq = 0.0
    result_sq = 0.0
    gate_sum = 0.0
    buf = part_ref[...]
    for t in range(sz.rows):
        both = xc_ref[t].astype(F32)
        normed = (proj_ref[t] - mean_c) * inv_c
        branch = (normed * gain_c + bias_c) * masks[t]
        result = both[:chans] + branch
        res_ref[t] = result
        branch_sq = branch_sq + branch * branch
        result_sq = result_sq + result * result * masks[t]
        grad = scale * (both[chans:] - (bg_c + normed * gg_c)) * masks[t]
        wide_grad = dot(pw_ref[...], grad.astype(BF16), 0, 0)
        ga_ref[t] = wide_grad
        act = act1_ref[t]
        gate_sum = gate_sum + wide_grad * act
        act = (act * gate_wide).astype(BF16)
        buf = buf + dot(act, placed_cells(grad, 2 * chans), 1, 1)
    rw = par_ref[8:16]
    sw = par_ref[16:24]
    pooled = seg_ref[0]
    gate = seg_ref[1]
    squeeze_pre = seg_ref[2, :, 0:8]
    slope = sigmoid(squeeze_pre)
    squeezed = squeeze_pre * slope
    slope = slope + squeezed * (1.0 - slope)
    live = (iota((8, 1), 0) < sz.own).astype(F32)
    gate_pre = seg_sums(sz, gate_sum) * gate * (1.0 - gate)
    squeeze_grad = dot(gate_pre, sw, 1, 1, True) * slope * live
    back = dot(squeeze_grad, rw, 1, 0, True) / info[8:16, 0:1]
    back_wide = seg_spread(sz, back)
    (scale_c,) = spread_rows([row_ref[1:2] * par_ref[2:3]])
    sum_b = 0.0
    sum_g = 0.0
    fields = []
    for t in range(sz.rows):
        grad = (ga_ref[t] * gate_wide + back_wide) * s1_ref[t]
        scaled_ref[t] = grad * scale_c
        sum_b = sum_b + grad
        sum_g = sum_g + grad * dc_ref[t]
        fields.append(grad)
    sum_b = row_sums(sum_b)
    sum_g = row_sums(sum_g) * row_ref[1:2]
    field_shifts(sz, fields, sh_ref, unit_ref, False)
    for e in range(0, sz.wide, 8):
        part = slice(e, e + 8)
        acts = [half_of(act0_ref, t, e) for t in range(sz.rows)]
        back = backward_parts(sz, sh_ref, tap_ref, part, acts, acc_ref)
        for t in range(sz.rows):
            mat_ref[t, part] = back[t] * s0_ref[t, part]
    buf = buf + placed_sums(acc_ref, 9, 3 * chans)
    for t in range(sz.rows):
        cells = placed_cells(xc_ref[t].astype(F32)[:chans], 0)
        buf = buf + dot(doubled(mat_ref[t]), jnp.concatenate([cells, cells], axis=1), 1, 1)
    at = 3 * chans + 27
    small = [dot(squeezed, gate_pre, 0, 0, True)[: sz.squeeze]]
    small.append(dot(squeeze_grad, pooled, 0, 0, True)[: sz.squeeze])
    small.append(jnp.sum(gate_pre, axis=0, keepdims=True))
    shape = (16, LANES)
    unit = jnp.where(iota(shape, 0) + at == iota(shape, 1), 1.0, 0.0).astype(BF16)
    buf_ref[...] = buf + spread_by(padded_rows(small, 16), unit)
    at = at + 2 * sz.squeeze + 1
    spots = iota((8, 1), 0)
    held = jnp.sum(squeeze_grad, axis=0, keepdims=True)
    column = jnp.zeros((8, 1), F32)
    for k in range(sz.squeeze):
        column = jnp.where(spots == k, held[:, k : k + 1], column)
    buf_ref[0:8, at : at + 1] = column
    column = jnp.zeros((8, 1), F32)
    squares = [
        jnp.sum(result_sq.reshape(chans // 8, 8, LANES), axis=0),
        sq_ref[0:8],
        sq_ref[8:16],
        jnp.sum(branch_sq.reshape(chans // 8, 8, LANES), axis=0),
    ]
    for k, square in enumerate(squares):
        value = jnp.sum(lane_sum(square), axis=0, keepdims=True)
        column = jnp.where(spots == k, value, column)
    buf_ref[8:16, at : at + 1] = column
    used = at + 1
    piece = LANES - used
    for k in range(-(-used // piece)):
        take = min(piece, used - k * piece)
        buf_ref[k * half : (k + 1) * half, used : used + take] = buf_ref[
            LANES : LANES + half, k * piece : k * piece + take
        ]
    each = LANES // sz.devices
    last = jnp.sum(near, axis=0, keepdims=True)
    block = wide_rows(sum_b, sum_g, half, last)
    send_block(out_pay, jnp.concatenate([block, jnp.zeros((4, LANES), F32)], axis=0))
    for k in range(each):
        held = buf_ref[pl.ds(k, sz.devices, stride=each), :]
        out_pay[pl.ds(4 + k, sz.devices, stride=8), :] = held


def stage_four_kernel(
    sz, pay_ref, scaled_ref, dc_ref, ec_ref, s0_ref, row0_ref, row1_ref, par_ref, *refs
):
    tap_ref, unit_ref, info_ref, out_pay, gp0_ref, bg1_ref, gg1_ref, mid_ref, sh_ref = refs
    half = sz.wide - LANES
    masks = mask_rows(sz, info_ref[...])
    block = jnp.sum(pay_ref[...].reshape(sz.devices, 8, LANES), axis=0)
    bias_grad, gain_grad = wide_pair(block, half)
    bg1_ref[...] = bias_grad.reshape(sz.wide)
    gg1_ref[...] = gain_grad.reshape(sz.wide)
    mid_ref[0:1] = bias_grad
    mid_ref[1:2] = gain_grad
    inv1 = row1_ref[1:2]
    scale = inv1 * par_ref[2:3] / row0_ref[2:3]
    bg_c, gg_c = spread_rows([bias_grad * scale, gain_grad * inv1 * scale])
    fields = []
    for t in range(sz.rows):
        grad = scaled_ref[t] - masks[t] * (bg_c + dc_ref[t] * gg_c)
        fields.append(grad.astype(BF16).astype(F32))
    field_shifts(sz, fields, sh_ref, unit_ref, True)
    total_b = []
    total_g = []
    for e in range(0, sz.wide, 8):
        part = slice(e, e + 8)
        back = backward_parts(sz, sh_ref, tap_ref, part, None, None)
        sum_b = 0.0
        sum_g = 0.0
        for t in range(sz.rows):
            grad = back[t] * s0_ref[t, part]
            gp0_ref[t, part] = grad
            sum_b = sum_b + grad
            sum_g = sum_g + grad * ec_ref[t, part]
        total_b.append(sum_b)
        total_g.append(sum_g)
    sum_b = row_sums(jnp.concatenate(total_b, axis=0))
    sum_g = row_sums(jnp.concatenate(total_g, axis=0)) * row0_ref[1:2]
    top = wide_rows(sum_b, sum_g, half, jnp.zeros((1, LANES), F32))
    send_block(out_pay, jnp.concatenate([top, block[4:8]], axis=0))


def back_kernel(sz, gp0_ref, res_ref, row0_ref, par_ref, w_ref, *refs):
    out_refs, all_ref = refs[:-1], refs[-1]
    chans = sz.chans
    (scale,) = spread_rows([row0_ref[1:2] * par_ref[0:1]])
    weights = w_ref[...]
    for g in range(sz.rows // 2):
        pieces = []
        for par in range(2):
            t = 2 * g + par
            pieces += [res_ref[t], dot(weights, (gp0_ref[t] * scale).astype(BF16), 1, 0)]
        pieces.append(jnp.zeros((LANES - 4 * chans, LANES), F32))
        turned = jnp.concatenate(pieces, axis=0).T.astype(BF16)
        all_ref[:, :, g] = turned.reshape(sz.tiles, sz.own, sz.width, LANES)
    for step, out_ref in enumerate(out_refs):
        out_ref[...] = all_ref[partner(sz, step)]


def far_kernel(sz, pay_ref, row0_ref, w_ref, after_ref, far_ref, buf_ref, near_ref):
    del after_ref
    chans = sz.chans
    held = every(sz, pay_ref, 3, 8)
    near_ref[...] = held[0:32]
    buf_ref[...] = jnp.zeros(buf_ref.shape, F32)
    for k in range(5):
        rows = min(32, sz.wide - 32 * k)
        buf_ref[32 * k : 32 * k + rows, 0:chans] = near_ref[0:rows, chans * k : chans * (k + 1)]
    far_ref[0:chans] = dot(eye(chans, LANES), buf_ref[...], 1, 1, True)
    x_row = [near_ref[chans + k : chans + k + 1, 5 * chans : LANES] for k in range(3)]
    x_row = jnp.concatenate(x_row, axis=1)
    x_column = columns_of([x_row])[:, 0:1]
    right = near_ref[0:chans, 5 * chans : LANES]
    below = right.T[0:8, 0:16]
    below = jnp.concatenate([below, right[16:chans]], axis=1)
    second = jnp.concatenate([near_ref[16:32, 4 * chans : 5 * chans], below], axis=0)
    second = second - x_column * x_row / row0_ref[2:3, :chans]
    wide = dot(second, w_ref[...].astype(F32), 1, 0, True)
    far_ref[chans : 2 * chans] = wide * row0_ref[1:2]
    far_ref[2 * chans : 3 * chans, 0:1] = x_column
    far_ref[3 * chans : 3 * chans + 1, 0:1] = near_ref[
        chans + 3 : chans + 4, 5 * chans : 5 * chans + 1
    ]


def return_kernel(sz, *refs):
    got_refs = refs[: sz.tiles]
    c_ref, out_ref, pre_ref = refs[sz.tiles :]
    chans = sz.chans
    for step, ref in enumerate(got_refs):
        first = partner(sz, sz.tiles - step) * sz.own
        for t in range(sz.rows):
            at = (t % 2) * 2 * chans
            out_ref[pl.ds(first, sz.own), t] = ref[:, t // 2, :, at : at + chans]
            back = ref[:, t // 2, :, at + chans : at + 2 * chans].astype(F32)
            pre_ref[pl.ds(first, sz.own), t] = back + c_ref[pl.ds(first, sz.own), t].astype(F32)


def last_kernel(
    sz,
    pay_ref,
    pre_ref,
    x_ref,
    far_ref,
    row0_ref,
    row1_ref,
    mid_ref,
    par_ref,
    w_ref,
    len_ref,
    count_ref,
    xg_ref,
    ew_ref,
    gg0_ref,
    bg0_ref,
    dw_ref,
    rw_ref,
    rb_ref,
    sw_ref,
    sb_ref,
    pw_ref,
    rms_ref,
    buf_ref,
):
    chans = sz.chans
    half = sz.wide - LANES
    each = LANES // sz.devices
    block = [jnp.sum(every(sz, pay_ref, at, 8), axis=0, keepdims=True) for at in range(3)]
    bias_grad, gain_grad = wide_pair(jnp.concatenate(block, axis=0), half)
    bg0_ref[...] = bias_grad.reshape(sz.wide)
    gg0_ref[...] = gain_grad.reshape(sz.wide)
    mean0 = row0_ref[0:1]
    inv0 = row0_ref[1:2]
    total = row0_ref[2:3]
    scale0 = inv0 * par_ref[0:1]
    bias_row = bias_grad / total
    gain_row = gain_grad / total
    weights = w_ref[...].astype(F32)
    factor = scale0 * gain_row * inv0
    matrix = dot(weights * factor, weights, 1, 1, True)
    offset = jnp.broadcast_to(scale0 * bias_row - factor * mean0, (8, sz.wide))
    offset = dot(offset, weights, 1, 1, True)[0:1]
    high = matrix.astype(BF16)
    low = (matrix - high.astype(F32)).astype(BF16)
    first = lax.axis_index("tile") * sz.rows
    for t in range(sz.rows):
        cells = x_ref[:, t].reshape(sz.segs * sz.width, chans)
        back = dot(cells, high, 1, 0) + dot(cells, low, 1, 0) + offset
        for s in range(sz.segs):
            length = jnp.where(s < count_ref[0], len_ref[s], 0)
            live = jnp.where(first + t < length, 1.0, 0.0)
            held = back[s * sz.width : (s + 1) * sz.width] * live
            xg_ref[s, t] = (pre_ref[s, t] - held).astype(BF16)
    used = 3 * chans + 29 + 2 * sz.squeeze
    piece = LANES - used
    for k in range(each):
        buf_ref[pl.ds(k, sz.devices, stride=each), :] = every(sz, pay_ref, 4 + k, 8)
    buf_ref[LANES:] = jnp.zeros((half, LANES), F32)
    for k in range(-(-used // piece)):
        take = min(piece, used - k * piece)
        buf_ref[LANES : LANES + half, k * piece : k * piece + take] = buf_ref[
            k * half : (k + 1) * half, used : used + take
        ]
    rows = dot(eye(LANES, LANES), buf_ref[...], 1, 1, True)
    inv1 = row1_ref[1:2]
    scale1 = inv1 * par_ref[2:3]
    bias1 = mid_ref[0:1] / total
    gain1 = mid_ref[1:2] * inv1 / total
    inner = rows[0:chans] - far_ref[0:chans] * bias1 - rows[chans : 2 * chans] * gain1
    x_sum = far_ref[2 * chans : 3 * chans, 0:1]
    ew_ref[...] = scale0 * (
        scale1 * inner - x_sum * bias_row - far_ref[chans : 2 * chans] * gain_row
    )
    pw_ref[...] = rows[2 * chans : 3 * chans]
    spot = 3 * chans
    held = rows[spot : spot + 9] - rows[spot + 9 : spot + 18] * bias1
    held = scale1 * (held - rows[spot + 18 : spot + 27] * gain1)
    for i in range(3):
        dw_ref[i] = held[3 * i : 3 * i + 3]
    spot = spot + 27
    sw_ref[...] = rows[spot : spot + sz.squeeze]
    spot = spot + sz.squeeze
    rw_ref[...] = rows[spot : spot + sz.squeeze]
    spot = spot + sz.squeeze
    sb_ref[...] = rows[spot : spot + 1].reshape(sz.wide)
    misc = rows[spot + 1 : spot + 2]
    rb_ref[...] = misc[:, : sz.squeeze].reshape(sz.squeeze)
    act0_sq = far_ref[3 * chans : 3 * chans + 1, 0:1]
    squares = jnp.concatenate(
        [misc[:, 8:9], act0_sq, misc[:, 9:10], misc[:, 10:11], misc[:, 11:12]], axis=1
    )
    chan_row = jnp.where(
        (iota((1, 5), 1) == 0) | (iota((1, 5), 1) == 4), float(chans), float(sz.wide)
    )
    rms_ref[...] = jnp.sqrt(squares / (total[:, :5] * chan_row)).reshape(5)


def call(kernel, sz, args, kinds, outs, scratch=(), cost=1.0, room=16):
    spaces = {"v": VMEM, "s": SMEM, "h": HBM, "a": pl.BlockSpec(memory_space=pl.ANY)}
    kinds = kinds + "v" * (len(args) - len(kinds))
    return pl.pallas_call(
        functools.partial(kernel, sz),
        out_shape=tuple(jax.ShapeDtypeStruct(shape, kind) for shape, kind in outs),
        in_specs=[spaces[kind] for kind in kinds],
        out_specs=tuple(VMEM for _ in outs),
        scratch_shapes=[pltpu.VMEM(*held) if isinstance(held, tuple) else held for held in scratch],
        compiler_params=pltpu.CompilerParams(vmem_limit_bytes=room * 1024 * 1024),
        cost_estimate=pl.CostEstimate(
            flops=int(cost * 1e9), bytes_accessed=int(cost * 3e6), transcendentals=0
        ),
        name=kernel.__name__,
    )(*args)


def everywhere(values):
    return lax.all_to_all(values, BOTH, 0, 0, tiled=True)


def passed(sz, parts):
    result = [parts[0]]
    for step in range(1, sz.tiles):
        pairs = [(i, (i + step) % sz.tiles) for i in range(sz.tiles)]
        result.append(lax.ppermute(parts[step], "tile", pairs))
    return result


def shards(
    x_input,
    expand_w,
    gain0,
    bias0,
    dw_kernel,
    gain1,
    bias1,
    reduce_w,
    reduce_b,
    restore_w,
    restore_b,
    project_w,
    gain2,
    bias2,
    cotangent,
    seg_count,
    seg_len,
):
    segs, rows, width, chans = x_input.shape
    wide, squeeze = reduce_w.shape
    tiles = lax.axis_size("tile")
    devices = lax.axis_size("seg") * tiles
    own = segs // tiles
    sz = Sizes(devices, tiles, segs, own, rows, width, chans, wide, squeeze)
    big = ((rows, wide, LANES), F32)
    small = ((rows, chans, LANES), F32)
    block = ((own, rows // 2, width, LANES), BF16)
    packed = ((rows, wide, LANES), BF16)
    both = ((rows, 2 * chans, LANES), BF16)
    column = ((wide, LANES), F32)
    taps = ((9, wide, LANES), F32)
    shifts = ((3, rows + 2, wide, LANES), F32)

    def pay_of(count):
        return ((devices * count, LANES), F32)

    (pay,) = call(
        entry_kernel,
        sz,
        [x_input, expand_w, seg_len, seg_count],
        "hhhh",
        [pay_of(4)],
        [
            (x_input.shape, BF16),
            (expand_w.shape, BF16),
            pltpu.SMEM(seg_len.shape, jnp.int32),
            pltpu.SMEM(seg_count.shape, jnp.int32),
            pltpu.SemaphoreType.DMA((4,)),
        ],
        room=60,
    )
    parts = call(send_kernel, sz, [x_input, cotangent, pay], "vva", [block] * tiles)
    par, tap, unit, info, pw_near, w_near = call(
        setup_kernel,
        sz,
        [gain0, bias0, gain1, bias1, restore_b, gain2, bias2, reduce_b, dw_kernel, reduce_w.T]
        + [restore_w, project_w.T, expand_w, seg_len, seg_count],
        "v" * 13 + "ss",
        [
            ((24, wide), F32),
            taps,
            ((2 * LANES, 4 * LANES), BF16),
            ((16, LANES), F32),
            ((chans, wide), BF16),
            ((chans, wide), BF16),
        ],
    )
    pay = everywhere(pay)
    parts = passed(sz, parts)
    exp, x_c = call(
        gather_kernel, sz, parts + [w_near], "", [big, both], [((tiles,) + block[0], BF16)]
    )
    pay, act0, deep, ec, s0, row0, near, part = call(
        stage_one_kernel,
        sz,
        [pay, exp, x_c, par, tap, unit, info],
        "",
        [pay_of(4), packed, big, big, big, ((3, wide), F32)]
        + [((max(32, devices), LANES), F32), column],
        [big, taps, shifts, column],
    )
    pay = everywhere(pay)
    pay, act1, dc, s1, proj, gate, seg_rows, row1, part, squares = call(
        stage_two_kernel,
        sz,
        [pay, deep, x_c, par, tap, unit, info, pw_near, near, act0, s0, part],
        "",
        [pay_of(2), big, big, big, small, column, ((3, 8, wide), F32), ((2, wide), F32)]
        + [column, ((16, LANES), F32)],
        [big, taps, shifts],
    )
    pay = everywhere(pay)
    pay, res, scaled, bg2, gg2 = call(
        stage_three_kernel,
        sz,
        [pay, proj, x_c, act0, act1, s0, dc, s1, gate, seg_rows, par, tap, unit, info]
        + [pw_near, part, squares, row1],
        "",
        [pay_of(8), small, big, ((chans,), F32), ((chans,), F32)],
        [big, big, taps, shifts, column],
    )
    far_pay = everywhere(pay)
    pay, gp0, bg1, gg1, mid = call(
        stage_four_kernel,
        sz,
        [far_pay, scaled, dc, ec, s0, row0, row1, par, tap, unit, info],
        "",
        [pay_of(8), big, ((wide,), F32), ((wide,), F32), ((2, wide), F32)],
        [shifts],
    )
    sent = call(
        back_kernel,
        sz,
        [gp0, res, row0, par, w_near],
        "",
        [block] * tiles,
        [((tiles,) + block[0], BF16)],
    )
    pay = everywhere(pay)
    (far,) = call(
        far_kernel,
        sz,
        [far_pay, row0, w_near, gp0],
        "vvva",
        [((3 * chans + 8, wide), F32)],
        [column, ((32, LANES), F32)],
    )
    sent = passed(sz, sent)
    block_out, pre = call(
        return_kernel,
        sz,
        sent + [cotangent],
        "",
        [(x_input.shape, BF16), (x_input.shape, F32)],
    )
    x_grad, ew, gg0, bg0, dw, rw, rb, sw, sb, pw, rms = call(
        last_kernel,
        sz,
        [pay, pre, x_input, far, row0, row1, mid, par, w_near, seg_len, seg_count],
        "v" * 9 + "ss",
        [
            (x_input.shape, BF16),
            ((chans, wide), F32),
            ((wide,), F32),
            ((wide,), F32),
            (dw_kernel.shape, F32),
            ((squeeze, wide), F32),
            ((squeeze,), F32),
            ((squeeze, wide), F32),
            ((wide,), F32),
            ((chans, wide), F32),
            ((5,), F32),
        ],
        [column],
    )
    return (
        block_out,
        x_grad,
        ew,
        gg0,
        bg0,
        dw,
        gg1,
        bg1,
        rw.T,
        rb,
        sw,
        sb,
        pw.T,
        gg2,
        bg2,
        rms,
    )


def solution(mesh):
    split = P("seg", "tile", None, None)
    return jax.shard_map(
        shards,
        mesh=mesh,
        in_specs=(split,) + (P(),) * 13 + (split, P("seg"), P("seg")),
        out_specs=(split, split) + (P(),) * 14,
        check_vma=False,
    )
```

time: 484 us -> 72.8 us (0.15)
  blocking collectives: 421 us -> 30.3 us
  other arithmetic: 30 us -> 0 us
  Pallas kernels: 0 us -> 19.4 us
  matrix products: 11.9 us -> 0 us
  starting transfers between devices: 5.17 us -> 16.4 us
  local copies, waits for them, and re-layouts: 5.88 us -> 0.66 us
    psum x12 -> x0, blocking collectives: 421 us -> none  [the longest x3 122 us: norm_back(): lax.psum((jnp.sum(grad_out, axis=(0, 1, 2)), jnp.sum(grad_out * normed, a...]
    all_to_all x0 -> x3, blocking collectives: none -> 30.3 us  [everywhere(): return lax.all_to_all(values, BOTH, 0, 0, tiled=True)]
    pallas_call x0 -> x12, Pallas kernels: none -> 19.4 us  [call(): pl.pallas_call(functools.partial(kernel, sz), out_shape=tuple((jax.ShapeD...]
    reduce_sum x11 -> x0, other arithmetic: 17.4 us -> none  [the longest x2 4.1 us: norm_back(): jnp.sum(grad_out, axis=(0, 1, 2))]
    dot_general x12 -> x0, matrix products: 11.9 us -> none  [the longest x2 2.74 us: row_dot(): jnp.einsum('stmc,cd->stmd', field, weight, preferred_element_type=jnp.flo...]
    all_to_all x0 -> x2, starting transfers between devices: none -> 9.88 us  [everywhere(): return lax.all_to_all(values, BOTH, 0, 0, tiled=True)]
  transfers between devices with their start and end apart: 4 -> 8, of which waited for: 2 -> 4; matrix products, arithmetic and copies ran while one was open for 1% -> 0% of each run, Pallas kernels for 0% -> 6%
where the time goes in v1:
time: 72.8 us; the launch traced here: 72.5 us
  blocking collectives  30.3 us (42%)
  Pallas kernels  19.4 us (27%)
  starting transfers between devices  16.4 us (23%)
  waiting for transfers between devices  4.12 us (6%)
  between operations  1.61 us (2%)
    all_to_all x3, blocking collectives, everywhere(): return lax.all_to_all(values, BOTH, 0, 0, tiled=True)  30.3 us
    pallas_call x12, Pallas kernels, call(): pl.pallas_call(functools.partial(kernel, sz), out_shape=tuple((jax.ShapeD...  19.4 us
    all_to_all x2, starting transfers between devices, everywhere(): return lax.all_to_all(values, BOTH, 0, 0, tiled=True)  9.88 us
    ppermute x6, starting transfers between devices, passed(): result.append(lax.ppermute(parts[step], 'tile', pairs))  6.47 us
    all_to_all x2, waiting for transfers between devices, everywhere(): return lax.all_to_all(values, BOTH, 0, 0, tiled=True)  3.13 us
  transfers between devices with their start and end apart: 8, of which 4 were waited for; matrix products, arithmetic and copies ran while one was open for 0% of the time, Pallas kernels for 6%

profile of v1, /device:TPU:0, one launch (start us, length us, event | category | flops | bytes accessed | tf_op | source)
XLA Modules:
  0.0 72.5 jit_solution(12336228457175122994)
XLA Ops:
  1.3 0.0 copy-start.1
  1.3 2.5 %entry_kernel.1.after_ref = f32[128,128]{1,0:T(8,128)} custom-call(bf16[8,6,16,24]{3,2,1,0:T(8,128)(2,1)} %x_ref.3, bf16[24,144]{1,0:T(8,128)(2,1)} %refs_12_.1, s32[8]{0:T(128)} %len_ref.1, s32[1]{0:T(128)S(6)} %copy.33.count_hbm.refs_14_.count_ref), custom_call_target="tpu_custom_call" | custom-call | flops 1000000000 | bytes 3000000 | tf_op jit(solution)/shard_map/entry_kernel/pallas_call | solution.py:914
  3.8 0.0 copy-start
  3.8 7.3 %all-to-all-start = ((f32[32,4,128]{2,1,0:T(4,128)}), f32[32,4,128]{2,1,0:T(4,128)S(1)}, u32[]{:S(2)}, u32[]{:S(2)}) async-start(f32[32,4,128]{2,1,0:T(4,128)} %bitcast.19), calls=%async_computation | async-start | bytes 131072 | tf_op jit(solution)/shard_map/all_to_all | solution.py:929
  11.2 0.0 copy-start.3
  11.2 0.0 copy-start.4
  11.2 0.0 copy-start.6
  11.2 0.0 copy-start.7
  11.2 0.0 copy-start.9
  11.2 0.0 copy-start.10
  11.2 0.0 copy-start.11
  11.3 0.0 copy-start.12
  11.3 0.0 copy-start.13
  11.3 0.0 copy-start.14
  11.3 0.0 copy-start.15
  11.3 0.0 copy-start.16
  11.3 0.2 send_kernel.1
  11.6 0.3 collective-permute-start
  11.9 1.7 %collective-permute-start.1 = (bf16[2,3,16,128]{3,2,1,0:T(8,128)(2,1)S(1)}, bf16[2,3,16,128]{3,2,1,0:T(8,128)(2,1)S(1)}, u32[]{:S(2)}, u32[]{:S(2)}) collective-permute-start(bf16[2,3,16,128]{3,2,1,0:T(8,128)(2,1)S(1)} %get-tuple-element.75), channel_id=1, source_target_pairs={{0,2},{1,3},{2,0},{3,1},{4,6},{5,7},{6,4},{7,5},{8,10},{9,11},{10,... | collective-permute-start | bytes 73736 | tf_op jit(solution)/shard_map/ppermute | solution.py:936
  13.5 1.3 %collective-permute-start.2 = (bf16[2,3,16,128]{3,2,1,0:T(8,128)(2,1)S(1)}, bf16[2,3,16,128]{3,2,1,0:T(8,128)(2,1)S(1)}, u32[]{:S(2)}, u32[]{:S(2)}) collective-permute-start(bf16[2,3,16,128]{3,2,1,0:T(8,128)(2,1)S(1)} %get-tuple-element.76), channel_id=1, source_target_pairs={{0,3},{1,0},{2,1},{3,2},{4,7},{5,4},{6,5},{7,6},{8,11},{9,8},{10,9... | collective-permute-start | bytes 73736 | tf_op jit(solution)/shard_map/ppermute | solution.py:936
  14.9 0.0 copy-done.3
  14.9 0.0 copy-done.6
  15.0 0.6 copy-done.8
  15.5 0.8 %setup_kernel.1 = (f32[24,144]{1,0:T(8,128)S(1)}, f32[9,144,128]{2,1,0:T(8,128)S(1)}, bf16[256,512]{1,0:T(8,128)(2,1)S(1)}, f32[16,128]{1,0:T(8,128)S(1)}, bf16[...) custom-call(f32[144]{0:T(256)S(1)} %copy-done.8, f32[144]{0:T(256)S(1)} %copy-done.9, f32[144]{0:T(256)S(1)} %copy-done.10, ...), custom_call_target="tpu_custom_call" | custom-call | flops 1000000000 | bytes 3000000 | tf_op jit(solution)/shard_map/setup_kernel/pallas_call | solution.py:914
  16.4 0.0 collective-permute-done.refs_1_
  16.4 0.0 collective-permute-done.1.refs_2_
  16.4 0.0 collective-permute-done.2.refs_3_
  16.4 0.6 gather_kernel.1
  17.0 1.6 %all-to-all-done = f32[32,4,128]{2,1,0:T(4,128)S(1)} async-done(((f32[32,4,128]{2,1,0:T(4,128)}), f32[32,4,128]{2,1,0:T(4,128)S(1)}, u32[]{:S(2)}, u32[]{:S(2)}) %all-to-all-start) | async-done | bytes 65568 | tf_op jit(solution)/shard_map/all_to_all | solution.py:929
  18.6 2.0 %stage_one_kernel.1 = (f32[128,128]{1,0:T(8,128)S(1)}, bf16[6,144,128]{2,1,0:T(8,128)(2,1)S(1)}, f32[6,144,128]{2,1,0:T(8,128)S(1)}, f32[6,144,128]{2,1,0:T(8,12...) custom-call(f32[128,128]{1,0:T(8,128)S(1)} %bitcast.18, ...), custom_call_target="tpu_custom_call" | custom-call | flops 1000000000 | bytes 3000000 | tf_op jit(solution)/shard_map/stage_one_kernel/pallas_call | solution.py:914
  20.5 11.4 %all_to_all.55 = f32[32,4,128]{2,1,0:T(4,128)S(1)} all-to-all(f32[32,4,128]{2,1,0:T(4,128)S(1)} %bitcast.21), channel_id=1, replica_groups=mesh['seg'=8,'tile'=4] {'seg','tile'}, dimensions={0} | all-to-all | bytes 131072 | tf_op jit(solution)/shard_map/all_to_all | solution.py:929
  32.0 3.1 %stage_two_kernel.1 = (f32[64,128]{1,0:T(8,128)S(1)}, f32[6,144,128]{2,1,0:T(8,128)S(1)}, f32[6,144,128]{2,1,0:T(8,128)S(1)}, f32[6,144,128]{2,1,0:T(8,128)S(1)}...) custom-call(f32[128,128]{1,0:T(8,128)S(1)} %bitcast.20, ...), custom_call_target="tpu_custom_call" | custom-call | flops 1000000000 | bytes 3000000 | tf_op jit(solution)/shard_map/stage_two_kernel/pallas_call | solution.py:914
  35.0 8.9 %all_to_all.56 = f32[32,2,128]{2,1,0:T(2,128)S(1)} all-to-all(f32[32,2,128]{2,1,0:T(2,128)S(1)} %bitcast.23), channel_id=1, replica_groups=mesh['seg'=8,'tile'=4] {'seg','tile'}, dimensions={0} | all-to-all | bytes 65536 | tf_op jit(solution)/shard_map/all_to_all | solution.py:929
  44.0 3.9 %stage_three_kernel.1 = (f32[256,128]{1,0:T(8,128)S(1)}, f32[6,24,128]{2,1,0:T(8,128)S(1)}, f32[6,144,128]{2,1,0:T(8,128)S(1)}, f32[24]{0:T(128)}, f32[24]{0:T(128)}) custom-call(f32[64,128]{1,0:T(8,128)S(1)} %bitcast.22, f32[6,24,128]{2,1,0:T(8,128)S(1)} %get-tuple-element.92.proj_ref, bf16[6,48,128]{2,1,0:T(8,128)(2,1)S(1)} %get-tuple-element.79.xc_ref, ...), custom_call_target="tpu_custom_call" | custom-call | flops 1000000000 | bytes 3000000 | tf_op jit(solution)/shard_map/stage_three_kernel/pallas_call | solution.py:914
  47.9 9.9 %all_to_all.57 = f32[32,8,128]{2,1,0:T(8,128)S(1)} all-to-all(f32[32,8,128]{2,1,0:T(8,128)S(1)} %bitcast.17), channel_id=1, replica_groups=mesh['seg'=8,'tile'=4] {'seg','tile'}, dimensions={0} | all-to-all | bytes 262144 | tf_op jit(solution)/shard_map/all_to_all | solution.py:929
  57.8 1.9 %stage_four_kernel.1 = (f32[256,128]{1,0:T(8,128)}, f32[6,144,128]{2,1,0:T(8,128)S(1)}, f32[144]{0:T(256)}, f32[144]{0:T(256)}, f32[2,144]{1,0:T(2,128)S(1)}) custom-call(f32[256,128]{1,0:T(8,128)S(1)} %bitcast.15, f32[6,144,128]{2,1,0:T(8,128)S(1)} %get-tuple-element.102.scaled_ref, f32[6,144,128]{2,1,0:T(8,128)S(1)} %get-tuple-element.94.dc_ref, ...), custom_call_target="tpu_custom_call" | custom-call | flops 1000000000 | bytes 3000000 | tf_op jit(solution)/shard_map/stage_four_kernel/pallas_call | solution.py:914
  59.7 2.6 %all-to-all-start.4 = ((f32[32,8,128]{2,1,0:T(8,128)}), f32[32,8,128]{2,1,0:T(8,128)S(1)}, u32[]{:S(2)}, u32[]{:S(2)}) async-start(f32[32,8,128]{2,1,0:T(8,128)} %bitcast.10), calls=%async_computation.4 | async-start | bytes 262144 | tf_op jit(solution)/shard_map/all_to_all | solution.py:929
  62.3 0.5 back_kernel.1
  62.8 0.2 collective-permute-start.3
  63.0 1.7 %collective-permute-start.4 = (bf16[2,3,16,128]{3,2,1,0:T(8,128)(2,1)S(1)}, bf16[2,3,16,128]{3,2,1,0:T(8,128)(2,1)S(1)}, u32[]{:S(2)}, u32[]{:S(2)}) collective-permute-start(bf16[2,3,16,128]{3,2,1,0:T(8,128)(2,1)S(1)} %get-tuple-element.109), channel_id=1, source_target_pairs={{0,2},{1,3},{2,0},{3,1},{4,6},{5,7},{6,4},{7,5},{8,10},{9,11},{10,... | collective-permute-start | bytes 73736 | tf_op jit(solution)/shard_map/ppermute | solution.py:936
  64.7 1.3 %collective-permute-start.5 = (bf16[2,3,16,128]{3,2,1,0:T(8,128)(2,1)S(1)}, bf16[2,3,16,128]{3,2,1,0:T(8,128)(2,1)S(1)}, u32[]{:S(2)}, u32[]{:S(2)}) collective-permute-start(bf16[2,3,16,128]{3,2,1,0:T(8,128)(2,1)S(1)} %get-tuple-element.110), channel_id=1, source_target_pairs={{0,3},{1,0},{2,1},{3,2},{4,7},{5,4},{6,5},{7,6},{8,11},{9,8},{10,9... | collective-permute-start | bytes 73736 | tf_op jit(solution)/shard_map/ppermute | solution.py:936
  66.0 0.5 far_kernel.1.far_ref
  66.5 0.0 collective-permute-done.3.refs_1_
  66.5 0.4 collective-permute-done.4.refs_2_
  67.0 0.5 collective-permute-done.5.refs_3_
  67.5 1.5 %return_kernel.1 = (bf16[8,6,16,24]{3,2,1,0:T(8,128)(2,1)}, f32[8,6,16,24]{3,2,1,0:T(8,128)S(1)}) custom-call(bf16[2,3,16,128]{3,2,1,0:T(8,128)(2,1)S(1)} %get-tuple-element.107.refs_0_, bf16[2,3,16,128]{3,2,1,0:T(8,128)(2,1)S(1)} %collective-permute-done.3.refs_1_, bf16[2,3,16,128]{3,2,1,0:T(8,128)(2,1)S(1)} %collective-permute-done.4.refs_2_, ...), custom_call_target="tpu_custom_call" | custom-call | flops 1000000000 | bytes 3000000 | tf_op jit(solution)/shard_map/return_kernel/pallas_call | solution.py:914
  69.0 1.6 %all-to-all-done.4 = f32[32,8,128]{2,1,0:T(8,128)S(1)} async-done(((f32[32,8,128]{2,1,0:T(8,128)}), f32[32,8,128]{2,1,0:T(8,128)S(1)}, u32[]{:S(2)}, u32[]{:S(2)}) %all-to-all-start.4) | async-done | bytes 131104 | tf_op jit(solution)/shard_map/all_to_all | solution.py:929
  70.5 1.9 %last_kernel.1 = (bf16[8,6,16,24]{3,2,1,0:T(8,128)(2,1)}, f32[24,144]{1,0:T(8,128)}, f32[144]{0:T(256)}, f32[144]{0:T(256)}, f32[3,3,144]{2,1,0:T(4,128)}, /*ind...) custom-call(f32[256,128]{1,0:T(8,128)S(1)} %bitcast.14, ...), custom_call_target="tpu_custom_call" | custom-call | flops 1000000000 | bytes 3000000 | tf_op jit(solution)/shard_map/last_kernel/pallas_call | solution.py:914
  (17 shorter events, 0.0 us)
Async XLA Ops:
  1.3 9.9 %copy-start.1 = (bf16[8,6,16,24]{3,2,1,0:T(8,128)(2,1)S(1)}, bf16[8,6,16,24]{3,2,1,0:T(8,128)(2,1)}, u32[]{:S(2)}) copy-start(bf16[8,6,16,24]{3,2,1,0:T(8,128)(2,1)} %refs_4_.3) | copy-start | bytes 110596
  1.3 9.9 %copy-start.2 = (bf16[8,6,16,24]{3,2,1,0:T(8,128)(2,1)S(1)}, bf16[8,6,16,24]{3,2,1,0:T(8,128)(2,1)}, u32[]{:S(2)}) copy-start(bf16[8,6,16,24]{3,2,1,0:T(8,128)(2,1)} %x_ref.3) | copy-start | bytes 110596
  3.8 7.3 %copy-start = (f32[128,128]{1,0:T(8,128)S(1)}, f32[128,128]{1,0:T(8,128)}, u32[]{:S(2)}) copy-start(f32[128,128]{1,0:T(8,128)} %entry_kernel.1.after_ref) | copy-start | bytes 196612
  3.8 14.7 %all-to-all-start = ((f32[32,4,128]{2,1,0:T(4,128)}), f32[32,4,128]{2,1,0:T(4,128)S(1)}, u32[]{:S(2)}, u32[]{:S(2)}) async-start(f32[32,4,128]{2,1,0:T(4,128)} %bitcast.19), calls=%async_computation | async-start | bytes 131072 | tf_op jit(solution)/shard_map/all_to_all | solution.py:929
  11.2 3.7 %copy-start.3 = (bf16[24,144]{1,0:T(8,128)(2,1)S(1)}, bf16[24,144]{1,0:T(8,128)(2,1)}, u32[]{:S(2)}) copy-start(bf16[24,144]{1,0:T(8,128)(2,1)} %refs_12_.1) | copy-start | bytes 20740
  11.2 3.7 %copy-start.4 = (bf16[144,24]{0,1:T(8,128)(2,1)S(1)}, bf16[144,24]{0,1:T(8,128)(2,1)}, u32[]{:S(2)}) copy-start(bf16[144,24]{0,1:T(8,128)(2,1)} %param.28) | copy-start | bytes 20740
  11.2 3.7 %copy-start.6 = (f32[6,144]{1,0:T(8,128)S(1)}, f32[6,144]{1,0:T(8,128)}, u32[]{:S(2)}) copy-start(f32[6,144]{1,0:T(8,128)} %refs_10_.1) | copy-start | bytes 10372
  11.2 3.7 %copy-start.7 = (bf16[3,3,144]{2,1,0:T(4,128)(2,1)S(1)}, bf16[3,3,144]{2,1,0:T(4,128)(2,1)}, u32[]{:S(2)}) copy-start(bf16[3,3,144]{2,1,0:T(4,128)(2,1)} %refs_8_.1) | copy-start | bytes 7780
  11.2 3.7 %copy-start.9 = (f32[144]{0:T(256)S(1)}, f32[144]{0:T(256)}, u32[]{:S(2)}) copy-start(f32[144]{0:T(256)} %refs_1_.1) | copy-start | bytes 1732
  11.2 3.7 %copy-start.10 = (f32[144]{0:T(256)S(1)}, f32[144]{0:T(256)}, u32[]{:S(2)}) copy-start(f32[144]{0:T(256)} %refs_2_.1) | copy-start | bytes 1732
  11.2 3.7 %copy-start.11 = (f32[144]{0:T(256)S(1)}, f32[144]{0:T(256)}, u32[]{:S(2)}) copy-start(f32[144]{0:T(256)} %refs_3_.1) | copy-start | bytes 1732
  11.3 3.7 %copy-start.12 = (f32[144]{0:T(256)S(1)}, f32[144]{0:T(256)}, u32[]{:S(2)}) copy-start(f32[144]{0:T(256)} %refs_4_.2) | copy-start | bytes 1732
  11.3 3.7 %copy-start.13 = (f32[24]{0:T(128)S(1)}, f32[24]{0:T(128)}, u32[]{:S(2)}) copy-start(f32[24]{0:T(128)} %refs_5_.1) | copy-start | bytes 292
  11.3 3.7 %copy-start.14 = (f32[24]{0:T(128)S(1)}, f32[24]{0:T(128)}, u32[]{:S(2)}) copy-start(f32[24]{0:T(128)} %refs_6_.1) | copy-start | bytes 292
  11.3 3.6 %copy-start.15 = (f32[6]{0:T(128)S(1)}, f32[6]{0:T(128)}, u32[]{:S(2)}) copy-start(f32[6]{0:T(128)} %refs_7_.1) | copy-start | bytes 76
  11.3 3.6 %copy-start.16 = (s32[8]{0:T(128)S(1)}, s32[8]{0:T(128)}, u32[]{:S(2)}) copy-start(s32[8]{0:T(128)} %len_ref.1) | copy-start | bytes 100
  11.5 3.4 %copy-start.5 = (f32[144,6]{0,1:T(8,128)S(1)}, f32[144,6]{0,1:T(8,128)}, u32[]{:S(2)}) copy-start(f32[144,6]{0,1:T(8,128)} %param.24) | copy-start | bytes 10372
  11.6 4.8 %collective-permute-start = (bf16[2,3,16,128]{3,2,1,0:T(8,128)(2,1)S(1)}, bf16[2,3,16,128]{3,2,1,0:T(8,128)(2,1)S(1)}, u32[]{:S(2)}, u32[]{:S(2)}) collective-permute-start(bf16[2,3,16,128]{3,2,1,0:T(8,128)(2,1)S(1)} %get-tuple-element.74), channel_id=1, source_target_pairs={{0,1},{1,2},{2,3},{3,0},{4,5},{5,6},{6,7},{7,4},{8,9},{9,10},{10,1... | collective-permute-start | bytes 73736 | tf_op jit(solution)/shard_map/ppermute | solution.py:936
  11.9 4.5 %collective-permute-start.1 = (bf16[2,3,16,128]{3,2,1,0:T(8,128)(2,1)S(1)}, bf16[2,3,16,128]{3,2,1,0:T(8,128)(2,1)S(1)}, u32[]{:S(2)}, u32[]{:S(2)}) collective-permute-start(bf16[2,3,16,128]{3,2,1,0:T(8,128)(2,1)S(1)} %get-tuple-element.75), channel_id=1, source_target_pairs={{0,2},{1,3},{2,0},{3,1},{4,6},{5,7},{6,4},{7,5},{8,10},{9,11},{10,... | collective-permute-start | bytes 73736 | tf_op jit(solution)/shard_map/ppermute | solution.py:936
  13.5 2.9 %collective-permute-start.2 = (bf16[2,3,16,128]{3,2,1,0:T(8,128)(2,1)S(1)}, bf16[2,3,16,128]{3,2,1,0:T(8,128)(2,1)S(1)}, u32[]{:S(2)}, u32[]{:S(2)}) collective-permute-start(bf16[2,3,16,128]{3,2,1,0:T(8,128)(2,1)S(1)} %get-tuple-element.76), channel_id=1, source_target_pairs={{0,3},{1,0},{2,1},{3,2},{4,7},{5,4},{6,5},{7,6},{8,11},{9,8},{10,9... | collective-permute-start | bytes 73736 | tf_op jit(solution)/shard_map/ppermute | solution.py:936
  14.9 0.7 copy-start.8
  59.7 10.8 %all-to-all-start.4 = ((f32[32,8,128]{2,1,0:T(8,128)}), f32[32,8,128]{2,1,0:T(8,128)S(1)}, u32[]{:S(2)}, u32[]{:S(2)}) async-start(f32[32,8,128]{2,1,0:T(8,128)} %bitcast.10), calls=%async_computation.4 | async-start | bytes 262144 | tf_op jit(solution)/shard_map/all_to_all | solution.py:929
  62.8 3.7 %collective-permute-start.3 = (bf16[2,3,16,128]{3,2,1,0:T(8,128)(2,1)S(1)}, bf16[2,3,16,128]{3,2,1,0:T(8,128)(2,1)S(1)}, u32[]{:S(2)}, u32[]{:S(2)}) collective-permute-start(bf16[2,3,16,128]{3,2,1,0:T(8,128)(2,1)S(1)} %get-tuple-element.108), channel_id=1, source_target_pairs={{0,1},{1,2},{2,3},{3,0},{4,5},{5,6},{6,7},{7,4},{8,9},{9,10},{10,1... | collective-permute-start | bytes 73736 | tf_op jit(solution)/shard_map/ppermute | solution.py:936
  63.0 4.0 %collective-permute-start.4 = (bf16[2,3,16,128]{3,2,1,0:T(8,128)(2,1)S(1)}, bf16[2,3,16,128]{3,2,1,0:T(8,128)(2,1)S(1)}, u32[]{:S(2)}, u32[]{:S(2)}) collective-permute-start(bf16[2,3,16,128]{3,2,1,0:T(8,128)(2,1)S(1)} %get-tuple-element.109), channel_id=1, source_target_pairs={{0,2},{1,3},{2,0},{3,1},{4,6},{5,7},{6,4},{7,5},{8,10},{9,11},{10,... | collective-permute-start | bytes 73736 | tf_op jit(solution)/shard_map/ppermute | solution.py:936
  64.7 2.8 %collective-permute-start.5 = (bf16[2,3,16,128]{3,2,1,0:T(8,128)(2,1)S(1)}, bf16[2,3,16,128]{3,2,1,0:T(8,128)(2,1)S(1)}, u32[]{:S(2)}, u32[]{:S(2)}) collective-permute-start(bf16[2,3,16,128]{3,2,1,0:T(8,128)(2,1)S(1)} %get-tuple-element.110), channel_id=1, source_target_pairs={{0,3},{1,0},{2,1},{3,2},{4,7},{5,4},{6,5},{7,6},{8,11},{9,8},{10,9... | collective-permute-start | bytes 73736 | tf_op jit(solution)/shard_map/ppermute | solution.py:936

commit v2 on v1

--- a/solution.py
+++ b/solution.py
@@ -111,6 +111,13 @@
     if spare:
         held = jnp.concatenate([held, jnp.zeros((8, spare), F32)], axis=1)
     return held.T[:width]
+
+
+def turned(cells):
+    rows, width = cells.shape
+    spare = (-width) % LANES
+    held = jnp.concatenate([cells.astype(F32), jnp.zeros((rows, spare), F32)], axis=1)
+    return held.T[:width].astype(cells.dtype)
 
 
 def placed_cells(cells, first):
@@ -255,21 +262,22 @@
         ref[at : at + 8] = block
 
 
-def partner(sz, step):
-    return lax.rem(lax.axis_index("tile") + step, sz.tiles)
+def partner(step):
+    return lax.bitwise_xor(lax.axis_index("tile"), step)
 
 
 def entry_kernel(sz, x_hbm, w_hbm, len_hbm, count_hbm, pay_ref, *scratch):
     x_ref, w_ref, len_ref, count_ref, sems = scratch
     copies = [
-        pltpu.make_async_copy(x_hbm, x_ref, sems.at[0]),
-        pltpu.make_async_copy(w_hbm, w_ref, sems.at[1]),
-        pltpu.make_async_copy(len_hbm, len_ref, sems.at[2]),
-        pltpu.make_async_copy(count_hbm, count_ref, sems.at[3]),
+        pltpu.make_async_copy(len_hbm, len_ref, sems.at[0]),
+        pltpu.make_async_copy(count_hbm, count_ref, sems.at[1]),
+        pltpu.make_async_copy(w_hbm, w_ref, sems.at[2]),
     ]
+    for s in range(sz.segs):
+        copies.append(pltpu.make_async_copy(x_hbm.at[s], x_ref.at[s], sems.at[3 + s]))
     for copy in copies:
         copy.start()
-    for copy in reversed(copies):
+    for copy in copies[:3]:
         copy.wait()
     tile_pos = lax.axis_index("tile")
     lane_seg = lax.div(iota((1, LANES), 1), sz.width)
@@ -281,16 +289,23 @@
         count = count + jnp.clip(held - tile_pos * sz.rows, 0, sz.rows)
     count = (count * sz.width).astype(F32)
     masks = [(tile_pos * sz.rows + t < length).astype(F32) for t in range(sz.rows)]
+    weights = w_ref[...]
+    for copy in copies[3:]:
+        copy.wait()
     unit = eye(sz.chans, sz.chans, BF16)
     cells = [dot(unit, x_ref[:, t].reshape(LANES, sz.chans), 1, 1) for t in range(sz.rows)]
-    sums = lane_sum(sum(cells[t] * masks[t] for t in range(sz.rows)))
-    mean_val = spread(sums / jnp.maximum(count, 1.0))
+    total = 0.0
+    for t in range(sz.rows):
+        total = total + cells[t] * masks[t]
+    x_row = padded_rows([row_sums(total)], 16)
+    wide_sum = dot(jnp.concatenate(thirds(x_row), axis=0), weights, 1, 0)
+    wide_sum = wide_sum[0:1] + wide_sum[16:17] + wide_sum[32:33]
+    mean_val = lane_sum(total) / jnp.maximum(count, 1.0)
     centred = [(cells[t] - mean_val) * masks[t] for t in range(sz.rows)]
     centred = jnp.concatenate(centred, axis=1)
     spare = dot(centred, centred, 1, 1, True)
-    weights = w_ref[...].astype(F32)
-    wide_sum = dot(jnp.broadcast_to(sums, (sz.chans, 8)), weights, 0, 0, True)[0:1]
-    square = jnp.sum(dot(spare, weights, 1, 0, True) * weights, axis=0, keepdims=True)
+    wide = sum(dot(held, weights, 1, 0) for held in thirds(spare))
+    square = jnp.sum(wide * weights.astype(F32), axis=0, keepdims=True)
     last = jnp.full((1, LANES), count, F32)
     send_block(pay_ref, wide_rows(wide_sum, square, sz.wide - LANES, last))
 
@@ -298,7 +313,7 @@
 def send_kernel(sz, x_ref, c_ref, after_ref, *out_refs):
     del after_ref
     for step, out_ref in enumerate(out_refs):
-        first = partner(sz, step) * sz.own
+        first = partner(step) * sz.own
         out_ref[...] = jnp.zeros(out_ref.shape, BF16)
         for t in range(sz.rows):
             at = (t % 2) * 2 * sz.chans
@@ -313,7 +328,7 @@
         refs[5:8],
         *refs[8:15],
     )
-    par_ref, tap_ref, unit_ref, info_ref, pw_ref, w_ref = refs[15:]
+    par_ref, tap_ref, unit_ref, info_ref, pw_ref, pwt_ref, w_ref, wt_ref, far_info = refs[15:]
     par_ref[...] = jnp.zeros(par_ref.shape, F32)
     for at, ref in enumerate(wide_refs):
         par_ref[at : at + 1] = vector(ref)
@@ -322,7 +337,9 @@
     par_ref[8 : 8 + sz.squeeze] = rw_ref[...]
     par_ref[16 : 16 + sz.squeeze] = sw_ref[...]
     pw_ref[...] = pw_in[...]
+    pwt_ref[...] = turned(pw_in[...])
     w_ref[...] = w_in[...]
+    wt_ref[...] = turned(w_in[...])
     taps = spread_rows([dw_ref[i, j : j + 1].astype(F32) for i in range(3) for j in range(3)])
     for at in range(9):
         tap_ref[at] = taps[at]
@@ -346,27 +363,34 @@
         info_ref[t : t + 1] = (block * sz.rows + t < length).astype(F32)
     info_ref[7:8] = jnp.full((1, LANES), (count * sz.width).astype(F32))
     info_ref[8:16] = frames
-
-
-def gather_kernel(sz, *refs):
-    own_refs, (w_ref, exp_ref, xc_ref, all_ref) = refs[: sz.tiles], refs[sz.tiles :]
+    lane_seg = lax.div(iota((1, LANES), 1), sz.width)
+    length = jnp.zeros((1, LANES), jnp.int32)
+    for s in range(sz.segs):
+        held = jnp.where(s < count_ref[0], len_ref[s], 0)
+        length = jnp.where(lane_seg == s, held, length)
+    far_info[...] = jnp.zeros(far_info.shape, F32)
+    first = lax.axis_index("tile") * sz.rows
+    for t in range(sz.rows):
+        far_info[t : t + 1] = (first + t < length).astype(F32)
+
+
+def stage_one_kernel(sz, pay_ref, *refs):
+    own_refs = refs[: sz.tiles]
+    wt_ref, par_ref, tap_ref, unit_ref, info_ref = refs[sz.tiles : sz.tiles + 5]
+    refs = refs[sz.tiles + 5 :]
+    out_pay, xc_ref, act0_ref, deep_ref, ec_ref, s0_ref, row_ref, near_ref, part_ref = refs[:9]
+    mat_ref, acc_ref, sh_ref, buf_ref, all_ref = refs[9:]
     for step, ref in enumerate(own_refs):
-        all_ref[partner(sz, sz.tiles - step)] = ref[...]
+        all_ref[partner(step)] = ref[...]
     unit = eye(LANES, LANES, BF16)
-    weights = w_ref[...]
+    expanded = []
     for g in range(sz.rows // 2):
         flat = dot(unit, all_ref[:, :, g].reshape(LANES, LANES), 1, 1)
         for par in range(2):
             at = par * 2 * sz.chans
-            t = 2 * g + par
-            x_at = flat[at : at + sz.chans]
-            xc_ref[t] = flat[at : at + 2 * sz.chans].astype(BF16)
-            exp_ref[t] = dot(weights, x_at.astype(BF16), 0, 0)
-
-
-def stage_one_kernel(sz, pay_ref, exp_ref, xc_ref, par_ref, tap_ref, unit_ref, info_ref, *refs):
-    out_pay, act0_ref, deep_ref, ec_ref, s0_ref, row_ref, near_ref, part_ref = refs[:8]
-    mat_ref, acc_ref, sh_ref, buf_ref = refs[8:]
+            xc_ref[2 * g + par] = flat[at : at + 2 * sz.chans].astype(BF16)
+            cells = flat[at : at + sz.chans].astype(BF16)
+            expanded.append(dot(wt_ref[...], cells, 1, 0))
     chans = sz.chans
     half = sz.wide - LANES
     mean0, inv0, total = wide_moments(sz, pay_ref, half)
@@ -380,7 +404,7 @@
     acts = []
     squares = 0.0
     for t in range(sz.rows):
-        centred = exp_ref[t] - mean_c
+        centred = expanded[t] - mean_c
         pre = centred * slope_c + bias_c
         gate = sigmoid(pre)
         held = pre * gate
@@ -398,30 +422,31 @@
     before = jnp.where(block == 0, 0.0, pltpu.roll(full[-1], step, 1))
     after = jnp.where(block == sz.tiles - 1, 0.0, pltpu.roll(full[0], LANES - step, 1))
     full = [before] + full + [after]
-    left = [jnp.where(spot == 0, 0.0, row) for row in full]
-    right = [jnp.where(spot == sz.width - 1, 0.0, row) for row in full]
-    moved = [right, full, left]
+    left = jnp.broadcast_to(jnp.where(spot == 0, 0.0, 1.0), (8, LANES))
+    right = jnp.broadcast_to(jnp.where(spot == sz.width - 1, 0.0, 1.0), (8, LANES))
     total_sum = []
     for e in range(0, sz.wide, 8):
         part = slice(e, e + 8)
         taps = [tap_ref[at, part] for at in range(9)]
         acts = [half_of(act0_ref, t, e) for t in range(sz.rows)]
         sums = 0.0
+        edged = [taps[3 * i] * right + taps[3 * i + 1] + taps[3 * i + 2] * left for i in range(3)]
         for t in range(sz.rows):
             deep = 0.0
             back = 0.0
             for i in range(3):
+                back = back + full[t + 2 - i] * edged[i]
                 for j in range(3):
                     deep = deep + sh_ref[j, t + i, part] * taps[3 * i + j]
-                    back = back + moved[j][t + 2 - i] * taps[3 * i + j]
             deep_ref[t, part] = deep
             sums = sums + deep * masks[t]
             mat_ref[t, part] = back * s0_ref[t, part]
         total_sum.append(sums)
         for i in range(3):
-            for j in range(3):
-                held = sum(moved[j][t + 2 - i] * acts[t] for t in range(sz.rows))
-                acc_ref[3 * i + j, part] = held
+            held = sum(full[t + 2 - i] * acts[t] for t in range(sz.rows))
+            acc_ref[3 * i, part] = held * right
+            acc_ref[3 * i + 1, part] = held
+            acc_ref[3 * i + 2, part] = held * left
     total_sum = jnp.concatenate(total_sum, axis=0)
     mean_own = lane_sum(total_sum) / jnp.maximum(count[:, 0:1], 1.0)
     square = 0.0
@@ -573,7 +598,7 @@
     tap_ref,
     unit_ref,
     info_ref,
-    pw_ref,
+    pwt_ref,
     part_ref,
     sq_ref,
     row_ref,
@@ -630,7 +655,7 @@
         branch_sq = branch_sq + branch * branch
         result_sq = result_sq + result * result * masks[t]
         grad = scale * (both[chans:] - (bg_c + normed * gg_c)) * masks[t]
-        wide_grad = dot(pw_ref[...], grad.astype(BF16), 0, 0)
+        wide_grad = dot(pwt_ref[...], grad.astype(BF16), 1, 0)
         ga_ref[t] = wide_grad
         act = act1_ref[t]
         gate_sum = gate_sum + wide_grad * act
@@ -767,74 +792,53 @@
         turned = jnp.concatenate(pieces, axis=0).T.astype(BF16)
         all_ref[:, :, g] = turned.reshape(sz.tiles, sz.own, sz.width, LANES)
     for step, out_ref in enumerate(out_refs):
-        out_ref[...] = all_ref[partner(sz, step)]
-
-
-def far_kernel(sz, pay_ref, row0_ref, w_ref, after_ref, far_ref, buf_ref, near_ref):
-    del after_ref
+        out_ref[...] = all_ref[partner(step)]
+
+
+def far_parts(sz, pay_ref, row0_ref, weights, buf_ref, near_ref):
     chans = sz.chans
-    held = every(sz, pay_ref, 3, 8)
-    near_ref[...] = held[0:32]
+    near_ref[...] = every(sz, pay_ref, 3, 8)[0:32]
     buf_ref[...] = jnp.zeros(buf_ref.shape, F32)
     for k in range(5):
         rows = min(32, sz.wide - 32 * k)
         buf_ref[32 * k : 32 * k + rows, 0:chans] = near_ref[0:rows, chans * k : chans * (k + 1)]
-    far_ref[0:chans] = dot(eye(chans, LANES), buf_ref[...], 1, 1, True)
+    two = picked_rows(buf_ref[...], chans)
     x_row = [near_ref[chans + k : chans + k + 1, 5 * chans : LANES] for k in range(3)]
     x_row = jnp.concatenate(x_row, axis=1)
     x_column = columns_of([x_row])[:, 0:1]
     right = near_ref[0:chans, 5 * chans : LANES]
-    below = right.T[0:8, 0:16]
-    below = jnp.concatenate([below, right[16:chans]], axis=1)
+    below = jnp.concatenate([right.T[0:8, 0:16], right[16:chans]], axis=1)
     second = jnp.concatenate([near_ref[16:32, 4 * chans : 5 * chans], below], axis=0)
     second = second - x_column * x_row / row0_ref[2:3, :chans]
-    wide = dot(second, w_ref[...].astype(F32), 1, 0, True)
-    far_ref[chans : 2 * chans] = wide * row0_ref[1:2]
-    far_ref[2 * chans : 3 * chans, 0:1] = x_column
-    far_ref[3 * chans : 3 * chans + 1, 0:1] = near_ref[
-        chans + 3 : chans + 4, 5 * chans : 5 * chans + 1
-    ]
-
-
-def return_kernel(sz, *refs):
-    got_refs = refs[: sz.tiles]
-    c_ref, out_ref, pre_ref = refs[sz.tiles :]
-    chans = sz.chans
-    for step, ref in enumerate(got_refs):
-        first = partner(sz, sz.tiles - step) * sz.own
-        for t in range(sz.rows):
-            at = (t % 2) * 2 * chans
-            out_ref[pl.ds(first, sz.own), t] = ref[:, t // 2, :, at : at + chans]
-            back = ref[:, t // 2, :, at + chans : at + 2 * chans].astype(F32)
-            pre_ref[pl.ds(first, sz.own), t] = back + c_ref[pl.ds(first, sz.own), t].astype(F32)
+    wide = dot(second, weights, 1, 0, True) * row0_ref[1:2]
+    spot = chans + 3
+    return two, wide, x_column, near_ref[spot : spot + 1, 5 * chans : 5 * chans + 1]
+
+
+def picked_rows(columns, count):
+    unit = eye(max(count, 16), LANES, BF16)
+    return dot(jnp.concatenate([unit] * 3, axis=1), tripled(columns), 1, 1)[0:count]
 
 
 def last_kernel(
     sz,
     pay_ref,
-    pre_ref,
+    far_pay,
     x_ref,
-    far_ref,
+    c_ref,
+    far_info,
     row0_ref,
     row1_ref,
     mid_ref,
     par_ref,
     w_ref,
-    len_ref,
-    count_ref,
-    xg_ref,
-    ew_ref,
-    gg0_ref,
-    bg0_ref,
-    dw_ref,
-    rw_ref,
-    rb_ref,
-    sw_ref,
-    sb_ref,
-    pw_ref,
-    rms_ref,
-    buf_ref,
+    *refs,
 ):
+    got_refs = refs[: sz.tiles]
+    out_ref, xg_ref, ew_ref, gg0_ref, bg0_ref, dw_ref, rw_ref, rb_ref = refs[
+        sz.tiles : sz.tiles + 8
+    ]
+    sw_ref, sb_ref, pw_ref, rms_ref, buf_ref, near_ref, corr_ref = refs[sz.tiles + 8 :]
     chans = sz.chans
     half = sz.wide - LANES
     each = LANES // sz.devices
@@ -855,15 +859,34 @@
     offset = dot(offset, weights, 1, 1, True)[0:1]
     high = matrix.astype(BF16)
     low = (matrix - high.astype(F32)).astype(BF16)
-    first = lax.axis_index("tile") * sz.rows
+    shape = (16, sz.rows * LANES)
+    unit = jnp.where(iota(shape, 0) == lax.div(iota(shape, 1), LANES), 1.0, 0.0).astype(BF16)
+    live = dot(far_info[...].astype(BF16), unit, 0, 0)
     for t in range(sz.rows):
         cells = x_ref[:, t].reshape(sz.segs * sz.width, chans)
         back = dot(cells, high, 1, 0) + dot(cells, low, 1, 0) + offset
-        for s in range(sz.segs):
-            length = jnp.where(s < count_ref[0], len_ref[s], 0)
-            live = jnp.where(first + t < length, 1.0, 0.0)
-            held = back[s * sz.width : (s + 1) * sz.width] * live
-            xg_ref[s, t] = (pre_ref[s, t] - held).astype(BF16)
+        corr_ref[t] = back * live[:, t * LANES : t * LANES + chans]
+    shape = (LANES, 4 * LANES)
+    column = iota(shape, 1)
+    spot = lax.rem(column, LANES)
+    source = spot + chans * lax.div(column, LANES)
+    unit = jnp.where((iota(shape, 0) == source) & (spot < chans), 1.0, 0.0).astype(BF16)
+    size = sz.own * sz.width
+    shape = (sz.own, sz.width, chans)
+    for step, ref in enumerate(got_refs):
+        first = partner(step) * sz.own
+        for g in range(sz.rows // 2):
+            cells = dot(ref[:, g].reshape(size, LANES), unit, 1, 0)
+            for par in range(2):
+                t = 2 * g + par
+                at = 2 * par * LANES
+                held = cells[:, at : at + chans]
+                out_ref[pl.ds(first, sz.own), t] = held.astype(BF16).reshape(shape)
+                at = at + LANES
+                held = cells[:, at : at + chans] - corr_ref[t, pl.ds(first * sz.width, size)]
+                held = held.reshape(shape) + c_ref[pl.ds(first, sz.own), t].astype(F32)
+                xg_ref[pl.ds(first, sz.own), t] = held.astype(BF16)
+    two, wide, x_sum, act0_sq = far_parts(sz, far_pay, row0_ref, weights, buf_ref, near_ref)
     used = 3 * chans + 29 + 2 * sz.squeeze
     piece = LANES - used
     for k in range(each):
@@ -874,16 +897,13 @@
         buf_ref[LANES : LANES + half, k * piece : k * piece + take] = buf_ref[
             k * half : (k + 1) * half, used : used + take
         ]
-    rows = dot(eye(LANES, LANES), buf_ref[...], 1, 1, True)
+    rows = picked_rows(buf_ref[...], LANES)
     inv1 = row1_ref[1:2]
     scale1 = inv1 * par_ref[2:3]
     bias1 = mid_ref[0:1] / total
     gain1 = mid_ref[1:2] * inv1 / total
-    inner = rows[0:chans] - far_ref[0:chans] * bias1 - rows[chans : 2 * chans] * gain1
-    x_sum = far_ref[2 * chans : 3 * chans, 0:1]
-    ew_ref[...] = scale0 * (
-        scale1 * inner - x_sum * bias_row - far_ref[chans : 2 * chans] * gain_row
-    )
+    inner = rows[0:chans] - two * bias1 - rows[chans : 2 * chans] * gain1
+    ew_ref[...] = scale0 * (scale1 * inner - x_sum * bias_row - wide * gain_row)
     pw_ref[...] = rows[2 * chans : 3 * chans]
     spot = 3 * chans
     held = rows[spot : spot + 9] - rows[spot + 9 : spot + 18] * bias1
@@ -898,7 +918,6 @@
     sb_ref[...] = rows[spot : spot + 1].reshape(sz.wide)
     misc = rows[spot + 1 : spot + 2]
     rb_ref[...] = misc[:, : sz.squeeze].reshape(sz.squeeze)
-    act0_sq = far_ref[3 * chans : 3 * chans + 1, 0:1]
     squares = jnp.concatenate(
         [misc[:, 8:9], act0_sq, misc[:, 9:10], misc[:, 10:11], misc[:, 11:12]], axis=1
     )
@@ -930,10 +949,10 @@
 
 
 def passed(sz, parts):
-    result = [parts[0]]
-    for step in range(1, sz.tiles):
-        pairs = [(i, (i + step) % sz.tiles) for i in range(sz.tiles)]
-        result.append(lax.ppermute(parts[step], "tile", pairs))
+    result = list(parts)
+    for step in list(range(2, sz.tiles)) + [1]:
+        pairs = [(i, i ^ step) for i in range(sz.tiles)]
+        result[step] = lax.ppermute(parts[step], "tile", pairs)
     return result
 
 
@@ -985,12 +1004,12 @@
             (expand_w.shape, BF16),
             pltpu.SMEM(seg_len.shape, jnp.int32),
             pltpu.SMEM(seg_count.shape, jnp.int32),
-            pltpu.SemaphoreType.DMA((4,)),
+            pltpu.SemaphoreType.DMA((3 + segs,)),
         ],
         room=60,
     )
     parts = call(send_kernel, sz, [x_input, cotangent, pay], "vva", [block] * tiles)
-    par, tap, unit, info, pw_near, w_near = call(
+    par, tap, unit, info, pw_near, pw_turned, w_near, w_turned, far_info = call(
         setup_kernel,
         sz,
         [gain0, bias0, gain1, bias1, restore_b, gain2, bias2, reduce_b, dw_kernel, reduce_w.T]
@@ -1002,22 +1021,22 @@
             ((2 * LANES, 4 * LANES), BF16),
             ((16, LANES), F32),
             ((chans, wide), BF16),
+            ((wide, chans), BF16),
             ((chans, wide), BF16),
+            ((wide, chans), BF16),
+            ((16, LANES), F32),
         ],
     )
     pay = everywhere(pay)
     parts = passed(sz, parts)
-    exp, x_c = call(
-        gather_kernel, sz, parts + [w_near], "", [big, both], [((tiles,) + block[0], BF16)]
-    )
-    pay, act0, deep, ec, s0, row0, near, part = call(
+    pay, x_c, act0, deep, ec, s0, row0, near, part = call(
         stage_one_kernel,
         sz,
-        [pay, exp, x_c, par, tap, unit, info],
+        [pay] + parts + [w_turned, par, tap, unit, info],
         "",
-        [pay_of(4), packed, big, big, big, ((3, wide), F32)]
+        [pay_of(4), both, packed, big, big, big, ((3, wide), F32)]
         + [((max(32, devices), LANES), F32), column],
-        [big, taps, shifts, column],
+        [big, taps, shifts, column, ((tiles,) + block[0], BF16)],
     )
     pay = everywhere(pay)
     pay, act1, dc, s1, proj, gate, seg_rows, row1, part, squares = call(
@@ -1034,7 +1053,7 @@
         stage_three_kernel,
         sz,
         [pay, proj, x_c, act0, act1, s0, dc, s1, gate, seg_rows, par, tap, unit, info]
-        + [pw_near, part, squares, row1],
+        + [pw_turned, part, squares, row1],
         "",
         [pay_of(8), small, big, ((chans,), F32), ((chans,), F32)],
         [big, big, taps, shifts, column],
@@ -1057,28 +1076,14 @@
         [((tiles,) + block[0], BF16)],
     )
     pay = everywhere(pay)
-    (far,) = call(
-        far_kernel,
-        sz,
-        [far_pay, row0, w_near, gp0],
-        "vvva",
-        [((3 * chans + 8, wide), F32)],
-        [column, ((32, LANES), F32)],
-    )
     sent = passed(sz, sent)
-    block_out, pre = call(
-        return_kernel,
-        sz,
-        sent + [cotangent],
-        "",
-        [(x_input.shape, BF16), (x_input.shape, F32)],
-    )
-    x_grad, ew, gg0, bg0, dw, rw, rb, sw, sb, pw, rms = call(
+    block_out, x_grad, ew, gg0, bg0, dw, rw, rb, sw, sb, pw, rms = call(
         last_kernel,
         sz,
-        [pay, pre, x_input, far, row0, row1, mid, par, w_near, seg_len, seg_count],
-        "v" * 9 + "ss",
+        [pay, far_pay, x_input, cotangent, far_info, row0, row1, mid, par, w_near] + sent,
+        "",
         [
+            (x_input.shape, BF16),
             (x_input.shape, BF16),
             ((chans, wide), F32),
             ((wide,), F32),
@@ -1091,7 +1096,7 @@
             ((chans, wide), F32),
             ((5,), F32),
         ],
-        [column],
+        [column, ((32, LANES), F32), ((rows, LANES, chans), F32)],
     )
     return (
         block_out,

time: 72.8 us -> 71.7 us (0.985)
  waiting for transfers between devices: 4.12 us -> 9.24 us
  Pallas kernels: 19.4 us -> 16.8 us
  starting transfers between devices: 16.4 us -> 13.8 us
  blocking collectives: 30.3 us -> 29.2 us
    ppermute x6, waiting for transfers between devices: 0.99 us -> 5.29 us  [passed(): result[step] = lax.ppermute(parts[step], 'tile', pairs)]
    pallas_call x12 -> x9, Pallas kernels: 19.4 us -> 16.8 us  [call(): pl.pallas_call(functools.partial(kernel, sz), out_shape=tuple((jax.ShapeD...]
    ppermute x6, starting transfers between devices: 6.47 us -> 3.96 us  [passed(): result[step] = lax.ppermute(parts[step], 'tile', pairs)]
    all_to_all x3, blocking collectives: 30.3 us -> 29.2 us  [everywhere(): return lax.all_to_all(values, BOTH, 0, 0, tiled=True)]
    all_to_all x2, waiting for transfers between devices: 3.13 us -> 3.95 us  [everywhere(): return lax.all_to_all(values, BOTH, 0, 0, tiled=True)]
  transfers between devices with their start and end apart: 8 -> 8, of which waited for: 4 -> 6; matrix products, arithmetic and copies ran while one was open for 0% -> 0% of each run, Pallas kernels for 6% -> 2%
where the time goes in v2:
time: 71.7 us; the launch traced here: 71.4 us
  blocking collectives  29.2 us (41%)
  Pallas kernels  16.8 us (23%)
  starting transfers between devices  13.8 us (19%)
  waiting for transfers between devices  9.24 us (13%)
  between operations  1.59 us (2%)
    all_to_all x3, blocking collectives, everywhere(): return lax.all_to_all(values, BOTH, 0, 0, tiled=True)  29.2 us
    pallas_call x9, Pallas kernels, call(): pl.pallas_call(functools.partial(kernel, sz), out_shape=tuple((jax.ShapeD...  16.8 us
    all_to_all x2, starting transfers between devices, everywhere(): return lax.all_to_all(values, BOTH, 0, 0, tiled=True)  9.88 us
    ppermute x6, waiting for transfers between devices, passed(): result[step] = lax.ppermute(parts[step], 'tile', pairs)  5.29 us
    ppermute x6, starting transfers between devices, passed(): result[step] = lax.ppermute(parts[step], 'tile', pairs)  3.96 us
    all_to_all x2, waiting for transfers between devices, everywhere(): return lax.all_to_all(values, BOTH, 0, 0, tiled=True)  3.95 us
  transfers between devices with their start and end apart: 8, of which 6 were waited for; matrix products, arithmetic and copies ran while one was open for 0% of the time, Pallas kernels for 2%

profile of v2, /device:TPU:0, one launch (start us, length us, event | category | flops | bytes accessed | tf_op | source)
XLA Modules:
  0.0 71.4 jit_solution(4556053942423913739)
XLA Ops:
  1.3 2.5 %entry_kernel.1.after_ref = f32[128,128]{1,0:T(8,128)} custom-call(bf16[8,6,16,24]{3,2,1,0:T(8,128)(2,1)} %x_ref.3, bf16[24,144]{1,0:T(8,128)(2,1)} %refs_12_.1, s32[8]{0:T(128)} %refs_13_.1, s32[1]{0:T(128)S(6)} %copy.33.count_hbm.refs_14_), custom_call_target="tpu_custom_call" | custom-call | flops 1000000000 | bytes 3000000 | tf_op jit(solution)/shard_map/entry_kernel/pallas_call | solution.py:933
  3.8 0.0 copy-start
  3.9 7.3 %all-to-all-start = ((f32[32,4,128]{2,1,0:T(4,128)}), f32[32,4,128]{2,1,0:T(4,128)S(1)}, u32[]{:S(2)}, u32[]{:S(2)}) async-start(f32[32,4,128]{2,1,0:T(4,128)} %bitcast.19), calls=%async_computation | async-start | bytes 131072 | tf_op jit(solution)/shard_map/all_to_all | solution.py:948
  11.2 0.0 copy-start.3
  11.2 0.0 copy-start.4
  11.2 0.0 copy-start.6
  11.2 0.0 copy-start.7
  11.2 0.0 copy-start.9
  11.3 0.0 copy-start.10
  11.3 0.0 copy-start.11
  11.3 0.0 copy-start.12
  11.3 0.0 copy-start.13
  11.3 0.0 copy-start.14
  11.3 0.0 copy-start.15
  11.3 0.0 copy-start.16
  11.3 0.2 send_kernel.1
  11.6 0.3 collective-permute-start
  11.9 1.7 %collective-permute-start.1 = (bf16[2,3,16,128]{3,2,1,0:T(8,128)(2,1)S(1)}, bf16[2,3,16,128]{3,2,1,0:T(8,128)(2,1)S(1)}, u32[]{:S(2)}, u32[]{:S(2)}) collective-permute-start(bf16[2,3,16,128]{3,2,1,0:T(8,128)(2,1)S(1)} %get-tuple-element.76), channel_id=1, source_target_pairs={{0,2},{1,3},{2,0},{3,1},{4,6},{5,7},{6,4},{7,5},{8,10},{9,11},{10,... | collective-permute-start | bytes 73736 | tf_op jit(solution)/shard_map/ppermute | solution.py:955
  13.6 0.0 collective-permute-start.2
  13.6 0.0 copy-done.6
  13.6 0.0 copy-done.7
  13.6 0.0 copy-done.9
  13.6 0.0 copy-done.10
  13.6 0.0 copy-done.11
  13.6 0.0 copy-done.12
  13.7 0.6 copy-done.8
  14.3 0.8 %setup_kernel.1 = (f32[24,144]{1,0:T(8,128)S(1)}, f32[9,144,128]{2,1,0:T(8,128)S(1)}, bf16[256,512]{1,0:T(8,128)(2,1)S(1)}, f32[16,128]{1,0:T(8,128)S(1)}, bf16[...) custom-call(f32[144]{0:T(256)S(1)} %copy-done.8, ...), custom_call_target="tpu_custom_call" | custom-call | flops 1000000000 | bytes 3000000 | tf_op jit(solution)/shard_map/setup_kernel/pallas_call | solution.py:933
  15.1 0.0 collective-permute-done.refs_1_
  15.1 0.7 collective-permute-done.1.refs_2_
  15.8 1.1 %collective-permute-done.2.refs_3_ = bf16[2,3,16,128]{3,2,1,0:T(8,128)(2,1)S(1)} collective-permute-done((bf16[2,3,16,128]{3,2,1,0:T(8,128)(2,1)S(1)}, bf16[2,3,16,128]{3,2,1,0:T(8,128)(2,1)S(1)}, u32[]{:S(2)}, u32[]{:S(2)}) %collective-permute-start.2) | collective-permute-done | bytes 24608 | tf_op jit(solution)/shard_map/ppermute | solution.py:955
  16.9 1.6 %all-to-all-done = f32[32,4,128]{2,1,0:T(4,128)S(1)} async-done(((f32[32,4,128]{2,1,0:T(4,128)}), f32[32,4,128]{2,1,0:T(4,128)S(1)}, u32[]{:S(2)}, u32[]{:S(2)}) %all-to-all-start) | async-done | bytes 65568 | tf_op jit(solution)/shard_map/all_to_all | solution.py:948
  18.6 2.2 %stage_one_kernel.1 = (f32[128,128]{1,0:T(8,128)S(1)}, bf16[6,48,128]{2,1,0:T(8,128)(2,1)S(1)}, bf16[6,144,128]{2,1,0:T(8,128)(2,1)S(1)}, f32[6,144,128]{2,1,0:T...) custom-call(f32[128,128]{1,0:T(8,128)S(1)} %bitcast.18, ...), custom_call_target="tpu_custom_call" | custom-call | flops 1000000000 | bytes 3000000 | tf_op jit(solution)/shard_map/stage_one_kernel/pallas_call | solution.py:933
  20.7 10.3 %all_to_all.55 = f32[32,4,128]{2,1,0:T(4,128)S(1)} all-to-all(f32[32,4,128]{2,1,0:T(4,128)S(1)} %bitcast.20), channel_id=1, replica_groups=mesh['seg'=8,'tile'=4] {'seg','tile'}, dimensions={0} | all-to-all | bytes 131072 | tf_op jit(solution)/shard_map/all_to_all | solution.py:948
  31.1 3.1 %stage_two_kernel.1 = (f32[64,128]{1,0:T(8,128)S(1)}, f32[6,144,128]{2,1,0:T(8,128)S(1)}, f32[6,144,128]{2,1,0:T(8,128)S(1)}, f32[6,144,128]{2,1,0:T(8,128)S(1)}...) custom-call(f32[128,128]{1,0:T(8,128)S(1)} %bitcast.21, ...), custom_call_target="tpu_custom_call" | custom-call | flops 1000000000 | bytes 3000000 | tf_op jit(solution)/shard_map/stage_two_kernel/pallas_call | solution.py:933
  34.2 8.9 %all_to_all.56 = f32[32,2,128]{2,1,0:T(2,128)S(1)} all-to-all(f32[32,2,128]{2,1,0:T(2,128)S(1)} %bitcast.23), channel_id=1, replica_groups=mesh['seg'=8,'tile'=4] {'seg','tile'}, dimensions={0} | all-to-all | bytes 65536 | tf_op jit(solution)/shard_map/all_to_all | solution.py:948
  43.1 3.9 %stage_three_kernel.1 = (f32[256,128]{1,0:T(8,128)S(1)}, f32[6,24,128]{2,1,0:T(8,128)S(1)}, f32[6,144,128]{2,1,0:T(8,128)S(1)}, f32[24]{0:T(128)}, f32[24]{0:T(128)}) custom-call(f32[64,128]{1,0:T(8,128)S(1)} %bitcast.22, f32[6,24,128]{2,1,0:T(8,128)S(1)} %get-tuple-element.92.proj_ref, bf16[6,48,128]{2,1,0:T(8,128)(2,1)S(1)} %get-tuple-element.85.xc_ref, ...), custom_call_target="tpu_custom_call" | custom-call | flops 1000000000 | bytes 3000000 | tf_op jit(solution)/shard_map/stage_three_kernel/pallas_call | solution.py:933
  47.0 9.9 %all_to_all.57 = f32[32,8,128]{2,1,0:T(8,128)S(1)} all-to-all(f32[32,8,128]{2,1,0:T(8,128)S(1)} %bitcast.17), channel_id=1, replica_groups=mesh['seg'=8,'tile'=4] {'seg','tile'}, dimensions={0} | all-to-all | bytes 262144 | tf_op jit(solution)/shard_map/all_to_all | solution.py:948
  57.0 1.9 %stage_four_kernel.1 = (f32[256,128]{1,0:T(8,128)}, f32[6,144,128]{2,1,0:T(8,128)S(1)}, f32[144]{0:T(256)}, f32[144]{0:T(256)}, f32[2,144]{1,0:T(2,128)S(1)}) custom-call(f32[256,128]{1,0:T(8,128)S(1)} %bitcast.14, f32[6,144,128]{2,1,0:T(8,128)S(1)} %get-tuple-element.103.scaled_ref, f32[6,144,128]{2,1,0:T(8,128)S(1)} %get-tuple-element.94.dc_ref, ...), custom_call_target="tpu_custom_call" | custom-call | flops 1000000000 | bytes 3000000 | tf_op jit(solution)/shard_map/stage_four_kernel/pallas_call | solution.py:933
  58.9 2.6 %all-to-all-start.4 = ((f32[32,8,128]{2,1,0:T(8,128)}), f32[32,8,128]{2,1,0:T(8,128)S(1)}, u32[]{:S(2)}, u32[]{:S(2)}) async-start(f32[32,8,128]{2,1,0:T(8,128)} %bitcast.10), calls=%async_computation.4 | async-start | bytes 262144 | tf_op jit(solution)/shard_map/all_to_all | solution.py:948
  61.4 0.5 back_kernel.1
  61.9 0.2 collective-permute-start.3
  62.1 1.7 %collective-permute-start.4 = (bf16[2,3,16,128]{3,2,1,0:T(8,128)(2,1)S(1)}, bf16[2,3,16,128]{3,2,1,0:T(8,128)(2,1)S(1)}, u32[]{:S(2)}, u32[]{:S(2)}) collective-permute-start(bf16[2,3,16,128]{3,2,1,0:T(8,128)(2,1)S(1)} %get-tuple-element.114), channel_id=1, source_target_pairs={{0,2},{1,3},{2,0},{3,1},{4,6},{5,7},{6,4},{7,5},{8,10},{9,11},{10,... | collective-permute-start | bytes 73736 | tf_op jit(solution)/shard_map/ppermute | solution.py:955
  63.8 0.1 collective-permute-start.5
  63.9 0.0 collective-permute-done.3.refs_1_
  63.9 2.2 %collective-permute-done.4.refs_2_ = bf16[2,3,16,128]{3,2,1,0:T(8,128)(2,1)S(1)} collective-permute-done((bf16[2,3,16,128]{3,2,1,0:T(8,128)(2,1)S(1)}, bf16[2,3,16,128]{3,2,1,0:T(8,128)(2,1)S(1)}, u32[]{:S(2)}, u32[]{:S(2)}) %collective-permute-start.4) | collective-permute-done | bytes 24608 | tf_op jit(solution)/shard_map/ppermute | solution.py:955
  66.1 1.2 %collective-permute-done.5.refs_3_ = bf16[2,3,16,128]{3,2,1,0:T(8,128)(2,1)S(1)} collective-permute-done((bf16[2,3,16,128]{3,2,1,0:T(8,128)(2,1)S(1)}, bf16[2,3,16,128]{3,2,1,0:T(8,128)(2,1)S(1)}, u32[]{:S(2)}, u32[]{:S(2)}) %collective-permute-start.5) | collective-permute-done | bytes 24608 | tf_op jit(solution)/shard_map/ppermute | solution.py:955
  67.4 2.3 %all-to-all-done.4 = f32[32,8,128]{2,1,0:T(8,128)S(1)} async-done(((f32[32,8,128]{2,1,0:T(8,128)}), f32[32,8,128]{2,1,0:T(8,128)S(1)}, u32[]{:S(2)}, u32[]{:S(2)}) %all-to-all-start.4) | async-done | bytes 131104 | tf_op jit(solution)/shard_map/all_to_all | solution.py:948
  69.7 1.7 %last_kernel.1 = (bf16[8,6,16,24]{3,2,1,0:T(8,128)(2,1)}, bf16[8,6,16,24]{3,2,1,0:T(8,128)(2,1)}, f32[24,144]{1,0:T(8,128)}, f32[144]{0:T(256)}, f32[144]{0:T(25...) custom-call(f32[256,128]{1,0:T(8,128)S(1)} %bitcast.16, ...), custom_call_target="tpu_custom_call" | custom-call | flops 1000000000 | bytes 3000000 | tf_op jit(solution)/shard_map/last_kernel/pallas_call | solution.py:933
  (14 shorter events, 0.0 us)
Async XLA Ops:
  1.3 9.9 %copy-start.1 = (bf16[8,6,16,24]{3,2,1,0:T(8,128)(2,1)S(1)}, bf16[8,6,16,24]{3,2,1,0:T(8,128)(2,1)}, u32[]{:S(2)}) copy-start(bf16[8,6,16,24]{3,2,1,0:T(8,128)(2,1)} %x_ref.3) | copy-start | bytes 110596
  1.3 9.9 %copy-start.2 = (bf16[8,6,16,24]{3,2,1,0:T(8,128)(2,1)S(1)}, bf16[8,6,16,24]{3,2,1,0:T(8,128)(2,1)}, u32[]{:S(2)}) copy-start(bf16[8,6,16,24]{3,2,1,0:T(8,128)(2,1)} %c_ref.3) | copy-start | bytes 110596
  3.8 7.3 %copy-start = (f32[128,128]{1,0:T(8,128)S(1)}, f32[128,128]{1,0:T(8,128)}, u32[]{:S(2)}) copy-start(f32[128,128]{1,0:T(8,128)} %entry_kernel.1.after_ref) | copy-start | bytes 196612
  3.9 14.7 %all-to-all-start = ((f32[32,4,128]{2,1,0:T(4,128)}), f32[32,4,128]{2,1,0:T(4,128)S(1)}, u32[]{:S(2)}, u32[]{:S(2)}) async-start(f32[32,4,128]{2,1,0:T(4,128)} %bitcast.19), calls=%async_computation | async-start | bytes 131072 | tf_op jit(solution)/shard_map/all_to_all | solution.py:948
  11.2 2.4 %copy-start.3 = (bf16[24,144]{1,0:T(8,128)(2,1)S(1)}, bf16[24,144]{1,0:T(8,128)(2,1)}, u32[]{:S(2)}) copy-start(bf16[24,144]{1,0:T(8,128)(2,1)} %refs_12_.1) | copy-start | bytes 20740
  11.2 2.4 %copy-start.4 = (bf16[144,24]{0,1:T(8,128)(2,1)S(1)}, bf16[144,24]{0,1:T(8,128)(2,1)}, u32[]{:S(2)}) copy-start(bf16[144,24]{0,1:T(8,128)(2,1)} %param.28) | copy-start | bytes 20740
  11.2 2.4 %copy-start.6 = (f32[6,144]{1,0:T(8,128)S(1)}, f32[6,144]{1,0:T(8,128)}, u32[]{:S(2)}) copy-start(f32[6,144]{1,0:T(8,128)} %refs_10_.1) | copy-start | bytes 10372
  11.2 2.4 %copy-start.7 = (bf16[3,3,144]{2,1,0:T(4,128)(2,1)S(1)}, bf16[3,3,144]{2,1,0:T(4,128)(2,1)}, u32[]{:S(2)}) copy-start(bf16[3,3,144]{2,1,0:T(4,128)(2,1)} %refs_8_.1) | copy-start | bytes 7780
  11.2 2.4 %copy-start.9 = (f32[144]{0:T(256)S(1)}, f32[144]{0:T(256)}, u32[]{:S(2)}) copy-start(f32[144]{0:T(256)} %refs_1_.1) | copy-start | bytes 1732
  11.3 2.4 %copy-start.10 = (f32[144]{0:T(256)S(1)}, f32[144]{0:T(256)}, u32[]{:S(2)}) copy-start(f32[144]{0:T(256)} %refs_2_.1) | copy-start | bytes 1732
  11.3 2.4 %copy-start.11 = (f32[144]{0:T(256)S(1)}, f32[144]{0:T(256)}, u32[]{:S(2)}) copy-start(f32[144]{0:T(256)} %refs_3_.1) | copy-start | bytes 1732
  11.3 2.4 %copy-start.12 = (f32[144]{0:T(256)S(1)}, f32[144]{0:T(256)}, u32[]{:S(2)}) copy-start(f32[144]{0:T(256)} %refs_4_.1) | copy-start | bytes 1732
  11.3 2.4 %copy-start.13 = (s32[8]{0:T(128)S(1)}, s32[8]{0:T(128)}, u32[]{:S(2)}) copy-start(s32[8]{0:T(128)} %refs_13_.1) | copy-start | bytes 100
  11.3 2.4 %copy-start.14 = (f32[24]{0:T(128)S(1)}, f32[24]{0:T(128)}, u32[]{:S(2)}) copy-start(f32[24]{0:T(128)} %refs_5_.1) | copy-start | bytes 292
  11.3 2.4 %copy-start.15 = (f32[24]{0:T(128)S(1)}, f32[24]{0:T(128)}, u32[]{:S(2)}) copy-start(f32[24]{0:T(128)} %refs_6_.1) | copy-start | bytes 292
  11.3 2.4 %copy-start.16 = (f32[6]{0:T(128)S(1)}, f32[6]{0:T(128)}, u32[]{:S(2)}) copy-start(f32[6]{0:T(128)} %refs_7_.1) | copy-start | bytes 76
  11.6 2.1 %copy-start.5 = (f32[144,6]{0,1:T(8,128)S(1)}, f32[144,6]{0,1:T(8,128)}, u32[]{:S(2)}) copy-start(f32[144,6]{0,1:T(8,128)} %param.24) | copy-start | bytes 10372
  11.6 3.5 %collective-permute-start = (bf16[2,3,16,128]{3,2,1,0:T(8,128)(2,1)S(1)}, bf16[2,3,16,128]{3,2,1,0:T(8,128)(2,1)S(1)}, u32[]{:S(2)}, u32[]{:S(2)}) collective-permute-start(bf16[2,3,16,128]{3,2,1,0:T(8,128)(2,1)S(1)} %get-tuple-element.75), channel_id=1, source_target_pairs={{0,1},{1,0},{2,3},{3,2},{4,5},{5,4},{6,7},{7,6},{8,9},{9,8},{10,11... | collective-permute-start | bytes 73736 | tf_op jit(solution)/shard_map/ppermute | solution.py:955
  11.9 3.9 %collective-permute-start.1 = (bf16[2,3,16,128]{3,2,1,0:T(8,128)(2,1)S(1)}, bf16[2,3,16,128]{3,2,1,0:T(8,128)(2,1)S(1)}, u32[]{:S(2)}, u32[]{:S(2)}) collective-permute-start(bf16[2,3,16,128]{3,2,1,0:T(8,128)(2,1)S(1)} %get-tuple-element.76), channel_id=1, source_target_pairs={{0,2},{1,3},{2,0},{3,1},{4,6},{5,7},{6,4},{7,5},{8,10},{9,11},{10,... | collective-permute-start | bytes 73736 | tf_op jit(solution)/shard_map/ppermute | solution.py:955
  13.6 3.4 %collective-permute-start.2 = (bf16[2,3,16,128]{3,2,1,0:T(8,128)(2,1)S(1)}, bf16[2,3,16,128]{3,2,1,0:T(8,128)(2,1)S(1)}, u32[]{:S(2)}, u32[]{:S(2)}) collective-permute-start(bf16[2,3,16,128]{3,2,1,0:T(8,128)(2,1)S(1)} %get-tuple-element.77), channel_id=1, source_target_pairs={{0,3},{1,2},{2,1},{3,0},{4,7},{5,6},{6,5},{7,4},{8,11},{9,10},{10,... | collective-permute-start | bytes 73736 | tf_op jit(solution)/shard_map/ppermute | solution.py:955
  13.6 0.7 copy-start.8
  58.9 10.8 %all-to-all-start.4 = ((f32[32,8,128]{2,1,0:T(8,128)}), f32[32,8,128]{2,1,0:T(8,128)S(1)}, u32[]{:S(2)}, u32[]{:S(2)}) async-start(f32[32,8,128]{2,1,0:T(8,128)} %bitcast.10), calls=%async_computation.4 | async-start | bytes 262144 | tf_op jit(solution)/shard_map/all_to_all | solution.py:948
  61.9 2.0 %collective-permute-start.3 = (bf16[2,3,16,128]{3,2,1,0:T(8,128)(2,1)S(1)}, bf16[2,3,16,128]{3,2,1,0:T(8,128)(2,1)S(1)}, u32[]{:S(2)}, u32[]{:S(2)}) collective-permute-start(bf16[2,3,16,128]{3,2,1,0:T(8,128)(2,1)S(1)} %get-tuple-element.113), channel_id=1, source_target_pairs={{0,1},{1,0},{2,3},{3,2},{4,5},{5,4},{6,7},{7,6},{8,9},{9,8},{10,11... | collective-permute-start | bytes 73736 | tf_op jit(solution)/shard_map/ppermute | solution.py:955
  62.1 4.0 %collective-permute-start.4 = (bf16[2,3,16,128]{3,2,1,0:T(8,128)(2,1)S(1)}, bf16[2,3,16,128]{3,2,1,0:T(8,128)(2,1)S(1)}, u32[]{:S(2)}, u32[]{:S(2)}) collective-permute-start(bf16[2,3,16,128]{3,2,1,0:T(8,128)(2,1)S(1)} %get-tuple-element.114), channel_id=1, source_target_pairs={{0,2},{1,3},{2,0},{3,1},{4,6},{5,7},{6,4},{7,5},{8,10},{9,11},{10,... | collective-permute-start | bytes 73736 | tf_op jit(solution)/shard_map/ppermute | solution.py:955
  63.8 3.5 %collective-permute-start.5 = (bf16[2,3,16,128]{3,2,1,0:T(8,128)(2,1)S(1)}, bf16[2,3,16,128]{3,2,1,0:T(8,128)(2,1)S(1)}, u32[]{:S(2)}, u32[]{:S(2)}) collective-permute-start(bf16[2,3,16,128]{3,2,1,0:T(8,128)(2,1)S(1)} %get-tuple-element.115), channel_id=1, source_target_pairs={{0,3},{1,2},{2,1},{3,0},{4,7},{5,6},{6,5},{7,4},{8,11},{9,10},{10,... | collective-permute-start | bytes 73736 | tf_op jit(solution)/shard_map/ppermute | solution.py:955

commit v3 on v2

--- a/solution.py
+++ b/solution.py
@@ -44,6 +44,15 @@
     )
 
 
+def fine_dot(left, right):
+    high = left.astype(BF16).astype(F32)
+    left = jnp.concatenate([high, left - high, high], axis=0).astype(BF16)
+    high = right.astype(BF16).astype(F32)
+    right = jnp.concatenate([high, high, right - high], axis=0).astype(BF16)
+    held = dot(left, right, 1, 1)
+    return held[0:8, 0:8] + held[8:16, 8:16] + held[16:24, 16:24]
+
+
 def eye(rows, cols, dtype=F32):
     return (iota((rows, cols), 0) == iota((rows, cols), 1)).astype(dtype)
 
@@ -118,13 +127,6 @@
     spare = (-width) % LANES
     held = jnp.concatenate([cells.astype(F32), jnp.zeros((rows, spare), F32)], axis=1)
     return held.T[:width].astype(cells.dtype)
-
-
-def placed_cells(cells, first):
-    rows = cells.shape[0]
-    parts = [jnp.zeros((first, LANES), F32)] if first else []
-    parts += [cells, jnp.zeros((LANES - first - rows, LANES), F32)]
-    return jnp.concatenate(parts, axis=0).astype(BF16)
 
 
 def placed_sums(acc_ref, count, start):
@@ -203,19 +205,33 @@
         sh_ref[2, t] = sides[part, LANES:]
 
 
+def pixel_product(values, pix_ref):
+    cells = pix_ref[...].reshape(-1, LANES)
+    even = jnp.concatenate(values[0::2], axis=1)
+    odd = jnp.concatenate(values[1::2], axis=1)
+    if even.dtype == F32:
+        cells = jnp.concatenate([cells, cells], axis=0)
+        even = doubled(even)
+        odd = doubled(odd)
+    return dot(even, cells, 1, 0), dot(odd, cells, 1, 0)
+
+
 def backward_parts(sz, sh_ref, tap_ref, part, acts, acc_ref):
     result = [0.0] * sz.rows
-    for i in range(3):
-        for j in range(3):
-            tap = tap_ref[3 * i + j, part]
-            held = 0.0
-            for t in range(sz.rows):
-                field = sh_ref[2 - j, t + 2 - i, part]
-                result[t] = result[t] + field * tap
-                if acts is not None:
-                    held = held + field * acts[t]
-            if acts is not None:
-                acc_ref[3 * i + j, part] = held
+    for j in range(3):
+        taps = [tap_ref[3 * i + j, part] for i in range(3)]
+        held = [0.0] * 3
+        for at in range(sz.rows + 2):
+            field = sh_ref[2 - j, at, part]
+            for i in range(3):
+                t = at - 2 + i
+                if 0 <= t < sz.rows:
+                    result[t] = result[t] + field * taps[i]
+                    if acts is not None:
+                        held[i] = held[i] + field * acts[t]
+        if acts is not None:
+            for i in range(3):
+                acc_ref[3 * i + j, part] = held[i]
     return result
 
 
@@ -266,48 +282,74 @@
     return lax.bitwise_xor(lax.axis_index("tile"), step)
 
 
-def entry_kernel(sz, x_hbm, w_hbm, len_hbm, count_hbm, pay_ref, *scratch):
+def entry_kernel(sz, x_hbm, w_hbm, len_hbm, count_hbm, pay_ref, info_ref, far_info, *scratch):
     x_ref, w_ref, len_ref, count_ref, sems = scratch
     copies = [
         pltpu.make_async_copy(len_hbm, len_ref, sems.at[0]),
         pltpu.make_async_copy(count_hbm, count_ref, sems.at[1]),
         pltpu.make_async_copy(w_hbm, w_ref, sems.at[2]),
+        pltpu.make_async_copy(x_hbm, x_ref, sems.at[3]),
     ]
-    for s in range(sz.segs):
-        copies.append(pltpu.make_async_copy(x_hbm.at[s], x_ref.at[s], sems.at[3 + s]))
     for copy in copies:
         copy.start()
-    for copy in copies[:3]:
+    for copy in copies[:2]:
         copy.wait()
     tile_pos = lax.axis_index("tile")
     lane_seg = lax.div(iota((1, LANES), 1), sz.width)
-    length = jnp.zeros((1, LANES), jnp.int32)
+    lengths = []
+    far_length = jnp.zeros((1, LANES), jnp.int32)
     count = jnp.zeros((), jnp.int32)
     for s in range(sz.segs):
         held = jnp.where(s < count_ref[0], len_ref[s], 0)
-        length = jnp.where(lane_seg == s, held, length)
+        far_length = jnp.where(lane_seg == s, held, far_length)
         count = count + jnp.clip(held - tile_pos * sz.rows, 0, sz.rows)
-    count = (count * sz.width).astype(F32)
-    masks = [(tile_pos * sz.rows + t < length).astype(F32) for t in range(sz.rows)]
+    count = jnp.full((1, LANES), (count * sz.width).astype(F32))
+    masks = [(tile_pos * sz.rows + t < far_length).astype(F32) for t in range(sz.rows)]
+    far_info[...] = jnp.zeros(far_info.shape, F32)
+    for t in range(sz.rows):
+        far_info[t : t + 1] = masks[t]
+    first = tile_pos * sz.own
+    _, slot, block = lane_at(sz)
+    length = jnp.zeros((1, LANES), jnp.int32)
+    own_count = jnp.zeros((), jnp.int32)
+    at = iota((8, LANES), 0)
+    frames = jnp.ones((8, LANES), F32)
+    for s in range(sz.own):
+        held = jnp.where(first + s < count_ref[0], len_ref[first + s], 0)
+        length = jnp.where(slot == s, held, length)
+        own_count = own_count + jnp.minimum(held, sz.rows * sz.tiles)
+        frame = jnp.maximum((held * sz.width).astype(F32), 1.0)
+        frames = jnp.where(at == s, frame, frames)
+    info_ref[...] = jnp.zeros(info_ref.shape, F32)
+    for t in range(sz.rows):
+        info_ref[t : t + 1] = (block * sz.rows + t < length).astype(F32)
+    info_ref[7:8] = jnp.full((1, LANES), (own_count * sz.width).astype(F32))
+    info_ref[8:16] = frames
+    unit = eye(sz.chans, sz.chans, BF16)
+    for copy in copies[2:]:
+        copy.wait()
     weights = w_ref[...]
-    for copy in copies[3:]:
-        copy.wait()
-    unit = eye(sz.chans, sz.chans, BF16)
     cells = [dot(unit, x_ref[:, t].reshape(LANES, sz.chans), 1, 1) for t in range(sz.rows)]
-    total = 0.0
-    for t in range(sz.rows):
-        total = total + cells[t] * masks[t]
-    x_row = padded_rows([row_sums(total)], 16)
-    wide_sum = dot(jnp.concatenate(thirds(x_row), axis=0), weights, 1, 0)
-    wide_sum = wide_sum[0:1] + wide_sum[16:17] + wide_sum[32:33]
-    mean_val = lane_sum(total) / jnp.maximum(count, 1.0)
-    centred = [(cells[t] - mean_val) * masks[t] for t in range(sz.rows)]
-    centred = jnp.concatenate(centred, axis=1)
-    spare = dot(centred, centred, 1, 1, True)
+    centre = cells[0][:, 0:1]
+    cells = jnp.concatenate([(cells[t] - centre) * masks[t] for t in range(sz.rows)], axis=1)
+    high = cells.astype(BF16)
+    low = (cells - high.astype(F32)).astype(BF16)
+    left = jnp.concatenate([high, low, high, low], axis=1)
+    right = jnp.concatenate([high, high, low, low], axis=1)
+    ones = jnp.ones((sz.chans, left.shape[1]), BF16)
+    second = dot(left, right, 1, 1)
+    halves = jnp.concatenate([high, low], axis=1)
+    ones = ones[:, : halves.shape[1]]
+    across = dot(ones, halves, 1, 1)
+    down = dot(halves, ones, 1, 1)
+    divided = jnp.maximum(count[:, : sz.chans], 1.0)
+    spare = second - down * (across / divided)
     wide = sum(dot(held, weights, 1, 0) for held in thirds(spare))
     square = jnp.sum(wide * weights.astype(F32), axis=0, keepdims=True)
-    last = jnp.full((1, LANES), count, F32)
-    send_block(pay_ref, wide_rows(wide_sum, square, sz.wide - LANES, last))
+    total = down + centre * count[:, : sz.chans]
+    wide_sum = jnp.concatenate([total[:, 0:1]] * 8, axis=1)
+    wide_sum = dot(wide_sum, weights.astype(F32), 0, 0, True)[0:1]
+    send_block(pay_ref, wide_rows(wide_sum, square, sz.wide - LANES, count))
 
 
 def send_kernel(sz, x_ref, c_ref, after_ref, *out_refs):
@@ -323,12 +365,15 @@
 
 
 def setup_kernel(sz, *refs):
-    wide_refs, small_refs, dw_ref, rw_ref, sw_ref, pw_in, w_in, len_ref, count_ref = (
+    wide_refs, small_refs, dw_ref, rw_ref, sw_ref, pw_in, w_in = (
         refs[0:5],
         refs[5:8],
-        *refs[8:15],
-    )
-    par_ref, tap_ref, unit_ref, info_ref, pw_ref, pwt_ref, w_ref, wt_ref, far_info = refs[15:]
+        *refs[8:13],
+    )
+    info_in, far_in, par_ref, tap_ref, unit_ref, pw_ref, pwt_ref, w_ref, wt_ref = refs[13:22]
+    info_ref, far_info = refs[22:]
+    info_ref[...] = info_in[...]
+    far_info[...] = far_in[...]
     par_ref[...] = jnp.zeros(par_ref.shape, F32)
     for at, ref in enumerate(wide_refs):
         par_ref[at : at + 1] = vector(ref)
@@ -347,60 +392,43 @@
         part = slice(at * 2 * LANES, (at + 1) * 2 * LANES)
         unit_ref[0:LANES, part] = unit
         unit_ref[LANES:, part] = unit
-    first = lax.axis_index("tile") * sz.own
-    _, slot, block = lane_at(sz)
-    length = jnp.zeros((1, LANES), jnp.int32)
-    count = jnp.zeros((), jnp.int32)
-    at = iota((8, LANES), 0)
-    frames = jnp.ones((8, LANES), F32)
-    for s in range(sz.own):
-        held = jnp.where(first + s < count_ref[0], len_ref[first + s], 0)
-        length = jnp.where(slot == s, held, length)
-        count = count + jnp.minimum(held, sz.rows * sz.tiles)
-        frame = jnp.maximum((held * sz.width).astype(F32), 1.0)
-        frames = jnp.where(at == s, frame, frames)
-    for t in range(sz.rows):
-        info_ref[t : t + 1] = (block * sz.rows + t < length).astype(F32)
-    info_ref[7:8] = jnp.full((1, LANES), (count * sz.width).astype(F32))
-    info_ref[8:16] = frames
-    lane_seg = lax.div(iota((1, LANES), 1), sz.width)
-    length = jnp.zeros((1, LANES), jnp.int32)
-    for s in range(sz.segs):
-        held = jnp.where(s < count_ref[0], len_ref[s], 0)
-        length = jnp.where(lane_seg == s, held, length)
-    far_info[...] = jnp.zeros(far_info.shape, F32)
-    first = lax.axis_index("tile") * sz.rows
-    for t in range(sz.rows):
-        far_info[t : t + 1] = (first + t < length).astype(F32)
-
-
-def stage_one_kernel(sz, pay_ref, *refs):
+
+
+def moment_kernel(sz, pay_ref, par_ref, row_ref, wide_ref):
+    mean0, inv0, total = wide_moments(sz, pay_ref, sz.wide - LANES)
+    row_ref[0:1] = mean0
+    row_ref[1:2] = inv0
+    row_ref[2:3] = total
+    for at, held in enumerate(spread_rows([mean0, inv0 * par_ref[0:1], par_ref[1:2]])):
+        wide_ref[at] = held
+
+
+def stage_one_kernel(sz, wide_ref, *refs):
     own_refs = refs[: sz.tiles]
-    wt_ref, par_ref, tap_ref, unit_ref, info_ref = refs[sz.tiles : sz.tiles + 5]
-    refs = refs[sz.tiles + 5 :]
-    out_pay, xc_ref, act0_ref, deep_ref, ec_ref, s0_ref, row_ref, near_ref, part_ref = refs[:9]
-    mat_ref, acc_ref, sh_ref, buf_ref, all_ref = refs[9:]
+    wt_ref, tap_ref, unit_ref, info_ref = refs[sz.tiles : sz.tiles + 4]
+    refs = refs[sz.tiles + 4 :]
+    out_pay, xc_ref, pix_ref, act0_ref, deep_ref, ec_ref, s0_ref, near_ref, part_ref = refs[:9]
+    mat_ref, acc_ref, sh_ref, buf_ref = refs[9:]
+    chans = sz.chans
+    half = sz.wide - LANES
+    size = sz.own * sz.width
     for step, ref in enumerate(own_refs):
-        all_ref[partner(step)] = ref[...]
+        source = partner(step)
+        for g in range(sz.rows // 2):
+            pix_ref[g, source] = ref[:, g].reshape(size, LANES)
     unit = eye(LANES, LANES, BF16)
     expanded = []
     for g in range(sz.rows // 2):
-        flat = dot(unit, all_ref[:, :, g].reshape(LANES, LANES), 1, 1)
+        flat = dot(unit, pix_ref[g].reshape(LANES, LANES), 1, 1)
         for par in range(2):
-            at = par * 2 * sz.chans
-            xc_ref[2 * g + par] = flat[at : at + 2 * sz.chans].astype(BF16)
-            cells = flat[at : at + sz.chans].astype(BF16)
+            at = par * 2 * chans
+            xc_ref[2 * g + par] = flat[at : at + 2 * chans].astype(BF16)
+            cells = flat[at : at + chans].astype(BF16)
             expanded.append(dot(wt_ref[...], cells, 1, 0))
-    chans = sz.chans
-    half = sz.wide - LANES
-    mean0, inv0, total = wide_moments(sz, pay_ref, half)
-    row_ref[0:1] = mean0
-    row_ref[1:2] = inv0
-    row_ref[2:3] = total
     info = info_ref[...]
     masks = mask_rows(sz, info)
     count = info[7:8]
-    mean_c, slope_c, bias_c = spread_rows([mean0, inv0 * par_ref[0:1], par_ref[1:2]])
+    mean_c, slope_c, bias_c = (wide_ref[at] for at in range(3))
     acts = []
     squares = 0.0
     for t in range(sz.rows):
@@ -431,15 +459,19 @@
         acts = [half_of(act0_ref, t, e) for t in range(sz.rows)]
         sums = 0.0
         edged = [taps[3 * i] * right + taps[3 * i + 1] + taps[3 * i + 2] * left for i in range(3)]
+        deep = [0.0] * sz.rows
+        for j in range(3):
+            for at in range(sz.rows + 2):
+                field = sh_ref[j, at, part]
+                for i in range(3):
+                    if 0 <= at - i < sz.rows:
+                        deep[at - i] = deep[at - i] + field * taps[3 * i + j]
         for t in range(sz.rows):
-            deep = 0.0
             back = 0.0
             for i in range(3):
                 back = back + full[t + 2 - i] * edged[i]
-                for j in range(3):
-                    deep = deep + sh_ref[j, t + i, part] * taps[3 * i + j]
-            deep_ref[t, part] = deep
-            sums = sums + deep * masks[t]
+            deep_ref[t, part] = deep[t]
+            sums = sums + deep[t] * masks[t]
             mat_ref[t, part] = back * s0_ref[t, part]
         total_sum.append(sums)
         for i in range(3):
@@ -455,16 +487,12 @@
         square = square + centred * centred
     send_block(out_pay, wide_rows(row_sums(total_sum), row_sums(square), half, count))
     part_ref[...] = placed_sums(acc_ref, 9, 3 * chans + 9)
-    held = jnp.zeros((sz.wide, LANES), F32)
-    second = jnp.zeros((chans, chans), F32)
-    x_sum = 0.0
-    for t in range(sz.rows):
-        x_at = xc_ref[t].astype(F32)[:chans]
-        cells = placed_cells(x_at, 0)
-        held = held + dot(doubled(mat_ref[t]), jnp.concatenate([cells, cells], axis=1), 1, 1)
-        kept = x_at * masks[t]
-        second = second + dot(kept.astype(BF16), x_at.astype(BF16), 1, 1)
-        x_sum = x_sum + kept
+    even, odd = pixel_product([mat_ref[t] for t in range(sz.rows)], pix_ref)
+    held = even + pltpu.roll(odd, LANES - 2 * chans, 1)
+    cells = [xc_ref[t].astype(F32)[:chans] * masks[t] for t in range(sz.rows)]
+    x_sum = sum(cells)
+    even, odd = pixel_product([cell.astype(BF16) for cell in cells], pix_ref)
+    second = even[:, :chans] + odd[:, 2 * chans : 3 * chans]
     near_ref[...] = jnp.zeros(near_ref.shape, F32)
     buf_ref[...] = held
     for k in range(5):
@@ -485,6 +513,7 @@
     pay_ref,
     deep_ref,
     xc_ref,
+    pix_ref,
     par_ref,
     tap_ref,
     unit_ref,
@@ -535,7 +564,7 @@
     pooled = seg_sums(sz, pool) / info[8:16, 0:1]
     rw = par_ref[8:16]
     sw = par_ref[16:24]
-    squeeze_pre = dot(pooled, rw, 1, 1, True) + par_ref[7:8, 0:8]
+    squeeze_pre = fine_dot(pooled, rw) + par_ref[7:8, 0:8]
     squeezed = squeeze_pre * sigmoid(squeeze_pre)
     gate = sigmoid(dot(squeezed, sw, 1, 0, True) + par_ref[4:5])
     seg_ref[0] = pooled
@@ -575,11 +604,11 @@
         back = backward_parts(sz, sh_ref, tap_ref, part, acts, acc_ref)
         for t in range(sz.rows):
             mat_ref[t, part] = back[t] * s0_ref[t, part]
-    buf = part_ref[...] + placed_sums(acc_ref, 9, 3 * chans + 18)
-    for t in range(sz.rows):
-        cells = placed_cells(xc_ref[t].astype(F32)[:chans], chans)
-        buf = buf + dot(doubled(mat_ref[t]), jnp.concatenate([cells, cells], axis=1), 1, 1)
-    buf_ref[...] = buf
+    even, odd = pixel_product([mat_ref[t] for t in range(sz.rows)], pix_ref)
+    lane = iota((1, LANES), 1)
+    held = pltpu.roll(even, 2 * chans, 1) + odd
+    held = jnp.where((lane >= 2 * chans) & (lane < 3 * chans), held, 0.0)
+    buf_ref[...] = part_ref[...] + placed_sums(acc_ref, 9, 3 * chans + 18) + held
 
 
 def stage_three_kernel(
@@ -587,6 +616,7 @@
     pay_ref,
     proj_ref,
     xc_ref,
+    pix_ref,
     act0_ref,
     act1_ref,
     s0_ref,
@@ -621,13 +651,13 @@
     near = every(sz, pay_ref, 1, 2)
     sums = jnp.sum(parts, axis=0, keepdims=True)
     counts = pltpu.roll(parts, LANES - 4 * chans, 1)
-    grads = pltpu.roll(parts, LANES - 2 * chans, 1)
+    shares = pltpu.roll(parts, LANES - 2 * chans, 1)
     total = sums[:, 4 * chans : 4 * chans + 1]
     mean_row = sums / total
     offset = parts - counts * mean_row
     scaled = offset / jnp.maximum(counts, 1.0)
     spare = jnp.sum(offset * scaled, axis=0, keepdims=True)
-    cross = jnp.sum(scaled * grads, axis=0, keepdims=True)
+    cross = jnp.sum(scaled * shares, axis=0, keepdims=True)
     square = sums[:, chans : 2 * chans] + spare[:, :chans]
     inv2 = lax.rsqrt(square / total + EPSILON)
     bias_grad = sums[:, 2 * chans : 3 * chans]
@@ -645,7 +675,8 @@
     branch_sq = 0.0
     result_sq = 0.0
     gate_sum = 0.0
-    buf = part_ref[...]
+    gated = []
+    grads = []
     for t in range(sz.rows):
         both = xc_ref[t].astype(F32)
         normed = (proj_ref[t] - mean_c) * inv_c
@@ -659,8 +690,9 @@
         ga_ref[t] = wide_grad
         act = act1_ref[t]
         gate_sum = gate_sum + wide_grad * act
-        act = (act * gate_wide).astype(BF16)
-        buf = buf + dot(act, placed_cells(grad, 2 * chans), 1, 1)
+        gated.append((act * gate_wide).astype(BF16))
+        grads.append(grad.astype(BF16))
+    grads = dot(jnp.concatenate(gated, axis=1), jnp.concatenate(grads, axis=1), 1, 1)
     rw = par_ref[8:16]
     sw = par_ref[16:24]
     pooled = seg_ref[0]
@@ -671,7 +703,7 @@
     slope = slope + squeezed * (1.0 - slope)
     live = (iota((8, 1), 0) < sz.own).astype(F32)
     gate_pre = seg_sums(sz, gate_sum) * gate * (1.0 - gate)
-    squeeze_grad = dot(gate_pre, sw, 1, 1, True) * slope * live
+    squeeze_grad = fine_dot(gate_pre, sw) * slope * live
     back = dot(squeeze_grad, rw, 1, 0, True) / info[8:16, 0:1]
     back_wide = seg_spread(sz, back)
     (scale_c,) = spread_rows([row_ref[1:2] * par_ref[2:3]])
@@ -693,10 +725,10 @@
         back = backward_parts(sz, sh_ref, tap_ref, part, acts, acc_ref)
         for t in range(sz.rows):
             mat_ref[t, part] = back[t] * s0_ref[t, part]
-    buf = buf + placed_sums(acc_ref, 9, 3 * chans)
-    for t in range(sz.rows):
-        cells = placed_cells(xc_ref[t].astype(F32)[:chans], 0)
-        buf = buf + dot(doubled(mat_ref[t]), jnp.concatenate([cells, cells], axis=1), 1, 1)
+    even, odd = pixel_product([mat_ref[t] for t in range(sz.rows)], pix_ref)
+    held = even + pltpu.roll(odd, LANES - 2 * chans, 1)
+    held = jnp.where(iota((1, LANES), 1) < chans, held, 0.0)
+    buf = part_ref[...] + placed_sums(acc_ref, 9, 3 * chans) + held
     at = 3 * chans + 27
     small = [dot(squeezed, gate_pre, 0, 0, True)[: sz.squeeze]]
     small.append(dot(squeeze_grad, pooled, 0, 0, True)[: sz.squeeze])
@@ -704,6 +736,7 @@
     shape = (16, LANES)
     unit = jnp.where(iota(shape, 0) + at == iota(shape, 1), 1.0, 0.0).astype(BF16)
     buf_ref[...] = buf + spread_by(padded_rows(small, 16), unit)
+    buf_ref[:, chans : 2 * chans] = grads
     at = at + 2 * sz.squeeze + 1
     spots = iota((8, 1), 0)
     held = jnp.sum(squeeze_grad, axis=0, keepdims=True)
@@ -795,14 +828,16 @@
         out_ref[...] = all_ref[partner(step)]
 
 
-def far_parts(sz, pay_ref, row0_ref, weights, buf_ref, near_ref):
+def far_kernel(sz, pay_ref, x_ref, far_info, row0_ref, w_ref, after_ref, *refs):
+    del after_ref
+    two_ref, wide_ref, misc_ref, live_ref, buf_ref, near_ref = refs
     chans = sz.chans
     near_ref[...] = every(sz, pay_ref, 3, 8)[0:32]
     buf_ref[...] = jnp.zeros(buf_ref.shape, F32)
     for k in range(5):
         rows = min(32, sz.wide - 32 * k)
         buf_ref[32 * k : 32 * k + rows, 0:chans] = near_ref[0:rows, chans * k : chans * (k + 1)]
-    two = picked_rows(buf_ref[...], chans)
+    two_ref[...] = picked_rows(buf_ref[...], chans)
     x_row = [near_ref[chans + k : chans + k + 1, 5 * chans : LANES] for k in range(3)]
     x_row = jnp.concatenate(x_row, axis=1)
     x_column = columns_of([x_row])[:, 0:1]
@@ -810,9 +845,21 @@
     below = jnp.concatenate([right.T[0:8, 0:16], right[16:chans]], axis=1)
     second = jnp.concatenate([near_ref[16:32, 4 * chans : 5 * chans], below], axis=0)
     second = second - x_column * x_row / row0_ref[2:3, :chans]
-    wide = dot(second, weights, 1, 0, True) * row0_ref[1:2]
+    wide_ref[...] = dot(second, w_ref[...].astype(F32), 1, 0, True) * row0_ref[1:2]
+    misc_ref[0:chans] = spread(x_column)
     spot = chans + 3
-    return two, wide, x_column, near_ref[spot : spot + 1, 5 * chans : 5 * chans + 1]
+    misc_ref[chans : chans + 8] = jnp.broadcast_to(
+        near_ref[spot : spot + 1, 5 * chans : 5 * chans + 1], (8, LANES)
+    )
+    shape = (16, sz.rows * LANES)
+    unit = jnp.where(iota(shape, 0) == lax.div(iota(shape, 1), LANES), 1.0, 0.0).astype(BF16)
+    live = dot(far_info[...].astype(BF16), unit, 0, 0)
+    lane = iota((1, 32), 1)
+    for t in range(sz.rows):
+        held = live[:, t * LANES : t * LANES + 32]
+        cells = x_ref[:, t].reshape(sz.segs * sz.width, chans).astype(F32)
+        cells = jnp.concatenate([cells, jnp.ones((LANES, 32 - chans), F32)], axis=1)
+        live_ref[t] = (jnp.where(lane <= chans, cells, 0.0) * held).astype(BF16)
 
 
 def picked_rows(columns, count):
@@ -820,13 +867,13 @@
     return dot(jnp.concatenate([unit] * 3, axis=1), tripled(columns), 1, 1)[0:count]
 
 
-def last_kernel(
+def weights_kernel(
     sz,
     pay_ref,
-    far_pay,
-    x_ref,
-    c_ref,
-    far_info,
+    two_ref,
+    wide_ref,
+    misc_ref,
+    live_ref,
     row0_ref,
     row1_ref,
     mid_ref,
@@ -834,11 +881,8 @@
     w_ref,
     *refs,
 ):
-    got_refs = refs[: sz.tiles]
-    out_ref, xg_ref, ew_ref, gg0_ref, bg0_ref, dw_ref, rw_ref, rb_ref = refs[
-        sz.tiles : sz.tiles + 8
-    ]
-    sw_ref, sb_ref, pw_ref, rms_ref, buf_ref, near_ref, corr_ref = refs[sz.tiles + 8 :]
+    ew_ref, gg0_ref, bg0_ref, dw_ref, rw_ref, rb_ref, sw_ref, sb_ref, pw_ref, rms_ref = refs[:10]
+    corr_ref, buf_ref = refs[10:]
     chans = sz.chans
     half = sz.wide - LANES
     each = LANES // sz.devices
@@ -857,15 +901,57 @@
     matrix = dot(weights * factor, weights, 1, 1, True)
     offset = jnp.broadcast_to(scale0 * bias_row - factor * mean0, (8, sz.wide))
     offset = dot(offset, weights, 1, 1, True)[0:1]
+    matrix = jnp.concatenate([matrix, offset, jnp.zeros((32 - chans - 1, chans), F32)], axis=0)
     high = matrix.astype(BF16)
     low = (matrix - high.astype(F32)).astype(BF16)
-    shape = (16, sz.rows * LANES)
-    unit = jnp.where(iota(shape, 0) == lax.div(iota(shape, 1), LANES), 1.0, 0.0).astype(BF16)
-    live = dot(far_info[...].astype(BF16), unit, 0, 0)
     for t in range(sz.rows):
-        cells = x_ref[:, t].reshape(sz.segs * sz.width, chans)
-        back = dot(cells, high, 1, 0) + dot(cells, low, 1, 0) + offset
-        corr_ref[t] = back * live[:, t * LANES : t * LANES + chans]
+        cells = live_ref[t]
+        corr_ref[t] = dot(cells, high, 1, 0) + dot(cells, low, 1, 0)
+    used = 3 * chans + 29 + 2 * sz.squeeze
+    piece = LANES - used
+    for k in range(each):
+        buf_ref[pl.ds(k, sz.devices, stride=each), :] = every(sz, pay_ref, 4 + k, 8)
+    buf_ref[LANES:] = jnp.zeros((half, LANES), F32)
+    for k in range(-(-used // piece)):
+        take = min(piece, used - k * piece)
+        buf_ref[LANES : LANES + half, k * piece : k * piece + take] = buf_ref[
+            k * half : (k + 1) * half, used : used + take
+        ]
+    rows = picked_rows(buf_ref[...], LANES)
+    inv1 = row1_ref[1:2]
+    scale1 = inv1 * par_ref[2:3]
+    bias1 = mid_ref[0:1] / total
+    gain1 = mid_ref[1:2] * inv1 / total
+    inner = rows[0:chans] - two_ref[...] * bias1 - rows[2 * chans : 3 * chans] * gain1
+    x_sum = misc_ref[0:chans, 0:1]
+    ew_ref[...] = scale0 * (scale1 * inner - x_sum * bias_row - wide_ref[...] * gain_row)
+    pw_ref[...] = rows[chans : 2 * chans]
+    spot = 3 * chans
+    held = rows[spot : spot + 9] - rows[spot + 9 : spot + 18] * bias1
+    held = scale1 * (held - rows[spot + 18 : spot + 27] * gain1)
+    for i in range(3):
+        dw_ref[i] = held[3 * i : 3 * i + 3]
+    spot = spot + 27
+    sw_ref[...] = rows[spot : spot + sz.squeeze]
+    spot = spot + sz.squeeze
+    rw_ref[...] = rows[spot : spot + sz.squeeze]
+    spot = spot + sz.squeeze
+    sb_ref[...] = rows[spot : spot + 1].reshape(sz.wide)
+    misc = rows[spot + 1 : spot + 2]
+    rb_ref[...] = misc[:, : sz.squeeze].reshape(sz.squeeze)
+    squares = jnp.concatenate(
+        [misc[:, 8:9], misc_ref[chans : chans + 1, 0:1], misc[:, 9:10], misc[:, 10:11], misc[:, 11:12]], axis=1
+    )
+    chan_row = jnp.where(
+        (iota((1, 5), 1) == 0) | (iota((1, 5), 1) == 4), float(chans), float(sz.wide)
+    )
+    rms_ref[...] = jnp.sqrt(squares / (total[:, :5] * chan_row)).reshape(5)
+
+
+def return_kernel(sz, c_ref, corr_ref, *refs):
+    got_refs = refs[: sz.tiles]
+    out_ref, xg_ref = refs[sz.tiles :]
+    chans = sz.chans
     shape = (LANES, 4 * LANES)
     column = iota(shape, 1)
     spot = lax.rem(column, LANES)
@@ -886,45 +972,6 @@
                 held = cells[:, at : at + chans] - corr_ref[t, pl.ds(first * sz.width, size)]
                 held = held.reshape(shape) + c_ref[pl.ds(first, sz.own), t].astype(F32)
                 xg_ref[pl.ds(first, sz.own), t] = held.astype(BF16)
-    two, wide, x_sum, act0_sq = far_parts(sz, far_pay, row0_ref, weights, buf_ref, near_ref)
-    used = 3 * chans + 29 + 2 * sz.squeeze
-    piece = LANES - used
-    for k in range(each):
-        buf_ref[pl.ds(k, sz.devices, stride=each), :] = every(sz, pay_ref, 4 + k, 8)
-    buf_ref[LANES:] = jnp.zeros((half, LANES), F32)
-    for k in range(-(-used // piece)):
-        take = min(piece, used - k * piece)
-        buf_ref[LANES : LANES + half, k * piece : k * piece + take] = buf_ref[
-            k * half : (k + 1) * half, used : used + take
-        ]
-    rows = picked_rows(buf_ref[...], LANES)
-    inv1 = row1_ref[1:2]
-    scale1 = inv1 * par_ref[2:3]
-    bias1 = mid_ref[0:1] / total
-    gain1 = mid_ref[1:2] * inv1 / total
-    inner = rows[0:chans] - two * bias1 - rows[chans : 2 * chans] * gain1
-    ew_ref[...] = scale0 * (scale1 * inner - x_sum * bias_row - wide * gain_row)
-    pw_ref[...] = rows[2 * chans : 3 * chans]
-    spot = 3 * chans
-    held = rows[spot : spot + 9] - rows[spot + 9 : spot + 18] * bias1
-    held = scale1 * (held - rows[spot + 18 : spot + 27] * gain1)
-    for i in range(3):
-        dw_ref[i] = held[3 * i : 3 * i + 3]
-    spot = spot + 27
-    sw_ref[...] = rows[spot : spot + sz.squeeze]
-    spot = spot + sz.squeeze
-    rw_ref[...] = rows[spot : spot + sz.squeeze]
-    spot = spot + sz.squeeze
-    sb_ref[...] = rows[spot : spot + 1].reshape(sz.wide)
-    misc = rows[spot + 1 : spot + 2]
-    rb_ref[...] = misc[:, : sz.squeeze].reshape(sz.squeeze)
-    squares = jnp.concatenate(
-        [misc[:, 8:9], act0_sq, misc[:, 9:10], misc[:, 10:11], misc[:, 11:12]], axis=1
-    )
-    chan_row = jnp.where(
-        (iota((1, 5), 1) == 0) | (iota((1, 5), 1) == 4), float(chans), float(sz.wide)
-    )
-    rms_ref[...] = jnp.sqrt(squares / (total[:, :5] * chan_row)).reshape(5)
 
 
 def call(kernel, sz, args, kinds, outs, scratch=(), cost=1.0, room=16):
@@ -993,56 +1040,59 @@
     def pay_of(count):
         return ((devices * count, LANES), F32)
 
-    (pay,) = call(
+    pay, info, far_info = call(
         entry_kernel,
         sz,
         [x_input, expand_w, seg_len, seg_count],
         "hhhh",
-        [pay_of(4)],
+        [pay_of(4), ((16, LANES), F32), ((16, LANES), F32)],
         [
             (x_input.shape, BF16),
             (expand_w.shape, BF16),
             pltpu.SMEM(seg_len.shape, jnp.int32),
             pltpu.SMEM(seg_count.shape, jnp.int32),
-            pltpu.SemaphoreType.DMA((3 + segs,)),
+            pltpu.SemaphoreType.DMA((4,)),
         ],
         room=60,
     )
-    parts = call(send_kernel, sz, [x_input, cotangent, pay], "vva", [block] * tiles)
-    par, tap, unit, info, pw_near, pw_turned, w_near, w_turned, far_info = call(
+    parts = call(send_kernel, sz, [x_input, cotangent, pay], "vvh", [block] * tiles)
+    par, tap, unit, pw_near, pw_turned, w_near, w_turned, info, far_info = call(
         setup_kernel,
         sz,
         [gain0, bias0, gain1, bias1, restore_b, gain2, bias2, reduce_b, dw_kernel, reduce_w.T]
-        + [restore_w, project_w.T, expand_w, seg_len, seg_count],
-        "v" * 13 + "ss",
+        + [restore_w, project_w.T, expand_w, info, far_info],
+        "",
         [
             ((24, wide), F32),
             taps,
             ((2 * LANES, 4 * LANES), BF16),
-            ((16, LANES), F32),
             ((chans, wide), BF16),
             ((wide, chans), BF16),
             ((chans, wide), BF16),
             ((wide, chans), BF16),
             ((16, LANES), F32),
+            ((16, LANES), F32),
         ],
     )
     pay = everywhere(pay)
     parts = passed(sz, parts)
-    pay, x_c, act0, deep, ec, s0, row0, near, part = call(
+    row0, wide0 = call(
+        moment_kernel, sz, [pay, par], "", [((3, wide), F32), ((3, wide, LANES), F32)]
+    )
+    pay, x_c, pix, act0, deep, ec, s0, near, part = call(
         stage_one_kernel,
         sz,
-        [pay] + parts + [w_turned, par, tap, unit, info],
+        [wide0] + parts + [w_turned, tap, unit, info],
         "",
-        [pay_of(4), both, packed, big, big, big, ((3, wide), F32)]
+        [pay_of(4), both, ((rows // 2, tiles, own * width, LANES), BF16), packed, big, big, big]
         + [((max(32, devices), LANES), F32), column],
-        [big, taps, shifts, column, ((tiles,) + block[0], BF16)],
+        [big, taps, shifts, column],
     )
     pay = everywhere(pay)
     pay, act1, dc, s1, proj, gate, seg_rows, row1, part, squares = call(
         stage_two_kernel,
         sz,
-        [pay, deep, x_c, par, tap, unit, info, pw_near, near, act0, s0, part],
+        [pay, deep, x_c, pix, par, tap, unit, info, pw_near, near, act0, s0, part],
         "",
         [pay_of(2), big, big, big, small, column, ((3, 8, wide), F32), ((2, wide), F32)]
         + [column, ((16, LANES), F32)],
@@ -1052,7 +1102,7 @@
     pay, res, scaled, bg2, gg2 = call(
         stage_three_kernel,
         sz,
-        [pay, proj, x_c, act0, act1, s0, dc, s1, gate, seg_rows, par, tap, unit, info]
+        [pay, proj, x_c, pix, act0, act1, s0, dc, s1, gate, seg_rows, par, tap, unit, info]
         + [pw_turned, part, squares, row1],
         "",
         [pay_of(8), small, big, ((chans,), F32), ((chans,), F32)],
@@ -1077,14 +1127,21 @@
     )
     pay = everywhere(pay)
     sent = passed(sz, sent)
-    block_out, x_grad, ew, gg0, bg0, dw, rw, rb, sw, sb, pw, rms = call(
-        last_kernel,
+    far = call(
+        far_kernel,
         sz,
-        [pay, far_pay, x_input, cotangent, far_info, row0, row1, mid, par, w_near] + sent,
+        [far_pay, x_input, far_info, row0, w_near, gp0],
+        "vvvvva",
+        [((chans, wide), F32), ((chans, wide), F32), ((chans + 8, LANES), F32)]
+        + [((rows, LANES, 32), BF16)],
+        [column, ((32, LANES), F32)],
+    )
+    ew, gg0, bg0, dw, rw, rb, sw, sb, pw, rms, corr = call(
+        weights_kernel,
+        sz,
+        [pay] + list(far) + [row0, row1, mid, par, w_near],
         "",
         [
-            (x_input.shape, BF16),
-            (x_input.shape, BF16),
             ((chans, wide), F32),
             ((wide,), F32),
             ((wide,), F32),
@@ -1095,8 +1152,16 @@
             ((wide,), F32),
             ((chans, wide), F32),
             ((5,), F32),
+            ((rows, LANES, chans), F32),
         ],
-        [column, ((32, LANES), F32), ((rows, LANES, chans), F32)],
+        [column],
+    )
+    block_out, x_grad = call(
+        return_kernel,
+        sz,
+        [cotangent, corr] + sent,
+        "",
+        [(x_input.shape, BF16), (x_input.shape, BF16)],
     )
     return (
         block_out,

time: 71.7 us -> 71.8 us (level)
    ppermute x6, waiting for transfers between devices: 5.29 us -> 0.02 us  [passed(): result[step] = lax.ppermute(parts[step], 'tile', pairs)]
    all_to_all x2, waiting for transfers between devices: 3.95 us -> 9.15 us  [everywhere(): return lax.all_to_all(values, BOTH, 0, 0, tiled=True)]
    pallas_call x9 -> x12, Pallas kernels: 16.8 us -> 17.4 us  [call(): pl.pallas_call(functools.partial(kernel, sz), out_shape=tuple((jax.ShapeD...]
  transfers between devices with their start and end apart: 8 -> 8, of which waited for: 6 -> 2; matrix products, arithmetic and copies ran while one was open for 0% -> 0% of each run, Pallas kernels for 2% -> 5%
where the time goes in v3:
time: 71.8 us; the launch traced here: 71.5 us
  blocking collectives  28.8 us (40%)
  Pallas kernels  17.4 us (24%)
  starting transfers between devices  13.8 us (19%)
  waiting for transfers between devices  9.17 us (13%)
  between operations  1.64 us (2%)
    all_to_all x3, blocking collectives, everywhere(): return lax.all_to_all(values, BOTH, 0, 0, tiled=True)  28.8 us
    pallas_call x12, Pallas kernels, call(): pl.pallas_call(functools.partial(kernel, sz), out_shape=tuple((jax.ShapeD...  17.4 us
    all_to_all x2, starting transfers between devices, everywhere(): return lax.all_to_all(values, BOTH, 0, 0, tiled=True)  9.88 us
    all_to_all x2, waiting for transfers between devices, everywhere(): return lax.all_to_all(values, BOTH, 0, 0, tiled=True)  9.15 us
    ppermute x6, starting transfers between devices, passed(): result[step] = lax.ppermute(parts[step], 'tile', pairs)  3.96 us
  transfers between devices with their start and end apart: 8, of which 2 were waited for; matrix products, arithmetic and copies ran while one was open for 0% of the time, Pallas kernels for 5%

profile of v3, /device:TPU:0, one launch (start us, length us, event | category | flops | bytes accessed | tf_op | source)
XLA Modules:
  0.0 71.5 jit_solution(396230379859920883)
XLA Ops:
  1.3 0.0 copy-start.1
  1.3 0.0 copy-start.2
  1.3 2.4 %entry_kernel.1 = (f32[128,128]{1,0:T(8,128)}, f32[16,128]{1,0:T(8,128)}, f32[16,128]{1,0:T(8,128)}) custom-call(bf16[8,6,16,24]{3,2,1,0:T(8,128)(2,1)} %x_ref.3, bf16[24,144]{1,0:T(8,128)(2,1)} %refs_12_.1, s32[8]{0:T(128)} %len_hbm.1, s32[1]{0:T(128)S(6)} %copy.33.count_hbm), custom_call_target="tpu_custom_call" | custom-call | flops 1000000000 | bytes 3000000 | tf_op jit(solution)/shard_map/entry_kernel/pallas_call | solution.py:980
  3.8 0.0 copy-start
  3.8 7.3 %all-to-all-start = ((f32[32,4,128]{2,1,0:T(4,128)}), f32[32,4,128]{2,1,0:T(4,128)S(1)}, u32[]{:S(2)}, u32[]{:S(2)}) async-start(f32[32,4,128]{2,1,0:T(4,128)} %bitcast.19), calls=%async_computation | async-start | bytes 131072 | tf_op jit(solution)/shard_map/all_to_all | solution.py:995
  11.1 0.0 copy-start.4
  11.1 0.0 copy-start.5
  11.1 0.0 copy-start.6
  11.1 0.0 copy-start.7
  11.2 0.0 copy-start.9
  11.2 0.0 copy-start.10
  11.2 0.0 copy-start.11
  11.2 0.0 copy-start.12
  11.2 0.0 copy-start.13
  11.2 0.0 copy-start.14
  11.2 0.0 copy-start.15
  11.2 0.0 copy-start.16
  11.3 0.0 copy-start.17
  11.3 0.2 send_kernel.1
  11.5 0.3 collective-permute-start
  11.8 1.7 %collective-permute-start.1 = (bf16[2,3,16,128]{3,2,1,0:T(8,128)(2,1)S(1)}, bf16[2,3,16,128]{3,2,1,0:T(8,128)(2,1)S(1)}, u32[]{:S(2)}, u32[]{:S(2)}) collective-permute-start(bf16[2,3,16,128]{3,2,1,0:T(8,128)(2,1)S(1)} %get-tuple-element.91), channel_id=1, source_target_pairs={{0,2},{1,3},{2,0},{3,1},{4,6},{5,7},{6,4},{7,5},{8,10},{9,11},{10,... | collective-permute-start | bytes 73736 | tf_op jit(solution)/shard_map/ppermute | solution.py:1002
  13.5 0.0 collective-permute-start.2
  13.6 0.5 copy-done.8
  14.2 0.3 setup_kernel.1
  14.5 4.0 %all-to-all-done = f32[32,4,128]{2,1,0:T(4,128)S(1)} async-done(((f32[32,4,128]{2,1,0:T(4,128)}), f32[32,4,128]{2,1,0:T(4,128)S(1)}, u32[]{:S(2)}, u32[]{:S(2)}) %all-to-all-start) | async-done | bytes 65568 | tf_op jit(solution)/shard_map/all_to_all | solution.py:995
  18.5 0.4 moment_kernel.1
  18.8 0.0 collective-permute-done.refs_1_
  18.8 0.0 collective-permute-done.1.refs_2_
  18.8 0.0 collective-permute-done.2.refs_3_
  18.9 2.2 %stage_one_kernel.1 = (f32[128,128]{1,0:T(8,128)S(1)}, bf16[6,48,128]{2,1,0:T(8,128)(2,1)S(1)}, bf16[3,4,32,128]{3,2,1,0:T(8,128)(2,1)S(1)}, bf16[6,144,128]{2,1...) custom-call(f32[3,144,128]{2,1,0:T(8,128)S(1)} %get-tuple-element.88, ...), custom_call_target="tpu_custom_call" | custom-call | flops 1000000000 | bytes 3000000 | tf_op jit(solution)/shard_map/stage_one_kernel/pallas_call | solution.py:980
  21.1 10.0 %all_to_all.55 = f32[32,4,128]{2,1,0:T(4,128)S(1)} all-to-all(f32[32,4,128]{2,1,0:T(4,128)S(1)} %bitcast.20), channel_id=1, replica_groups=mesh['seg'=8,'tile'=4] {'seg','tile'}, dimensions={0} | all-to-all | bytes 131072 | tf_op jit(solution)/shard_map/all_to_all | solution.py:995
  31.0 2.8 %stage_two_kernel.1 = (f32[64,128]{1,0:T(8,128)S(1)}, f32[6,144,128]{2,1,0:T(8,128)S(1)}, f32[6,144,128]{2,1,0:T(8,128)S(1)}, f32[6,144,128]{2,1,0:T(8,128)S(1)}...) custom-call(f32[128,128]{1,0:T(8,128)S(1)} %bitcast.21, ...), custom_call_target="tpu_custom_call" | custom-call | flops 1000000000 | bytes 3000000 | tf_op jit(solution)/shard_map/stage_two_kernel/pallas_call | solution.py:980
  33.8 8.9 %all_to_all.56 = f32[32,2,128]{2,1,0:T(2,128)S(1)} all-to-all(f32[32,2,128]{2,1,0:T(2,128)S(1)} %bitcast.23), channel_id=1, replica_groups=mesh['seg'=8,'tile'=4] {'seg','tile'}, dimensions={0} | all-to-all | bytes 65536 | tf_op jit(solution)/shard_map/all_to_all | solution.py:995
  42.7 3.7 %stage_three_kernel.1 = (f32[256,128]{1,0:T(8,128)S(1)}, f32[6,24,128]{2,1,0:T(8,128)S(1)}, f32[6,144,128]{2,1,0:T(8,128)S(1)}, f32[24]{0:T(128)}, f32[24]{0:T(128)}) custom-call(f32[64,128]{1,0:T(8,128)S(1)} %bitcast.22, f32[6,24,128]{2,1,0:T(8,128)S(1)} %get-tuple-element.107.proj_ref, bf16[6,48,128]{2,1,0:T(8,128)(2,1)S(1)} %get-tuple-element.99.xc_ref, ...), custom_call_target="tpu_custom_call" | custom-call | flops 1000000000 | bytes 3000000 | tf_op jit(solution)/shard_map/stage_three_kernel/pallas_call | solution.py:980
  46.5 9.9 %all_to_all.57 = f32[32,8,128]{2,1,0:T(8,128)S(1)} all-to-all(f32[32,8,128]{2,1,0:T(8,128)S(1)} %bitcast.17), channel_id=1, replica_groups=mesh['seg'=8,'tile'=4] {'seg','tile'}, dimensions={0} | all-to-all | bytes 262144 | tf_op jit(solution)/shard_map/all_to_all | solution.py:995
  56.4 1.9 %stage_four_kernel.1 = (f32[256,128]{1,0:T(8,128)}, f32[6,144,128]{2,1,0:T(8,128)S(1)}, f32[144]{0:T(256)}, f32[144]{0:T(256)}, f32[2,144]{1,0:T(2,128)S(1)}) custom-call(f32[256,128]{1,0:T(8,128)S(1)} %bitcast.15, f32[6,144,128]{2,1,0:T(8,128)S(1)} %get-tuple-element.118.scaled_ref, f32[6,144,128]{2,1,0:T(8,128)S(1)} %get-tuple-element.109.dc_ref, ...), custom_call_target="tpu_custom_call" | custom-call | flops 1000000000 | bytes 3000000 | tf_op jit(solution)/shard_map/stage_four_kernel/pallas_call | solution.py:980
  58.3 2.6 %all-to-all-start.4 = ((f32[32,8,128]{2,1,0:T(8,128)}), f32[32,8,128]{2,1,0:T(8,128)S(1)}, u32[]{:S(2)}, u32[]{:S(2)}) async-start(f32[32,8,128]{2,1,0:T(8,128)} %bitcast.10), calls=%async_computation.4 | async-start | bytes 262144 | tf_op jit(solution)/shard_map/all_to_all | solution.py:995
  60.9 0.5 back_kernel.1
  61.4 0.2 collective-permute-start.3
  61.5 1.7 %collective-permute-start.4 = (bf16[2,3,16,128]{3,2,1,0:T(8,128)(2,1)S(1)}, bf16[2,3,16,128]{3,2,1,0:T(8,128)(2,1)S(1)}, u32[]{:S(2)}, u32[]{:S(2)}) collective-permute-start(bf16[2,3,16,128]{3,2,1,0:T(8,128)(2,1)S(1)} %get-tuple-element.134), channel_id=1, source_target_pairs={{0,2},{1,3},{2,0},{3,1},{4,6},{5,7},{6,4},{7,5},{8,10},{9,11},{10,... | collective-permute-start | bytes 73736 | tf_op jit(solution)/shard_map/ppermute | solution.py:1002
  63.3 0.1 collective-permute-start.5
  63.3 0.6 far_kernel.1
  64.0 5.1 %all-to-all-done.4 = f32[32,8,128]{2,1,0:T(8,128)S(1)} async-done(((f32[32,8,128]{2,1,0:T(8,128)}), f32[32,8,128]{2,1,0:T(8,128)S(1)}, u32[]{:S(2)}, u32[]{:S(2)}) %all-to-all-start.4) | async-done | bytes 131104 | tf_op jit(solution)/shard_map/all_to_all | solution.py:995
  69.1 1.3 %weights_kernel.1 = (f32[24,144]{1,0:T(8,128)}, f32[144]{0:T(256)}, f32[144]{0:T(256)}, f32[3,3,144]{2,1,0:T(4,128)}, f32[6,144]{1,0:T(8,128)}, /*index=5*/f32[6...) custom-call(f32[256,128]{1,0:T(8,128)S(1)} %bitcast.14, ...), custom_call_target="tpu_custom_call" | custom-call | flops 1000000000 | bytes 3000000 | tf_op jit(solution)/shard_map/weights_kernel/pallas_call | solution.py:980
  70.4 0.0 collective-permute-done.3.refs_1_
  70.4 0.0 collective-permute-done.4.refs_2_
  70.4 0.0 collective-permute-done.5.refs_3_
  70.4 1.1 %return_kernel.1 = (bf16[8,6,16,24]{3,2,1,0:T(8,128)(2,1)}, bf16[8,6,16,24]{3,2,1,0:T(8,128)(2,1)}) custom-call(bf16[8,6,16,24]{3,2,1,0:T(8,128)(2,1)S(1)} %copy-done.2, f32[6,128,24]{2,1,0:T(8,128)S(1)} %get-tuple-element.130.corr_ref, bf16[2,3,16,128]{3,2,1,0:T(8,128)(2,1)S(1)} %get-tuple-element.132.refs_0_, ...), custom_call_target="tpu_custom_call" | custom-call | flops 1000000000 | bytes 3000000 | tf_op jit(solution)/shard_map/return_kernel/pallas_call | solution.py:980
  (19 shorter events, 0.0 us)
Async XLA Ops:
  1.3 9.8 %copy-start.1 = (bf16[8,6,16,24]{3,2,1,0:T(8,128)(2,1)S(1)}, bf16[8,6,16,24]{3,2,1,0:T(8,128)(2,1)}, u32[]{:S(2)}) copy-start(bf16[8,6,16,24]{3,2,1,0:T(8,128)(2,1)} %x_ref.3) | copy-start | bytes 110596
  1.3 9.8 %copy-start.2 = (bf16[8,6,16,24]{3,2,1,0:T(8,128)(2,1)S(1)}, bf16[8,6,16,24]{3,2,1,0:T(8,128)(2,1)}, u32[]{:S(2)}) copy-start(bf16[8,6,16,24]{3,2,1,0:T(8,128)(2,1)} %c_ref.3) | copy-start | bytes 110596
  3.8 7.3 %copy-start = (f32[128,128]{1,0:T(8,128)S(1)}, f32[128,128]{1,0:T(8,128)}, u32[]{:S(2)}) copy-start(f32[128,128]{1,0:T(8,128)} %get-tuple-element.84.after_ref) | copy-start | bytes 196612
  3.8 14.7 %all-to-all-start = ((f32[32,4,128]{2,1,0:T(4,128)}), f32[32,4,128]{2,1,0:T(4,128)S(1)}, u32[]{:S(2)}, u32[]{:S(2)}) async-start(f32[32,4,128]{2,1,0:T(4,128)} %bitcast.19), calls=%async_computation | async-start | bytes 131072 | tf_op jit(solution)/shard_map/all_to_all | solution.py:995
  11.1 2.4 %copy-start.4 = (bf16[144,24]{0,1:T(8,128)(2,1)S(1)}, bf16[144,24]{0,1:T(8,128)(2,1)}, u32[]{:S(2)}) copy-start(bf16[144,24]{0,1:T(8,128)(2,1)} %param.28) | copy-start | bytes 20740
  11.1 2.4 %copy-start.5 = (f32[144,6]{0,1:T(8,128)S(1)}, f32[144,6]{0,1:T(8,128)}, u32[]{:S(2)}) copy-start(f32[144,6]{0,1:T(8,128)} %param.24) | copy-start | bytes 10372
  11.1 2.4 %copy-start.6 = (f32[6,144]{1,0:T(8,128)S(1)}, f32[6,144]{1,0:T(8,128)}, u32[]{:S(2)}) copy-start(f32[6,144]{1,0:T(8,128)} %refs_10_.1) | copy-start | bytes 10372
  11.1 2.4 %copy-start.7 = (bf16[3,3,144]{2,1,0:T(4,128)(2,1)S(1)}, bf16[3,3,144]{2,1,0:T(4,128)(2,1)}, u32[]{:S(2)}) copy-start(bf16[3,3,144]{2,1,0:T(4,128)(2,1)} %refs_8_.1) | copy-start | bytes 7780
  11.2 2.4 %copy-start.9 = (f32[144]{0:T(256)S(1)}, f32[144]{0:T(256)}, u32[]{:S(2)}) copy-start(f32[144]{0:T(256)} %refs_1_.1) | copy-start | bytes 1732
  11.2 2.4 %copy-start.10 = (f32[144]{0:T(256)S(1)}, f32[144]{0:T(256)}, u32[]{:S(2)}) copy-start(f32[144]{0:T(256)} %refs_2_.1) | copy-start | bytes 1732
  11.2 2.4 %copy-start.11 = (f32[144]{0:T(256)S(1)}, f32[144]{0:T(256)}, u32[]{:S(2)}) copy-start(f32[144]{0:T(256)} %refs_3_.1) | copy-start | bytes 1732
  11.2 2.4 %copy-start.12 = (f32[144]{0:T(256)S(1)}, f32[144]{0:T(256)}, u32[]{:S(2)}) copy-start(f32[144]{0:T(256)} %refs_4_.1) | copy-start | bytes 1732
  11.2 2.4 %copy-start.13 = (f32[24]{0:T(128)S(1)}, f32[24]{0:T(128)}, u32[]{:S(2)}) copy-start(f32[24]{0:T(128)} %refs_5_.1) | copy-start | bytes 292
  11.2 2.4 %copy-start.14 = (f32[24]{0:T(128)S(1)}, f32[24]{0:T(128)}, u32[]{:S(2)}) copy-start(f32[24]{0:T(128)} %refs_6_.1) | copy-start | bytes 292
  11.2 2.4 %copy-start.15 = (f32[6]{0:T(128)S(1)}, f32[6]{0:T(128)}, u32[]{:S(2)}) copy-start(f32[6]{0:T(128)} %refs_7_.1) | copy-start | bytes 76
  11.2 2.4 %copy-start.16 = (f32[16,128]{1,0:T(8,128)S(1)}, f32[16,128]{1,0:T(8,128)}, u32[]{:S(2)}) copy-start(f32[16,128]{1,0:T(8,128)} %get-tuple-element.85.refs_13_) | copy-start | bytes 24580
  11.3 2.4 %copy-start.17 = (f32[16,128]{1,0:T(8,128)S(1)}, f32[16,128]{1,0:T(8,128)}, u32[]{:S(2)}) copy-start(f32[16,128]{1,0:T(8,128)} %get-tuple-element.86.refs_14_) | copy-start | bytes 24580
  11.5 2.1 %copy-start.3 = (bf16[24,144]{1,0:T(8,128)(2,1)S(1)}, bf16[24,144]{1,0:T(8,128)(2,1)}, u32[]{:S(2)}) copy-start(bf16[24,144]{1,0:T(8,128)(2,1)} %refs_12_.1) | copy-start | bytes 20740
  11.5 7.3 %collective-permute-start = (bf16[2,3,16,128]{3,2,1,0:T(8,128)(2,1)S(1)}, bf16[2,3,16,128]{3,2,1,0:T(8,128)(2,1)S(1)}, u32[]{:S(2)}, u32[]{:S(2)}) collective-permute-start(bf16[2,3,16,128]{3,2,1,0:T(8,128)(2,1)S(1)} %get-tuple-element.90), channel_id=1, source_target_pairs={{0,1},{1,0},{2,3},{3,2},{4,5},{5,4},{6,7},{7,6},{8,9},{9,8},{10,11... | collective-permute-start | bytes 73736 | tf_op jit(solution)/shard_map/ppermute | solution.py:1002
  11.8 7.0 %collective-permute-start.1 = (bf16[2,3,16,128]{3,2,1,0:T(8,128)(2,1)S(1)}, bf16[2,3,16,128]{3,2,1,0:T(8,128)(2,1)S(1)}, u32[]{:S(2)}, u32[]{:S(2)}) collective-permute-start(bf16[2,3,16,128]{3,2,1,0:T(8,128)(2,1)S(1)} %get-tuple-element.91), channel_id=1, source_target_pairs={{0,2},{1,3},{2,0},{3,1},{4,6},{5,7},{6,4},{7,5},{8,10},{9,11},{10,... | collective-permute-start | bytes 73736 | tf_op jit(solution)/shard_map/ppermute | solution.py:1002
  13.5 5.4 %collective-permute-start.2 = (bf16[2,3,16,128]{3,2,1,0:T(8,128)(2,1)S(1)}, bf16[2,3,16,128]{3,2,1,0:T(8,128)(2,1)S(1)}, u32[]{:S(2)}, u32[]{:S(2)}) collective-permute-start(bf16[2,3,16,128]{3,2,1,0:T(8,128)(2,1)S(1)} %get-tuple-element.92), channel_id=1, source_target_pairs={{0,3},{1,2},{2,1},{3,0},{4,7},{5,6},{6,5},{7,4},{8,11},{9,10},{10,... | collective-permute-start | bytes 73736 | tf_op jit(solution)/shard_map/ppermute | solution.py:1002
  13.5 0.7 copy-start.8
  58.3 10.8 %all-to-all-start.4 = ((f32[32,8,128]{2,1,0:T(8,128)}), f32[32,8,128]{2,1,0:T(8,128)S(1)}, u32[]{:S(2)}, u32[]{:S(2)}) async-start(f32[32,8,128]{2,1,0:T(8,128)} %bitcast.10), calls=%async_computation.4 | async-start | bytes 262144 | tf_op jit(solution)/shard_map/all_to_all | solution.py:995
  61.4 9.0 %collective-permute-start.3 = (bf16[2,3,16,128]{3,2,1,0:T(8,128)(2,1)S(1)}, bf16[2,3,16,128]{3,2,1,0:T(8,128)(2,1)S(1)}, u32[]{:S(2)}, u32[]{:S(2)}) collective-permute-start(bf16[2,3,16,128]{3,2,1,0:T(8,128)(2,1)S(1)} %get-tuple-element.133), channel_id=1, source_target_pairs={{0,1},{1,0},{2,3},{3,2},{4,5},{5,4},{6,7},{7,6},{8,9},{9,8},{10,11... | collective-permute-start | bytes 73736 | tf_op jit(solution)/shard_map/ppermute | solution.py:1002
  61.5 8.8 %collective-permute-start.4 = (bf16[2,3,16,128]{3,2,1,0:T(8,128)(2,1)S(1)}, bf16[2,3,16,128]{3,2,1,0:T(8,128)(2,1)S(1)}, u32[]{:S(2)}, u32[]{:S(2)}) collective-permute-start(bf16[2,3,16,128]{3,2,1,0:T(8,128)(2,1)S(1)} %get-tuple-element.134), channel_id=1, source_target_pairs={{0,2},{1,3},{2,0},{3,1},{4,6},{5,7},{6,4},{7,5},{8,10},{9,11},{10,... | collective-permute-start | bytes 73736 | tf_op jit(solution)/shard_map/ppermute | solution.py:1002
  63.3 7.1 %collective-permute-start.5 = (bf16[2,3,16,128]{3,2,1,0:T(8,128)(2,1)S(1)}, bf16[2,3,16,128]{3,2,1,0:T(8,128)(2,1)S(1)}, u32[]{:S(2)}, u32[]{:S(2)}) collective-permute-start(bf16[2,3,16,128]{3,2,1,0:T(8,128)(2,1)S(1)} %get-tuple-element.135), channel_id=1, source_target_pairs={{0,3},{1,2},{2,1},{3,0},{4,7},{5,6},{6,5},{7,4},{8,11},{9,10},{10,... | collective-permute-start | bytes 73736 | tf_op jit(solution)/shard_map/ppermute | solution.py:1002

commit v4 on v3

--- a/solution.py
+++ b/solution.py
@@ -276,6 +276,10 @@
         block = jnp.concatenate([block] * (8 // count), axis=0)
     for at in range(0, ref.shape[0], 8):
         ref[at : at + 8] = block
+
+
+def steps(sz):
+    return [0] + list(range(2, sz.tiles)) + [1]
 
 
 def partner(step):
@@ -354,7 +358,7 @@
 
 def send_kernel(sz, x_ref, c_ref, after_ref, *out_refs):
     del after_ref
-    for step, out_ref in enumerate(out_refs):
+    for step, out_ref in zip(steps(sz), out_refs):
         first = partner(step) * sz.own
         out_ref[...] = jnp.zeros(out_ref.shape, BF16)
         for t in range(sz.rows):
@@ -412,7 +416,7 @@
     chans = sz.chans
     half = sz.wide - LANES
     size = sz.own * sz.width
-    for step, ref in enumerate(own_refs):
+    for step, ref in zip(steps(sz), own_refs):
         source = partner(step)
         for g in range(sz.rows // 2):
             pix_ref[g, source] = ref[:, g].reshape(size, LANES)
@@ -824,7 +828,7 @@
         pieces.append(jnp.zeros((LANES - 4 * chans, LANES), F32))
         turned = jnp.concatenate(pieces, axis=0).T.astype(BF16)
         all_ref[:, :, g] = turned.reshape(sz.tiles, sz.own, sz.width, LANES)
-    for step, out_ref in enumerate(out_refs):
+    for step, out_ref in zip(steps(sz), out_refs):
         out_ref[...] = all_ref[partner(step)]
 
 
@@ -867,7 +871,7 @@
     return dot(jnp.concatenate([unit] * 3, axis=1), tripled(columns), 1, 1)[0:count]
 
 
-def weights_kernel(
+def last_kernel(
     sz,
     pay_ref,
     two_ref,
@@ -879,10 +883,14 @@
     mid_ref,
     par_ref,
     w_ref,
+    c_ref,
     *refs,
 ):
-    ew_ref, gg0_ref, bg0_ref, dw_ref, rw_ref, rb_ref, sw_ref, sb_ref, pw_ref, rms_ref = refs[:10]
-    corr_ref, buf_ref = refs[10:]
+    got_refs = refs[: sz.tiles]
+    out_ref, xg_ref, ew_ref, gg0_ref, bg0_ref, dw_ref, rw_ref, rb_ref = refs[
+        sz.tiles : sz.tiles + 8
+    ]
+    sw_ref, sb_ref, pw_ref, rms_ref, corr_ref, buf_ref = refs[sz.tiles + 8 :]
     chans = sz.chans
     half = sz.wide - LANES
     each = LANES // sz.devices
@@ -907,6 +915,26 @@
     for t in range(sz.rows):
         cells = live_ref[t]
         corr_ref[t] = dot(cells, high, 1, 0) + dot(cells, low, 1, 0)
+    shape = (LANES, 4 * LANES)
+    column = iota(shape, 1)
+    spot = lax.rem(column, LANES)
+    source = spot + chans * lax.div(column, LANES)
+    unit = jnp.where((iota(shape, 0) == source) & (spot < chans), 1.0, 0.0).astype(BF16)
+    size = sz.own * sz.width
+    shape = (sz.own, sz.width, chans)
+    for step, ref in zip(steps(sz), got_refs):
+        first = partner(step) * sz.own
+        for g in range(sz.rows // 2):
+            cells = dot(ref[:, g].reshape(size, LANES), unit, 1, 0)
+            for par in range(2):
+                t = 2 * g + par
+                at = 2 * par * LANES
+                held = cells[:, at : at + chans]
+                out_ref[pl.ds(first, sz.own), t] = held.astype(BF16).reshape(shape)
+                at = at + LANES
+                held = cells[:, at : at + chans] - corr_ref[t, pl.ds(first * sz.width, size)]
+                held = held.reshape(shape) + c_ref[pl.ds(first, sz.own), t].astype(F32)
+                xg_ref[pl.ds(first, sz.own), t] = held.astype(BF16)
     used = 3 * chans + 29 + 2 * sz.squeeze
     piece = LANES - used
     for k in range(each):
@@ -948,32 +976,6 @@
     rms_ref[...] = jnp.sqrt(squares / (total[:, :5] * chan_row)).reshape(5)
 
 
-def return_kernel(sz, c_ref, corr_ref, *refs):
-    got_refs = refs[: sz.tiles]
-    out_ref, xg_ref = refs[sz.tiles :]
-    chans = sz.chans
-    shape = (LANES, 4 * LANES)
-    column = iota(shape, 1)
-    spot = lax.rem(column, LANES)
-    source = spot + chans * lax.div(column, LANES)
-    unit = jnp.where((iota(shape, 0) == source) & (spot < chans), 1.0, 0.0).astype(BF16)
-    size = sz.own * sz.width
-    shape = (sz.own, sz.width, chans)
-    for step, ref in enumerate(got_refs):
-        first = partner(step) * sz.own
-        for g in range(sz.rows // 2):
-            cells = dot(ref[:, g].reshape(size, LANES), unit, 1, 0)
-            for par in range(2):
-                t = 2 * g + par
-                at = 2 * par * LANES
-                held = cells[:, at : at + chans]
-                out_ref[pl.ds(first, sz.own), t] = held.astype(BF16).reshape(shape)
-                at = at + LANES
-                held = cells[:, at : at + chans] - corr_ref[t, pl.ds(first * sz.width, size)]
-                held = held.reshape(shape) + c_ref[pl.ds(first, sz.own), t].astype(F32)
-                xg_ref[pl.ds(first, sz.own), t] = held.astype(BF16)
-
-
 def call(kernel, sz, args, kinds, outs, scratch=(), cost=1.0, room=16):
     spaces = {"v": VMEM, "s": SMEM, "h": HBM, "a": pl.BlockSpec(memory_space=pl.ANY)}
     kinds = kinds + "v" * (len(args) - len(kinds))
@@ -996,10 +998,10 @@
 
 
 def passed(sz, parts):
-    result = list(parts)
-    for step in list(range(2, sz.tiles)) + [1]:
+    result = [parts[0]]
+    for step, part in zip(steps(sz)[1:], parts[1:]):
         pairs = [(i, i ^ step) for i in range(sz.tiles)]
-        result[step] = lax.ppermute(parts[step], "tile", pairs)
+        result.append(lax.ppermute(part, "tile", pairs))
     return result
 
 
@@ -1136,12 +1138,14 @@
         + [((rows, LANES, 32), BF16)],
         [column, ((32, LANES), F32)],
     )
-    ew, gg0, bg0, dw, rw, rb, sw, sb, pw, rms, corr = call(
-        weights_kernel,
+    block_out, x_grad, ew, gg0, bg0, dw, rw, rb, sw, sb, pw, rms = call(
+        last_kernel,
         sz,
-        [pay] + list(far) + [row0, row1, mid, par, w_near],
+        [pay] + list(far) + [row0, row1, mid, par, w_near, cotangent] + sent,
         "",
         [
+            (x_input.shape, BF16),
+            (x_input.shape, BF16),
             ((chans, wide), F32),
             ((wide,), F32),
             ((wide,), F32),
@@ -1152,16 +1156,8 @@
             ((wide,), F32),
             ((chans, wide), F32),
             ((5,), F32),
-            ((rows, LANES, chans), F32),
         ],
-        [column],
-    )
-    block_out, x_grad = call(
-        return_kernel,
-        sz,
-        [cotangent, corr] + sent,
-        "",
-        [(x_input.shape, BF16), (x_input.shape, BF16)],
+        [((rows, LANES, chans), F32), column],
     )
     return (
         block_out,

time: 71.8 us -> 70.9 us (0.987)
  Pallas kernels: 17.4 us -> 16.6 us
    all_to_all x2, waiting for transfers between devices: 9.15 us -> 6.04 us  [everywhere(): return lax.all_to_all(values, BOTH, 0, 0, tiled=True)]
    ppermute x6, waiting for transfers between devices: 0.02 us -> 2.67 us  [passed(): result.append(lax.ppermute(part, 'tile', pairs))]
    pallas_call x12 -> x11, Pallas kernels: 17.4 us -> 16.6 us  [call(): pl.pallas_call(functools.partial(kernel, sz), out_shape=tuple((jax.ShapeD...]
  transfers between devices with their start and end apart: 8 -> 8, of which waited for: 2 -> 4; matrix products, arithmetic and copies ran while one was open for 0% -> 0% of each run, Pallas kernels for 5% -> 3%
where the time goes in v4:
time: 70.9 us; the launch traced here: 70.5 us
  blocking collectives  28.7 us (40%)
  Pallas kernels  16.6 us (23%)
  starting transfers between devices  14.3 us (20%)
  waiting for transfers between devices  8.71 us (12%)
  between operations  1.61 us (2%)
    all_to_all x3, blocking collectives, everywhere(): return lax.all_to_all(values, BOTH, 0, 0, tiled=True)  28.7 us
    pallas_call x11, Pallas kernels, call(): pl.pallas_call(functools.partial(kernel, sz), out_shape=tuple((jax.ShapeD...  16.6 us
    all_to_all x2, starting transfers between devices, everywhere(): return lax.all_to_all(values, BOTH, 0, 0, tiled=True)  9.88 us
    all_to_all x2, waiting for transfers between devices, everywhere(): return lax.all_to_all(values, BOTH, 0, 0, tiled=True)  6.04 us
    ppermute x6, starting transfers between devices, passed(): result.append(lax.ppermute(part, 'tile', pairs))  4.41 us
    ppermute x6, waiting for transfers between devices, passed(): result.append(lax.ppermute(part, 'tile', pairs))  2.67 us
  transfers between devices with their start and end apart: 8, of which 4 were waited for; matrix products, arithmetic and copies ran while one was open for 0% of the time, Pallas kernels for 3%

profile of v4, /device:TPU:0, one launch (start us, length us, event | category | flops | bytes accessed | tf_op | source)
XLA Modules:
  0.0 70.5 jit_solution(10575890778258770567)
XLA Ops:
  1.3 2.4 %entry_kernel.1 = (f32[128,128]{1,0:T(8,128)}, f32[16,128]{1,0:T(8,128)}, f32[16,128]{1,0:T(8,128)}) custom-call(bf16[8,6,16,24]{3,2,1,0:T(8,128)(2,1)} %x_ref.3, bf16[24,144]{1,0:T(8,128)(2,1)} %refs_12_.1, s32[8]{0:T(128)} %len_hbm.1, s32[1]{0:T(128)S(6)} %copy.33.count_hbm), custom_call_target="tpu_custom_call" | custom-call | flops 1000000000 | bytes 3000000 | tf_op jit(solution)/shard_map/entry_kernel/pallas_call | solution.py:982
  3.8 0.0 copy-start
  3.8 7.3 %all-to-all-start = ((f32[32,4,128]{2,1,0:T(4,128)}), f32[32,4,128]{2,1,0:T(4,128)S(1)}, u32[]{:S(2)}, u32[]{:S(2)}) async-start(f32[32,4,128]{2,1,0:T(4,128)} %bitcast.19), calls=%async_computation | async-start | bytes 131072 | tf_op jit(solution)/shard_map/all_to_all | solution.py:997
  11.1 0.0 copy-done.1
  11.1 0.0 copy-done.2
  11.1 0.0 copy-done
  11.1 0.0 copy-start.4
  11.1 0.0 copy-start.5
  11.1 0.0 copy-start.6
  11.1 0.0 copy-start.7
  11.2 0.0 copy-start.9
  11.2 0.0 copy-start.10
  11.2 0.0 copy-start.11
  11.2 0.0 copy-start.12
  11.2 0.0 copy-start.13
  11.2 0.0 copy-start.14
  11.2 0.0 copy-start.15
  11.2 0.0 copy-start.16
  11.2 0.0 copy-start.17
  11.3 0.2 send_kernel.1
  11.5 1.8 %collective-permute-start = (bf16[2,3,16,128]{3,2,1,0:T(8,128)(2,1)S(1)}, bf16[2,3,16,128]{3,2,1,0:T(8,128)(2,1)S(1)}, u32[]{:S(2)}, u32[]{:S(2)}) collective-permute-start(bf16[2,3,16,128]{3,2,1,0:T(8,128)(2,1)S(1)} %get-tuple-element.89), channel_id=1, source_target_pairs={{0,2},{1,3},{2,0},{3,1},{4,6},{5,7},{6,4},{7,5},{8,10},{9,11},{10,... | collective-permute-start | bytes 73736 | tf_op jit(solution)/shard_map/ppermute | solution.py:1004
  13.3 0.0 collective-permute-start.1
  13.3 0.4 collective-permute-start.2
  13.8 0.6 copy-done.8
  14.4 0.3 setup_kernel.1
  14.7 3.8 %all-to-all-done = f32[32,4,128]{2,1,0:T(4,128)S(1)} async-done(((f32[32,4,128]{2,1,0:T(4,128)}), f32[32,4,128]{2,1,0:T(4,128)S(1)}, u32[]{:S(2)}, u32[]{:S(2)}) %all-to-all-start) | async-done | bytes 65568 | tf_op jit(solution)/shard_map/all_to_all | solution.py:997
  18.5 0.4 moment_kernel.1
  18.8 0.0 collective-permute-done.refs_1_
  18.8 0.0 collective-permute-done.1.refs_2_
  18.8 0.0 collective-permute-done.2.refs_3_
  18.9 2.2 %stage_one_kernel.1 = (f32[128,128]{1,0:T(8,128)S(1)}, bf16[6,48,128]{2,1,0:T(8,128)(2,1)S(1)}, bf16[3,4,32,128]{3,2,1,0:T(8,128)(2,1)S(1)}, bf16[6,144,128]{2,1...) custom-call(f32[3,144,128]{2,1,0:T(8,128)S(1)} %get-tuple-element.87, ...), custom_call_target="tpu_custom_call" | custom-call | flops 1000000000 | bytes 3000000 | tf_op jit(solution)/shard_map/stage_one_kernel/pallas_call | solution.py:982
  21.1 9.8 %all_to_all.55 = f32[32,4,128]{2,1,0:T(4,128)S(1)} all-to-all(f32[32,4,128]{2,1,0:T(4,128)S(1)} %bitcast.20), channel_id=1, replica_groups=mesh['seg'=8,'tile'=4] {'seg','tile'}, dimensions={0} | all-to-all | bytes 131072 | tf_op jit(solution)/shard_map/all_to_all | solution.py:997
  30.9 2.8 %stage_two_kernel.1 = (f32[64,128]{1,0:T(8,128)S(1)}, f32[6,144,128]{2,1,0:T(8,128)S(1)}, f32[6,144,128]{2,1,0:T(8,128)S(1)}, f32[6,144,128]{2,1,0:T(8,128)S(1)}...) custom-call(f32[128,128]{1,0:T(8,128)S(1)} %bitcast.21, ...), custom_call_target="tpu_custom_call" | custom-call | flops 1000000000 | bytes 3000000 | tf_op jit(solution)/shard_map/stage_two_kernel/pallas_call | solution.py:982
  33.6 8.9 %all_to_all.56 = f32[32,2,128]{2,1,0:T(2,128)S(1)} all-to-all(f32[32,2,128]{2,1,0:T(2,128)S(1)} %bitcast.23), channel_id=1, replica_groups=mesh['seg'=8,'tile'=4] {'seg','tile'}, dimensions={0} | all-to-all | bytes 65536 | tf_op jit(solution)/shard_map/all_to_all | solution.py:997
  42.6 3.7 %stage_three_kernel.1 = (f32[256,128]{1,0:T(8,128)S(1)}, f32[6,24,128]{2,1,0:T(8,128)S(1)}, f32[6,144,128]{2,1,0:T(8,128)S(1)}, f32[24]{0:T(128)}, f32[24]{0:T(128)}) custom-call(f32[64,128]{1,0:T(8,128)S(1)} %bitcast.22, f32[6,24,128]{2,1,0:T(8,128)S(1)} %get-tuple-element.106.proj_ref, bf16[6,48,128]{2,1,0:T(8,128)(2,1)S(1)} %get-tuple-element.98.xc_ref, ...), custom_call_target="tpu_custom_call" | custom-call | flops 1000000000 | bytes 3000000 | tf_op jit(solution)/shard_map/stage_three_kernel/pallas_call | solution.py:982
  46.3 9.9 %all_to_all.57 = f32[32,8,128]{2,1,0:T(8,128)S(1)} all-to-all(f32[32,8,128]{2,1,0:T(8,128)S(1)} %bitcast.17), channel_id=1, replica_groups=mesh['seg'=8,'tile'=4] {'seg','tile'}, dimensions={0} | all-to-all | bytes 262144 | tf_op jit(solution)/shard_map/all_to_all | solution.py:997
  56.2 1.9 %stage_four_kernel.1 = (f32[256,128]{1,0:T(8,128)}, f32[6,144,128]{2,1,0:T(8,128)S(1)}, f32[144]{0:T(256)}, f32[144]{0:T(256)}, f32[2,144]{1,0:T(2,128)S(1)}) custom-call(f32[256,128]{1,0:T(8,128)S(1)} %bitcast.15, f32[6,144,128]{2,1,0:T(8,128)S(1)} %get-tuple-element.117.scaled_ref, f32[6,144,128]{2,1,0:T(8,128)S(1)} %get-tuple-element.108.dc_ref, ...), custom_call_target="tpu_custom_call" | custom-call | flops 1000000000 | bytes 3000000 | tf_op jit(solution)/shard_map/stage_four_kernel/pallas_call | solution.py:982
  58.1 2.6 %all-to-all-start.4 = ((f32[32,8,128]{2,1,0:T(8,128)}), f32[32,8,128]{2,1,0:T(8,128)S(1)}, u32[]{:S(2)}, u32[]{:S(2)}) async-start(f32[32,8,128]{2,1,0:T(8,128)} %bitcast.10), calls=%async_computation.4 | async-start | bytes 262144 | tf_op jit(solution)/shard_map/all_to_all | solution.py:997
  60.7 0.5 back_kernel.1
  61.2 1.7 %collective-permute-start.3 = (bf16[2,3,16,128]{3,2,1,0:T(8,128)(2,1)S(1)}, bf16[2,3,16,128]{3,2,1,0:T(8,128)(2,1)S(1)}, u32[]{:S(2)}, u32[]{:S(2)}) collective-permute-start(bf16[2,3,16,128]{3,2,1,0:T(8,128)(2,1)S(1)} %get-tuple-element.131), channel_id=1, source_target_pairs={{0,2},{1,3},{2,0},{3,1},{4,6},{5,7},{6,4},{7,5},{8,10},{9,11},{10,... | collective-permute-start | bytes 73736 | tf_op jit(solution)/shard_map/ppermute | solution.py:1004
  62.9 0.0 collective-permute-start.4
  62.9 0.5 collective-permute-start.5
  63.4 0.6 far_kernel.1
  64.1 1.2 %collective-permute-done.3.refs_1_ = bf16[2,3,16,128]{3,2,1,0:T(8,128)(2,1)S(1)} collective-permute-done((bf16[2,3,16,128]{3,2,1,0:T(8,128)(2,1)S(1)}, bf16[2,3,16,128]{3,2,1,0:T(8,128)(2,1)S(1)}, u32[]{:S(2)}, u32[]{:S(2)}) %collective-permute-start.3) | collective-permute-done | bytes 24608 | tf_op jit(solution)/shard_map/ppermute | solution.py:1004
  65.2 1.5 %collective-permute-done.4.refs_2_ = bf16[2,3,16,128]{3,2,1,0:T(8,128)(2,1)S(1)} collective-permute-done((bf16[2,3,16,128]{3,2,1,0:T(8,128)(2,1)S(1)}, bf16[2,3,16,128]{3,2,1,0:T(8,128)(2,1)S(1)}, u32[]{:S(2)}, u32[]{:S(2)}) %collective-permute-start.4) | collective-permute-done | bytes 24608 | tf_op jit(solution)/shard_map/ppermute | solution.py:1004
  66.7 0.0 collective-permute-done.5.refs_3_
  66.7 2.2 %all-to-all-done.4 = f32[32,8,128]{2,1,0:T(8,128)S(1)} async-done(((f32[32,8,128]{2,1,0:T(8,128)}), f32[32,8,128]{2,1,0:T(8,128)S(1)}, u32[]{:S(2)}, u32[]{:S(2)}) %all-to-all-start.4) | async-done | bytes 131104 | tf_op jit(solution)/shard_map/all_to_all | solution.py:997
  69.0 1.6 %last_kernel.1 = (bf16[8,6,16,24]{3,2,1,0:T(8,128)(2,1)}, bf16[8,6,16,24]{3,2,1,0:T(8,128)(2,1)}, f32[24,144]{1,0:T(8,128)}, f32[144]{0:T(256)}, f32[144]{0:T(25...) custom-call(f32[256,128]{1,0:T(8,128)S(1)} %bitcast.14, ...), custom_call_target="tpu_custom_call" | custom-call | flops 1000000000 | bytes 3000000 | tf_op jit(solution)/shard_map/last_kernel/pallas_call | solution.py:982
  (18 shorter events, 0.0 us)
Async XLA Ops:
  1.3 9.8 %copy-start.1 = (bf16[8,6,16,24]{3,2,1,0:T(8,128)(2,1)S(1)}, bf16[8,6,16,24]{3,2,1,0:T(8,128)(2,1)}, u32[]{:S(2)}) copy-start(bf16[8,6,16,24]{3,2,1,0:T(8,128)(2,1)} %x_ref.3) | copy-start | bytes 110596
  1.3 9.8 %copy-start.2 = (bf16[8,6,16,24]{3,2,1,0:T(8,128)(2,1)S(1)}, bf16[8,6,16,24]{3,2,1,0:T(8,128)(2,1)}, u32[]{:S(2)}) copy-start(bf16[8,6,16,24]{3,2,1,0:T(8,128)(2,1)} %c_ref.3) | copy-start | bytes 110596
  3.8 7.3 %copy-start = (f32[128,128]{1,0:T(8,128)S(1)}, f32[128,128]{1,0:T(8,128)}, u32[]{:S(2)}) copy-start(f32[128,128]{1,0:T(8,128)} %get-tuple-element.83.after_ref) | copy-start | bytes 196612
  3.8 14.7 %all-to-all-start = ((f32[32,4,128]{2,1,0:T(4,128)}), f32[32,4,128]{2,1,0:T(4,128)S(1)}, u32[]{:S(2)}, u32[]{:S(2)}) async-start(f32[32,4,128]{2,1,0:T(4,128)} %bitcast.19), calls=%async_computation | async-start | bytes 131072 | tf_op jit(solution)/shard_map/all_to_all | solution.py:997
  11.1 2.6 %copy-start.4 = (bf16[144,24]{0,1:T(8,128)(2,1)S(1)}, bf16[144,24]{0,1:T(8,128)(2,1)}, u32[]{:S(2)}) copy-start(bf16[144,24]{0,1:T(8,128)(2,1)} %param.28) | copy-start | bytes 20740
  11.1 2.6 %copy-start.5 = (f32[144,6]{0,1:T(8,128)S(1)}, f32[144,6]{0,1:T(8,128)}, u32[]{:S(2)}) copy-start(f32[144,6]{0,1:T(8,128)} %param.24) | copy-start | bytes 10372
  11.1 2.6 %copy-start.6 = (f32[6,144]{1,0:T(8,128)S(1)}, f32[6,144]{1,0:T(8,128)}, u32[]{:S(2)}) copy-start(f32[6,144]{1,0:T(8,128)} %refs_10_.1) | copy-start | bytes 10372
  11.1 2.6 %copy-start.7 = (bf16[3,3,144]{2,1,0:T(4,128)(2,1)S(1)}, bf16[3,3,144]{2,1,0:T(4,128)(2,1)}, u32[]{:S(2)}) copy-start(bf16[3,3,144]{2,1,0:T(4,128)(2,1)} %refs_8_.1) | copy-start | bytes 7780
  11.2 2.6 %copy-start.9 = (f32[144]{0:T(256)S(1)}, f32[144]{0:T(256)}, u32[]{:S(2)}) copy-start(f32[144]{0:T(256)} %refs_1_.1) | copy-start | bytes 1732
  11.2 2.6 %copy-start.10 = (f32[144]{0:T(256)S(1)}, f32[144]{0:T(256)}, u32[]{:S(2)}) copy-start(f32[144]{0:T(256)} %refs_2_.1) | copy-start | bytes 1732
  11.2 2.6 %copy-start.11 = (f32[144]{0:T(256)S(1)}, f32[144]{0:T(256)}, u32[]{:S(2)}) copy-start(f32[144]{0:T(256)} %refs_3_.1) | copy-start | bytes 1732
  11.2 2.6 %copy-start.12 = (f32[144]{0:T(256)S(1)}, f32[144]{0:T(256)}, u32[]{:S(2)}) copy-start(f32[144]{0:T(256)} %refs_4_.1) | copy-start | bytes 1732
  11.2 2.6 %copy-start.13 = (f32[24]{0:T(128)S(1)}, f32[24]{0:T(128)}, u32[]{:S(2)}) copy-start(f32[24]{0:T(128)} %refs_5_.1) | copy-start | bytes 292
  11.2 2.6 %copy-start.14 = (f32[24]{0:T(128)S(1)}, f32[24]{0:T(128)}, u32[]{:S(2)}) copy-start(f32[24]{0:T(128)} %refs_6_.1) | copy-start | bytes 292
  11.2 2.6 %copy-start.15 = (f32[6]{0:T(128)S(1)}, f32[6]{0:T(128)}, u32[]{:S(2)}) copy-start(f32[6]{0:T(128)} %refs_7_.1) | copy-start | bytes 76
  11.2 2.6 %copy-start.16 = (f32[16,128]{1,0:T(8,128)S(1)}, f32[16,128]{1,0:T(8,128)}, u32[]{:S(2)}) copy-start(f32[16,128]{1,0:T(8,128)} %get-tuple-element.84.refs_13_) | copy-start | bytes 24580
  11.2 2.6 %copy-start.17 = (f32[16,128]{1,0:T(8,128)S(1)}, f32[16,128]{1,0:T(8,128)}, u32[]{:S(2)}) copy-start(f32[16,128]{1,0:T(8,128)} %get-tuple-element.85.refs_14_) | copy-start | bytes 24580
  11.5 2.3 %copy-start.3 = (bf16[24,144]{1,0:T(8,128)(2,1)S(1)}, bf16[24,144]{1,0:T(8,128)(2,1)}, u32[]{:S(2)}) copy-start(bf16[24,144]{1,0:T(8,128)(2,1)} %refs_12_.1) | copy-start | bytes 20740
  11.5 7.3 %collective-permute-start = (bf16[2,3,16,128]{3,2,1,0:T(8,128)(2,1)S(1)}, bf16[2,3,16,128]{3,2,1,0:T(8,128)(2,1)S(1)}, u32[]{:S(2)}, u32[]{:S(2)}) collective-permute-start(bf16[2,3,16,128]{3,2,1,0:T(8,128)(2,1)S(1)} %get-tuple-element.89), channel_id=1, source_target_pairs={{0,2},{1,3},{2,0},{3,1},{4,6},{5,7},{6,4},{7,5},{8,10},{9,11},{10,... | collective-permute-start | bytes 73736 | tf_op jit(solution)/shard_map/ppermute | solution.py:1004
  13.3 5.5 %collective-permute-start.1 = (bf16[2,3,16,128]{3,2,1,0:T(8,128)(2,1)S(1)}, bf16[2,3,16,128]{3,2,1,0:T(8,128)(2,1)S(1)}, u32[]{:S(2)}, u32[]{:S(2)}) collective-permute-start(bf16[2,3,16,128]{3,2,1,0:T(8,128)(2,1)S(1)} %get-tuple-element.90), channel_id=1, source_target_pairs={{0,3},{1,2},{2,1},{3,0},{4,7},{5,6},{6,5},{7,4},{8,11},{9,10},{10,... | collective-permute-start | bytes 73736 | tf_op jit(solution)/shard_map/ppermute | solution.py:1004
  13.3 5.5 %collective-permute-start.2 = (bf16[2,3,16,128]{3,2,1,0:T(8,128)(2,1)S(1)}, bf16[2,3,16,128]{3,2,1,0:T(8,128)(2,1)S(1)}, u32[]{:S(2)}, u32[]{:S(2)}) collective-permute-start(bf16[2,3,16,128]{3,2,1,0:T(8,128)(2,1)S(1)} %get-tuple-element.91), channel_id=1, source_target_pairs={{0,1},{1,0},{2,3},{3,2},{4,5},{5,4},{6,7},{7,6},{8,9},{9,8},{10,11... | collective-permute-start | bytes 73736 | tf_op jit(solution)/shard_map/ppermute | solution.py:1004
  13.7 0.7 copy-start.8
  58.1 10.8 %all-to-all-start.4 = ((f32[32,8,128]{2,1,0:T(8,128)}), f32[32,8,128]{2,1,0:T(8,128)S(1)}, u32[]{:S(2)}, u32[]{:S(2)}) async-start(f32[32,8,128]{2,1,0:T(8,128)} %bitcast.10), calls=%async_computation.4 | async-start | bytes 262144 | tf_op jit(solution)/shard_map/all_to_all | solution.py:997
  61.2 4.0 %collective-permute-start.3 = (bf16[2,3,16,128]{3,2,1,0:T(8,128)(2,1)S(1)}, bf16[2,3,16,128]{3,2,1,0:T(8,128)(2,1)S(1)}, u32[]{:S(2)}, u32[]{:S(2)}) collective-permute-start(bf16[2,3,16,128]{3,2,1,0:T(8,128)(2,1)S(1)} %get-tuple-element.131), channel_id=1, source_target_pairs={{0,2},{1,3},{2,0},{3,1},{4,6},{5,7},{6,4},{7,5},{8,10},{9,11},{10,... | collective-permute-start | bytes 73736 | tf_op jit(solution)/shard_map/ppermute | solution.py:1004
  62.9 3.8 %collective-permute-start.4 = (bf16[2,3,16,128]{3,2,1,0:T(8,128)(2,1)S(1)}, bf16[2,3,16,128]{3,2,1,0:T(8,128)(2,1)S(1)}, u32[]{:S(2)}, u32[]{:S(2)}) collective-permute-start(bf16[2,3,16,128]{3,2,1,0:T(8,128)(2,1)S(1)} %get-tuple-element.132), channel_id=1, source_target_pairs={{0,3},{1,2},{2,1},{3,0},{4,7},{5,6},{6,5},{7,4},{8,11},{9,10},{10,... | collective-permute-start | bytes 73736 | tf_op jit(solution)/shard_map/ppermute | solution.py:1004
  62.9 3.8 %collective-permute-start.5 = (bf16[2,3,16,128]{3,2,1,0:T(8,128)(2,1)S(1)}, bf16[2,3,16,128]{3,2,1,0:T(8,128)(2,1)S(1)}, u32[]{:S(2)}, u32[]{:S(2)}) collective-permute-start(bf16[2,3,16,128]{3,2,1,0:T(8,128)(2,1)S(1)} %get-tuple-element.133), channel_id=1, source_target_pairs={{0,1},{1,0},{2,3},{3,2},{4,5},{5,4},{6,7},{7,6},{8,9},{9,8},{10,11... | collective-permute-start | bytes 73736 | tf_op jit(solution)/shard_map/ppermute | solution.py:1004

commit v5 on v4

--- a/solution.py
+++ b/solution.py
@@ -537,6 +537,7 @@
     row_ref,
     buf_ref,
     sq_ref,
+    slope_ref,
     mat_ref,
     acc_ref,
     sh_ref,
@@ -550,6 +551,7 @@
     masks = mask_rows(sz, info)
     count = info[7:8]
     mean_c, slope_c, bias_c = spread_rows([mean1, inv1 * par_ref[2:3], par_ref[3:4]])
+    slope_ref[...] = slope_c
     pool = 0.0
     squares = 0.0
     fields = []
@@ -636,6 +638,7 @@
     part_ref,
     sq_ref,
     row_ref,
+    slope_ref,
     out_pay,
     res_ref,
     scaled_ref,
@@ -710,7 +713,7 @@
     squeeze_grad = fine_dot(gate_pre, sw) * slope * live
     back = dot(squeeze_grad, rw, 1, 0, True) / info[8:16, 0:1]
     back_wide = seg_spread(sz, back)
-    (scale_c,) = spread_rows([row_ref[1:2] * par_ref[2:3]])
+    scale_c = slope_ref[...]
     sum_b = 0.0
     sum_g = 0.0
     fields = []
@@ -815,10 +818,10 @@
     send_block(out_pay, jnp.concatenate([top, block[4:8]], axis=0))
 
 
-def back_kernel(sz, gp0_ref, res_ref, row0_ref, par_ref, w_ref, *refs):
+def back_kernel(sz, gp0_ref, res_ref, wide_ref, w_ref, *refs):
     out_refs, all_ref = refs[:-1], refs[-1]
     chans = sz.chans
-    (scale,) = spread_rows([row0_ref[1:2] * par_ref[0:1]])
+    scale = wide_ref[1]
     weights = w_ref[...]
     for g in range(sz.rows // 2):
         pieces = []
@@ -1091,13 +1094,13 @@
         [big, taps, shifts, column],
     )
     pay = everywhere(pay)
-    pay, act1, dc, s1, proj, gate, seg_rows, row1, part, squares = call(
+    pay, act1, dc, s1, proj, gate, seg_rows, row1, part, squares, slope1 = call(
         stage_two_kernel,
         sz,
         [pay, deep, x_c, pix, par, tap, unit, info, pw_near, near, act0, s0, part],
         "",
         [pay_of(2), big, big, big, small, column, ((3, 8, wide), F32), ((2, wide), F32)]
-        + [column, ((16, LANES), F32)],
+        + [column, ((16, LANES), F32), column],
         [big, taps, shifts],
     )
     pay = everywhere(pay)
@@ -1105,7 +1108,7 @@
         stage_three_kernel,
         sz,
         [pay, proj, x_c, pix, act0, act1, s0, dc, s1, gate, seg_rows, par, tap, unit, info]
-        + [pw_turned, part, squares, row1],
+        + [pw_turned, part, squares, row1, slope1],
         "",
         [pay_of(8), small, big, ((chans,), F32), ((chans,), F32)],
         [big, big, taps, shifts, column],
@@ -1122,7 +1125,7 @@
     sent = call(
         back_kernel,
         sz,
-        [gp0, res, row0, par, w_near],
+        [gp0, res, wide0, w_near],
         "",
         [block] * tiles,
         [((tiles,) + block[0], BF16)],

time: 70.9 us -> 70.9 us (level)
  no operation moved by 1% of the time
where the time goes in v5:
time: 70.9 us; the launch traced here: 70.6 us
  blocking collectives  28.7 us (40%)
  Pallas kernels  16.4 us (23%)
  starting transfers between devices  14.3 us (20%)
  waiting for transfers between devices  8.91 us (13%)
  between operations  1.61 us (2%)
    all_to_all x3, blocking collectives, everywhere(): return lax.all_to_all(values, BOTH, 0, 0, tiled=True)  28.7 us
    pallas_call x11, Pallas kernels, call(): pl.pallas_call(functools.partial(kernel, sz), out_shape=tuple((jax.ShapeD...  16.4 us
    all_to_all x2, starting transfers between devices, everywhere(): return lax.all_to_all(values, BOTH, 0, 0, tiled=True)  9.88 us
    all_to_all x2, waiting for transfers between devices, everywhere(): return lax.all_to_all(values, BOTH, 0, 0, tiled=True)  6.37 us
    ppermute x6, starting transfers between devices, passed(): result.append(lax.ppermute(part, 'tile', pairs))  4.41 us
    ppermute x6, waiting for transfers between devices, passed(): result.append(lax.ppermute(part, 'tile', pairs))  2.54 us
  transfers between devices with their start and end apart: 8, of which 4 were waited for; matrix products, arithmetic and copies ran while one was open for 0% of the time, Pallas kernels for 3%

profile of v5, /device:TPU:0, one launch (start us, length us, event | category | flops | bytes accessed | tf_op | source)
XLA Modules:
  0.0 70.6 jit_solution(1395721711146911720)
XLA Ops:
  1.3 2.4 %entry_kernel.1 = (f32[128,128]{1,0:T(8,128)}, f32[16,128]{1,0:T(8,128)}, f32[16,128]{1,0:T(8,128)}) custom-call(bf16[8,6,16,24]{3,2,1,0:T(8,128)(2,1)} %x_ref.3, bf16[24,144]{1,0:T(8,128)(2,1)} %refs_12_.1, s32[8]{0:T(128)} %len_hbm.1, s32[1]{0:T(128)S(6)} %copy.33.count_hbm), custom_call_target="tpu_custom_call" | custom-call | flops 1000000000 | bytes 3000000 | tf_op jit(solution)/shard_map/entry_kernel/pallas_call | solution.py:985
  3.8 0.0 copy-start
  3.8 7.3 %all-to-all-start = ((f32[32,4,128]{2,1,0:T(4,128)}), f32[32,4,128]{2,1,0:T(4,128)S(1)}, u32[]{:S(2)}, u32[]{:S(2)}) async-start(f32[32,4,128]{2,1,0:T(4,128)} %bitcast.19), calls=%async_computation | async-start | bytes 131072 | tf_op jit(solution)/shard_map/all_to_all | solution.py:1000
  11.1 0.0 copy-done.1
  11.1 0.0 copy-done.2
  11.1 0.0 copy-done
  11.1 0.0 copy-start.4
  11.1 0.0 copy-start.5
  11.1 0.0 copy-start.6
  11.1 0.0 copy-start.7
  11.2 0.0 copy-start.9
  11.2 0.0 copy-start.10
  11.2 0.0 copy-start.11
  11.2 0.0 copy-start.12
  11.2 0.0 copy-start.13
  11.2 0.0 copy-start.14
  11.2 0.0 copy-start.15
  11.2 0.0 copy-start.16
  11.2 0.0 copy-start.17
  11.3 0.2 send_kernel.1
  11.5 1.8 %collective-permute-start = (bf16[2,3,16,128]{3,2,1,0:T(8,128)(2,1)S(1)}, bf16[2,3,16,128]{3,2,1,0:T(8,128)(2,1)S(1)}, u32[]{:S(2)}, u32[]{:S(2)}) collective-permute-start(bf16[2,3,16,128]{3,2,1,0:T(8,128)(2,1)S(1)} %get-tuple-element.90), channel_id=1, source_target_pairs={{0,2},{1,3},{2,0},{3,1},{4,6},{5,7},{6,4},{7,5},{8,10},{9,11},{10,... | collective-permute-start | bytes 73736 | tf_op jit(solution)/shard_map/ppermute | solution.py:1007
  13.3 0.0 collective-permute-start.1
  13.3 0.4 collective-permute-start.2
  13.8 0.6 copy-done.8
  14.4 0.3 setup_kernel.1
  14.7 3.8 %all-to-all-done = f32[32,4,128]{2,1,0:T(4,128)S(1)} async-done(((f32[32,4,128]{2,1,0:T(4,128)}), f32[32,4,128]{2,1,0:T(4,128)S(1)}, u32[]{:S(2)}, u32[]{:S(2)}) %all-to-all-start) | async-done | bytes 65568 | tf_op jit(solution)/shard_map/all_to_all | solution.py:1000
  18.5 0.4 moment_kernel.1
  18.8 0.0 collective-permute-done.refs_1_
  18.8 0.0 collective-permute-done.1.refs_2_
  18.8 0.0 collective-permute-done.2.refs_3_
  18.9 2.2 %stage_one_kernel.1 = (f32[128,128]{1,0:T(8,128)S(1)}, bf16[6,48,128]{2,1,0:T(8,128)(2,1)S(1)}, bf16[3,4,32,128]{3,2,1,0:T(8,128)(2,1)S(1)}, bf16[6,144,128]{2,1...) custom-call(f32[3,144,128]{2,1,0:T(8,128)S(1)} %get-tuple-element.88, ...), custom_call_target="tpu_custom_call" | custom-call | flops 1000000000 | bytes 3000000 | tf_op jit(solution)/shard_map/stage_one_kernel/pallas_call | solution.py:985
  21.1 9.8 %all_to_all.55 = f32[32,4,128]{2,1,0:T(4,128)S(1)} all-to-all(f32[32,4,128]{2,1,0:T(4,128)S(1)} %bitcast.21), channel_id=1, replica_groups=mesh['seg'=8,'tile'=4] {'seg','tile'}, dimensions={0} | all-to-all | bytes 131072 | tf_op jit(solution)/shard_map/all_to_all | solution.py:1000
  30.9 2.8 %stage_two_kernel.1 = (f32[64,128]{1,0:T(8,128)S(1)}, f32[6,144,128]{2,1,0:T(8,128)S(1)}, f32[6,144,128]{2,1,0:T(8,128)S(1)}, f32[6,144,128]{2,1,0:T(8,128)S(1)}...) custom-call(f32[128,128]{1,0:T(8,128)S(1)} %bitcast.20, ...), custom_call_target="tpu_custom_call" | custom-call | flops 1000000000 | bytes 3000000 | tf_op jit(solution)/shard_map/stage_two_kernel/pallas_call | solution.py:985
  33.6 8.9 %all_to_all.56 = f32[32,2,128]{2,1,0:T(2,128)S(1)} all-to-all(f32[32,2,128]{2,1,0:T(2,128)S(1)} %bitcast.23), channel_id=1, replica_groups=mesh['seg'=8,'tile'=4] {'seg','tile'}, dimensions={0} | all-to-all | bytes 65536 | tf_op jit(solution)/shard_map/all_to_all | solution.py:1000
  42.6 3.8 %stage_three_kernel.1 = (f32[256,128]{1,0:T(8,128)S(1)}, f32[6,24,128]{2,1,0:T(8,128)S(1)}, f32[6,144,128]{2,1,0:T(8,128)S(1)}, f32[24]{0:T(128)}, f32[24]{0:T(128)}) custom-call(f32[64,128]{1,0:T(8,128)S(1)} %bitcast.22, f32[6,24,128]{2,1,0:T(8,128)S(1)} %get-tuple-element.107.proj_ref, bf16[6,48,128]{2,1,0:T(8,128)(2,1)S(1)} %get-tuple-element.99.xc_ref, ...), custom_call_target="tpu_custom_call" | custom-call | flops 1000000000 | bytes 3000000 | tf_op jit(solution)/shard_map/stage_three_kernel/pallas_call | solution.py:985
  46.4 9.9 %all_to_all.57 = f32[32,8,128]{2,1,0:T(8,128)S(1)} all-to-all(f32[32,8,128]{2,1,0:T(8,128)S(1)} %bitcast.17), channel_id=1, replica_groups=mesh['seg'=8,'tile'=4] {'seg','tile'}, dimensions={0} | all-to-all | bytes 262144 | tf_op jit(solution)/shard_map/all_to_all | solution.py:1000
  56.3 1.9 %stage_four_kernel.1 = (f32[256,128]{1,0:T(8,128)}, f32[6,144,128]{2,1,0:T(8,128)S(1)}, f32[144]{0:T(256)}, f32[144]{0:T(256)}, f32[2,144]{1,0:T(2,128)S(1)}) custom-call(f32[256,128]{1,0:T(8,128)S(1)} %bitcast.15, f32[6,144,128]{2,1,0:T(8,128)S(1)} %get-tuple-element.119.scaled_ref, f32[6,144,128]{2,1,0:T(8,128)S(1)} %get-tuple-element.109.dc_ref, ...), custom_call_target="tpu_custom_call" | custom-call | flops 1000000000 | bytes 3000000 | tf_op jit(solution)/shard_map/stage_four_kernel/pallas_call | solution.py:985
  58.2 2.6 %all-to-all-start.4 = ((f32[32,8,128]{2,1,0:T(8,128)}), f32[32,8,128]{2,1,0:T(8,128)S(1)}, u32[]{:S(2)}, u32[]{:S(2)}) async-start(f32[32,8,128]{2,1,0:T(8,128)} %bitcast.10), calls=%async_computation.4 | async-start | bytes 262144 | tf_op jit(solution)/shard_map/all_to_all | solution.py:1000
  60.8 0.3 back_kernel.1
  61.1 1.7 %collective-permute-start.3 = (bf16[2,3,16,128]{3,2,1,0:T(8,128)(2,1)S(1)}, bf16[2,3,16,128]{3,2,1,0:T(8,128)(2,1)S(1)}, u32[]{:S(2)}, u32[]{:S(2)}) collective-permute-start(bf16[2,3,16,128]{3,2,1,0:T(8,128)(2,1)S(1)} %get-tuple-element.133), channel_id=1, source_target_pairs={{0,2},{1,3},{2,0},{3,1},{4,6},{5,7},{6,4},{7,5},{8,10},{9,11},{10,... | collective-permute-start | bytes 73736 | tf_op jit(solution)/shard_map/ppermute | solution.py:1007
  62.8 0.0 collective-permute-start.4
  62.8 0.5 collective-permute-start.5
  63.3 0.6 far_kernel.1
  63.9 1.1 %collective-permute-done.3.refs_1_ = bf16[2,3,16,128]{3,2,1,0:T(8,128)(2,1)S(1)} collective-permute-done((bf16[2,3,16,128]{3,2,1,0:T(8,128)(2,1)S(1)}, bf16[2,3,16,128]{3,2,1,0:T(8,128)(2,1)S(1)}, u32[]{:S(2)}, u32[]{:S(2)}) %collective-permute-start.3) | collective-permute-done | bytes 24608 | tf_op jit(solution)/shard_map/ppermute | solution.py:1007
  65.0 1.4 %collective-permute-done.4.refs_2_ = bf16[2,3,16,128]{3,2,1,0:T(8,128)(2,1)S(1)} collective-permute-done((bf16[2,3,16,128]{3,2,1,0:T(8,128)(2,1)S(1)}, bf16[2,3,16,128]{3,2,1,0:T(8,128)(2,1)S(1)}, u32[]{:S(2)}, u32[]{:S(2)}) %collective-permute-start.4) | collective-permute-done | bytes 24608 | tf_op jit(solution)/shard_map/ppermute | solution.py:1007
  66.4 0.0 collective-permute-done.5.refs_3_
  66.4 2.6 %all-to-all-done.4 = f32[32,8,128]{2,1,0:T(8,128)S(1)} async-done(((f32[32,8,128]{2,1,0:T(8,128)}), f32[32,8,128]{2,1,0:T(8,128)S(1)}, u32[]{:S(2)}, u32[]{:S(2)}) %all-to-all-start.4) | async-done | bytes 131104 | tf_op jit(solution)/shard_map/all_to_all | solution.py:1000
  69.0 1.6 %last_kernel.1 = (bf16[8,6,16,24]{3,2,1,0:T(8,128)(2,1)}, bf16[8,6,16,24]{3,2,1,0:T(8,128)(2,1)}, f32[24,144]{1,0:T(8,128)}, f32[144]{0:T(256)}, f32[144]{0:T(25...) custom-call(f32[256,128]{1,0:T(8,128)S(1)} %bitcast.14, ...), custom_call_target="tpu_custom_call" | custom-call | flops 1000000000 | bytes 3000000 | tf_op jit(solution)/shard_map/last_kernel/pallas_call | solution.py:985
  (18 shorter events, 0.0 us)
Async XLA Ops:
  1.3 9.8 %copy-start.1 = (bf16[8,6,16,24]{3,2,1,0:T(8,128)(2,1)S(1)}, bf16[8,6,16,24]{3,2,1,0:T(8,128)(2,1)}, u32[]{:S(2)}) copy-start(bf16[8,6,16,24]{3,2,1,0:T(8,128)(2,1)} %x_ref.3) | copy-start | bytes 110596
  1.3 9.8 %copy-start.2 = (bf16[8,6,16,24]{3,2,1,0:T(8,128)(2,1)S(1)}, bf16[8,6,16,24]{3,2,1,0:T(8,128)(2,1)}, u32[]{:S(2)}) copy-start(bf16[8,6,16,24]{3,2,1,0:T(8,128)(2,1)} %c_ref.3) | copy-start | bytes 110596
  3.8 7.3 %copy-start = (f32[128,128]{1,0:T(8,128)S(1)}, f32[128,128]{1,0:T(8,128)}, u32[]{:S(2)}) copy-start(f32[128,128]{1,0:T(8,128)} %get-tuple-element.84.after_ref) | copy-start | bytes 196612
  3.8 14.7 %all-to-all-start = ((f32[32,4,128]{2,1,0:T(4,128)}), f32[32,4,128]{2,1,0:T(4,128)S(1)}, u32[]{:S(2)}, u32[]{:S(2)}) async-start(f32[32,4,128]{2,1,0:T(4,128)} %bitcast.19), calls=%async_computation | async-start | bytes 131072 | tf_op jit(solution)/shard_map/all_to_all | solution.py:1000
  11.1 2.6 %copy-start.4 = (bf16[144,24]{0,1:T(8,128)(2,1)S(1)}, bf16[144,24]{0,1:T(8,128)(2,1)}, u32[]{:S(2)}) copy-start(bf16[144,24]{0,1:T(8,128)(2,1)} %param.28) | copy-start | bytes 20740
  11.1 2.6 %copy-start.5 = (f32[144,6]{0,1:T(8,128)S(1)}, f32[144,6]{0,1:T(8,128)}, u32[]{:S(2)}) copy-start(f32[144,6]{0,1:T(8,128)} %param.24) | copy-start | bytes 10372
  11.1 2.6 %copy-start.6 = (f32[6,144]{1,0:T(8,128)S(1)}, f32[6,144]{1,0:T(8,128)}, u32[]{:S(2)}) copy-start(f32[6,144]{1,0:T(8,128)} %refs_10_.1) | copy-start | bytes 10372
  11.1 2.6 %copy-start.7 = (bf16[3,3,144]{2,1,0:T(4,128)(2,1)S(1)}, bf16[3,3,144]{2,1,0:T(4,128)(2,1)}, u32[]{:S(2)}) copy-start(bf16[3,3,144]{2,1,0:T(4,128)(2,1)} %refs_8_.1) | copy-start | bytes 7780
  11.2 2.6 %copy-start.9 = (f32[144]{0:T(256)S(1)}, f32[144]{0:T(256)}, u32[]{:S(2)}) copy-start(f32[144]{0:T(256)} %refs_1_.1) | copy-start | bytes 1732
  11.2 2.6 %copy-start.10 = (f32[144]{0:T(256)S(1)}, f32[144]{0:T(256)}, u32[]{:S(2)}) copy-start(f32[144]{0:T(256)} %refs_2_.1) | copy-start | bytes 1732
  11.2 2.6 %copy-start.11 = (f32[144]{0:T(256)S(1)}, f32[144]{0:T(256)}, u32[]{:S(2)}) copy-start(f32[144]{0:T(256)} %refs_3_.1) | copy-start | bytes 1732
  11.2 2.6 %copy-start.12 = (f32[144]{0:T(256)S(1)}, f32[144]{0:T(256)}, u32[]{:S(2)}) copy-start(f32[144]{0:T(256)} %refs_4_.1) | copy-start | bytes 1732
  11.2 2.6 %copy-start.13 = (f32[24]{0:T(128)S(1)}, f32[24]{0:T(128)}, u32[]{:S(2)}) copy-start(f32[24]{0:T(128)} %refs_5_.1) | copy-start | bytes 292
  11.2 2.6 %copy-start.14 = (f32[24]{0:T(128)S(1)}, f32[24]{0:T(128)}, u32[]{:S(2)}) copy-start(f32[24]{0:T(128)} %refs_6_.1) | copy-start | bytes 292
  11.2 2.6 %copy-start.15 = (f32[6]{0:T(128)S(1)}, f32[6]{0:T(128)}, u32[]{:S(2)}) copy-start(f32[6]{0:T(128)} %refs_7_.1) | copy-start | bytes 76
  11.2 2.6 %copy-start.16 = (f32[16,128]{1,0:T(8,128)S(1)}, f32[16,128]{1,0:T(8,128)}, u32[]{:S(2)}) copy-start(f32[16,128]{1,0:T(8,128)} %get-tuple-element.85.refs_13_) | copy-start | bytes 24580
  11.2 2.6 %copy-start.17 = (f32[16,128]{1,0:T(8,128)S(1)}, f32[16,128]{1,0:T(8,128)}, u32[]{:S(2)}) copy-start(f32[16,128]{1,0:T(8,128)} %get-tuple-element.86.refs_14_) | copy-start | bytes 24580
  11.5 2.3 %copy-start.3 = (bf16[24,144]{1,0:T(8,128)(2,1)S(1)}, bf16[24,144]{1,0:T(8,128)(2,1)}, u32[]{:S(2)}) copy-start(bf16[24,144]{1,0:T(8,128)(2,1)} %refs_12_.1) | copy-start | bytes 20740
  11.5 7.3 %collective-permute-start = (bf16[2,3,16,128]{3,2,1,0:T(8,128)(2,1)S(1)}, bf16[2,3,16,128]{3,2,1,0:T(8,128)(2,1)S(1)}, u32[]{:S(2)}, u32[]{:S(2)}) collective-permute-start(bf16[2,3,16,128]{3,2,1,0:T(8,128)(2,1)S(1)} %get-tuple-element.90), channel_id=1, source_target_pairs={{0,2},{1,3},{2,0},{3,1},{4,6},{5,7},{6,4},{7,5},{8,10},{9,11},{10,... | collective-permute-start | bytes 73736 | tf_op jit(solution)/shard_map/ppermute | solution.py:1007
  13.3 5.5 %collective-permute-start.1 = (bf16[2,3,16,128]{3,2,1,0:T(8,128)(2,1)S(1)}, bf16[2,3,16,128]{3,2,1,0:T(8,128)(2,1)S(1)}, u32[]{:S(2)}, u32[]{:S(2)}) collective-permute-start(bf16[2,3,16,128]{3,2,1,0:T(8,128)(2,1)S(1)} %get-tuple-element.91), channel_id=1, source_target_pairs={{0,3},{1,2},{2,1},{3,0},{4,7},{5,6},{6,5},{7,4},{8,11},{9,10},{10,... | collective-permute-start | bytes 73736 | tf_op jit(solution)/shard_map/ppermute | solution.py:1007
  13.3 5.5 %collective-permute-start.2 = (bf16[2,3,16,128]{3,2,1,0:T(8,128)(2,1)S(1)}, bf16[2,3,16,128]{3,2,1,0:T(8,128)(2,1)S(1)}, u32[]{:S(2)}, u32[]{:S(2)}) collective-permute-start(bf16[2,3,16,128]{3,2,1,0:T(8,128)(2,1)S(1)} %get-tuple-element.92), channel_id=1, source_target_pairs={{0,1},{1,0},{2,3},{3,2},{4,5},{5,4},{6,7},{7,6},{8,9},{9,8},{10,11... | collective-permute-start | bytes 73736 | tf_op jit(solution)/shard_map/ppermute | solution.py:1007
  13.7 0.7 copy-start.8
  58.2 10.8 %all-to-all-start.4 = ((f32[32,8,128]{2,1,0:T(8,128)}), f32[32,8,128]{2,1,0:T(8,128)S(1)}, u32[]{:S(2)}, u32[]{:S(2)}) async-start(f32[32,8,128]{2,1,0:T(8,128)} %bitcast.10), calls=%async_computation.4 | async-start | bytes 262144 | tf_op jit(solution)/shard_map/all_to_all | solution.py:1000
  61.1 3.9 %collective-permute-start.3 = (bf16[2,3,16,128]{3,2,1,0:T(8,128)(2,1)S(1)}, bf16[2,3,16,128]{3,2,1,0:T(8,128)(2,1)S(1)}, u32[]{:S(2)}, u32[]{:S(2)}) collective-permute-start(bf16[2,3,16,128]{3,2,1,0:T(8,128)(2,1)S(1)} %get-tuple-element.133), channel_id=1, source_target_pairs={{0,2},{1,3},{2,0},{3,1},{4,6},{5,7},{6,4},{7,5},{8,10},{9,11},{10,... | collective-permute-start | bytes 73736 | tf_op jit(solution)/shard_map/ppermute | solution.py:1007
  62.8 3.6 %collective-permute-start.4 = (bf16[2,3,16,128]{3,2,1,0:T(8,128)(2,1)S(1)}, bf16[2,3,16,128]{3,2,1,0:T(8,128)(2,1)S(1)}, u32[]{:S(2)}, u32[]{:S(2)}) collective-permute-start(bf16[2,3,16,128]{3,2,1,0:T(8,128)(2,1)S(1)} %get-tuple-element.134), channel_id=1, source_target_pairs={{0,3},{1,2},{2,1},{3,0},{4,7},{5,6},{6,5},{7,4},{8,11},{9,10},{10,... | collective-permute-start | bytes 73736 | tf_op jit(solution)/shard_map/ppermute | solution.py:1007
  62.8 3.6 %collective-permute-start.5 = (bf16[2,3,16,128]{3,2,1,0:T(8,128)(2,1)S(1)}, bf16[2,3,16,128]{3,2,1,0:T(8,128)(2,1)S(1)}, u32[]{:S(2)}, u32[]{:S(2)}) collective-permute-start(bf16[2,3,16,128]{3,2,1,0:T(8,128)(2,1)S(1)} %get-tuple-element.135), channel_id=1, source_target_pairs={{0,1},{1,0},{2,3},{3,2},{4,5},{5,4},{6,7},{7,6},{8,9},{9,8},{10,11... | collective-permute-start | bytes 73736 | tf_op jit(solution)/shard_map/ppermute | solution.py:1007
